TPU v7x, 32 devices: a whole 2x2x4 slice. The times are simulated.
32 devices in a mesh: pole: 2 (over y), row: 4 (over z), col: 4 (over x, core).
Axes of the slice: x: 2, y: 2, z: 4, core: 2. Of those that a mesh axis runs over, the one named last changes fastest.
Arguments:
- inverse_root: float32 [2048, 1024], P(('pole', 'row'), 'col'), parts along dimension 0, may hold values from -6 to 6, as said below
- lower_first: float32 [2048, 512], P(('pole', 'col'), 'row'), parts along dimension 0, may hold values from -0.1875 to 0.1875
- mask_first: int32 [8, 4], P('col', 'row'), may hold values 0 or 1
- dinv_first: float32 [256, 512], P('pole', 'col'), parts along dimension 0, may hold values from -6 to 6
- lower_second: float32 [2048, 512], P(('pole', 'col'), 'row'), parts along dimension 0, may hold values from -0.1875 to 0.1875
- mask_second: int32 [8, 4], P('col', 'row'), may hold values 0 or 1
- parent: int32 [4], replicated, may hold values from 0 to 3
- lower_parent: float32 [256, 512], P('pole', 'col'), parts along dimension 0, may hold values from -0.5 to 0.5
- dinv_second: float32 [256, 512], P('pole', 'col'), parts along dimension 0, may hold values from -6 to 6
Outputs:
- inverse_first: float32 [2048, 512], P(('pole', 'row'), 'col'), parts along dimension 0
- diag_first: float32 [256, 512], P('pole', 'col'), parts along dimension 0
- inverse_second: float32 [2048, 512], P(('pole', 'row'), 'col'), parts along dimension 0
- diag_second: float32 [256, 512], P('pole', 'col'), parts along dimension 0
There are 2 independent parts, one for each index of `pole`. A program takes and returns all parts, laid end to end along the dimension named above; an argument that names none is the same for every part. Nothing has to cross between parts.
Inputs may be any that keep to these rules, and one draw needn't show every extreme that they name: `inverse_root`: symmetric.
All inputs are finite; a program needn't handle non-finite values. No bound on the sum of `mask_first` or of `mask_second` on one device may be relied on, other than what follows from the above.
Results may differ from a plain program's by a relative error of at most 0.000071.
Values sent between devices are 32-bit elements; how exact they have to be, the bound alone decides.
No kernel may reach another device: no remote copies, remote signals or barrier semaphores. Data moves between devices by JAX's collectives and lax.ppermute only.
A program may use at most 64 MiB of HBM per device.

v0:
```python
import jax
import jax.numpy as jnp
from jax import lax
from jax.sharding import PartitionSpec as P

highest = lax.Precision.HIGHEST


def masked_blocks(values, pattern):
    rows_blocks = pattern.shape[0]
    cols_blocks = pattern.shape[1]
    grid = values.reshape(
        rows_blocks, values.shape[0] // rows_blocks, cols_blocks, values.shape[1] // cols_blocks
    )
    return (grid * pattern.astype(jnp.float32)[:, None, :, None]).reshape(values.shape)


def diag_blocks(left, right, block_size):
    count = left.shape[1] // block_size
    left_cube = left.reshape(left.shape[0], count, block_size)
    right_cube = right.reshape(right.shape[0], count, block_size)
    result = jnp.einsum("rkb,rkc->bkc", left_cube, right_cube, precision=highest)
    return result.reshape(block_size, count * block_size)


def parent_terms(values, diagonal, lower_blocks, parent_ids, first_ids):
    block_size = lower_blocks.shape[0]
    second_count = parent_ids.shape[0]
    first_count = first_ids.shape[0]
    selector = (parent_ids[:, None] == first_ids[None, :]).astype(jnp.float32)
    lower_cube = lower_blocks.reshape(block_size, second_count, block_size)
    weights = jnp.einsum("kj,bkc->jbkc", selector, lower_cube, precision=highest)
    weights = weights.reshape(first_count * block_size, second_count * block_size)
    coupling = jnp.dot(values, weights, precision=highest, preferred_element_type=jnp.float32)
    diag_cube = diagonal.reshape(block_size, first_count, block_size)
    chosen = jnp.einsum("kj,bji->kbi", selector, diag_cube, precision=highest)
    product = jnp.einsum("kbi,ikc->bkc", chosen, lower_cube, precision=highest)
    return (coupling, product.reshape(block_size, second_count * block_size))


def on_device(
    inverse_root,
    lower_first,
    mask_first,
    dinv_first,
    lower_second,
    mask_second,
    parent,
    lower_parent,
    dinv_second,
):
    block_size = dinv_first.shape[0]
    local_rows = inverse_root.shape[0]
    row_index = lax.axis_index("row")
    col_index = lax.axis_index("col")
    first = masked_blocks(lower_first, mask_first)
    second = masked_blocks(lower_second, mask_second)
    first_full, second_full = (
        lax.all_gather(first, "row", axis=1, tiled=True),
        lax.all_gather(second, "row", axis=1, tiled=True),
    )
    first_part = jnp.dot(
        inverse_root, first_full, precision=highest, preferred_element_type=jnp.float32
    )
    second_part = jnp.dot(
        inverse_root, second_full, precision=highest, preferred_element_type=jnp.float32
    )
    first_total, second_sum = (
        lax.psum_scatter(first_part, "col", scatter_dimension=1, tiled=True),
        lax.psum_scatter(second_part, "col", scatter_dimension=1, tiled=True),
    )
    inverse_first = -first_total
    first_turned, second_turned = (
        lax.all_to_all(first_full, "col", split_axis=1, concat_axis=0, tiled=True),
        lax.all_to_all(second_full, "col", split_axis=1, concat_axis=0, tiled=True),
    )
    first_mine = lax.dynamic_slice_in_dim(first_turned, row_index * local_rows, local_rows, 0)
    first_terms = diag_blocks(first_mine, inverse_first, block_size)
    diag_first = dinv_first - lax.psum(first_terms, "row")
    local_count = lower_parent.shape[1] // block_size
    parent_mine = lax.dynamic_slice_in_dim(parent, col_index * local_count, local_count, 0)
    pieces = (
        lax.all_gather(inverse_first, "col", axis=1, tiled=True),
        lax.all_gather(diag_first, "col", axis=1, tiled=True),
    )
    count_here = pieces[0].shape[1] // block_size
    piece_ids = jnp.arange(count_here)
    coupling_here, product_here = parent_terms(
        pieces[0], pieces[1], lower_parent, parent_mine, piece_ids
    )
    inverse_second = -(second_sum + coupling_here)
    second_mine = lax.dynamic_slice_in_dim(second_turned, row_index * local_rows, local_rows, 0)
    second_terms = diag_blocks(coupling_here, second_mine, block_size) - diag_blocks(
        second_mine, inverse_second, block_size
    )
    diag_second = (
        dinv_second
        + lax.psum(second_terms, "row")
        + diag_blocks(lower_parent, product_here, block_size)
    )
    return (inverse_first, diag_first, inverse_second, diag_second)


def solution(mesh):
    in_specs = (
        P(("pole", "row"), "col"),
        P(("pole", "col"), "row"),
        P("col", "row"),
        P("pole", "col"),
        P(("pole", "col"), "row"),
        P("col", "row"),
        P(),
        P("pole", "col"),
        P("pole", "col"),
    )
    out_specs = (
        P(("pole", "row"), "col"),
        P("pole", "col"),
        P(("pole", "row"), "col"),
        P("pole", "col"),
    )
    return jax.shard_map(
        on_device, mesh=mesh, in_specs=in_specs, out_specs=out_specs, check_vma=False
    )
```

profile of v0, /device:TPU:0, one launch (start us, length us, event | category | flops | bytes accessed | tf_op | source)
XLA Modules:
  0.0 135.8 jit_solution(3812554968638542582)
XLA Ops:
  7.2 1.0 copy.27
  8.4 18.0 %all_gather.12 = f32[256,512]{0,1:T(8,128)} all-gather(f32[256,128]{0,1:T(8,128)S(1)} %broadcast_multiply_fusion.2), channel_id=1, replica_groups=mesh['pole'=2,'row'=4,'col'=4] {'row'}, dimensions={1}, use_global_device_ids=true | all-gather | bytes 655360 | tf_op jit(solution)/shard_map/all_gather | solution.py:59
  26.4 2.5 %convolution_bitcast_fusion.1 = f32[256,512]{0,1:T(8,128)} fusion(f32[256,512]{0,1:T(8,128)} %all_gather.12, f32[256,256]{1,0:T(8,128)S(1)} %copy-done), kind=kOutput, calls=%fused_computation.1 | convolution fusion | flops 402653184 | bytes 1310720 | tf_op jit(solution)/shard_map/dot_general | solution.py:62
  28.9 3.6 %all-to-all-start = ((f32[256,4,128]{0,2,1:T(8,128)}), f32[256,4,128]{0,2,1:T(8,128)S(1)}, u32[]{:S(2)}, u32[]{:S(2)}) async-start(f32[256,4,128]{0,2,1:T(8,128)} %bitcast.3), calls=%async_computation.1 | async-start | bytes 1048576 | tf_op jit(solution)/shard_map/all_to_all | solution.py:74
  33.3 17.5 %all_gather.13 = f32[256,512]{0,1:T(8,128)} all-gather(f32[256,128]{0,1:T(8,128)S(1)} %broadcast_multiply_fusion.1), channel_id=1, replica_groups=mesh['pole'=2,'row'=4,'col'=4] {'row'}, dimensions={1}, use_global_device_ids=true | all-gather | bytes 655360 | tf_op jit(solution)/shard_map/all_gather | solution.py:60
  50.8 3.5 %all-to-all-start.1 = ((f32[256,4,128]{0,2,1:T(8,128)}), f32[256,4,128]{0,2,1:T(8,128)S(1)}, u32[]{:S(2)}, u32[]{:S(2)}) async-start(f32[256,4,128]{0,2,1:T(8,128)} %bitcast.19), calls=%async_computation.3 | async-start | bytes 1048576 | tf_op jit(solution)/shard_map/all_to_all | solution.py:75
  54.3 2.5 %convolution_bitcast_fusion = f32[256,512]{0,1:T(8,128)} fusion(f32[256,512]{0,1:T(8,128)} %all_gather.13, f32[256,256]{1,0:T(8,128)S(1)} %copy-done), kind=kOutput, calls=%fused_computation | convolution fusion | flops 402653184 | bytes 1310720 | tf_op jit(solution)/shard_map/dot_general | solution.py:65
  59.1 4.0 %all-to-all-done.1 = f32[256,4,128]{0,2,1:T(8,128)S(1)} async-done(((f32[256,4,128]{0,2,1:T(8,128)}), f32[256,4,128]{0,2,1:T(8,128)S(1)}, u32[]{:S(2)}, u32[]{:S(2)}) %all-to-all-start.1) | async-done | bytes 524320 | tf_op jit(solution)/shard_map/all_to_all | solution.py:75
  63.3 0.9 neg.6
  64.2 6.6 %all_gather.14 = f32[256,512]{0,1:T(8,128)S(1)} all-gather(f32[256,128]{0,1:T(8,128)S(1)} %neg.6), channel_id=1, replica_groups=mesh['pole'=2,'row'=4,'col'=4] {'col'}, dimensions={1}, use_global_device_ids=true | all-gather | bytes 655360 | tf_op jit(solution)/shard_map/all_gather | solution.py:83
  70.8 1.0 fusion.15
  72.3 9.1 %reduce-scatter.5.cloned.1.call-done = f32[256,128]{0,1:T(8,128)} async-done(((f32[256,512]{0,1:T(8,128)}), f32[256,128]{0,1:T(8,128)}) %reduce-scatter.5.cloned.1.call-update) | async-done | bytes 131088 | tf_op jit(solution)/shard_map/reduce_scatter | solution.py:70
  81.4 0.9 add_negate_fusion
  82.3 0.9 fusion.1
  83.2 0.9 convolution_bitcast_fusion.3
  84.2 0.8 copy-done.5
  85.1 0.7 copy-done.6
  85.9 0.8 copy.34
  86.7 0.8 copy.36
  87.4 31.5 %all-reduce.3.cloned.1.call-done = (f32[128,128]{0,1:T(8,128)}, f32[128,128]{0,1:T(8,128)}) async-done(((f32[128,128]{0,1:T(8,128)}, f32[128,128]{0,1:T(8,128)}), (f32[128,128]{0,1:T(8,128)}, f32[128,128]{0,1:T(8,128)})) %all-reduce.3.cloned.1.call-update) | async-done | bytes 131088 | tf_op jit(solution)/shard_map/psum | solution.py:79
  118.9 0.8 sub.15
  120.5 5.8 %all_gather.15 = f32[128,512]{0,1:T(8,128)S(1)} all-gather(f32[128,128]{0,1:T(8,128)S(1)} %sub.15), channel_id=1, replica_groups=mesh['pole'=2,'row'=4,'col'=4] {'col'}, dimensions={1}, use_global_device_ids=true | all-gather | bytes 327680 | tf_op jit(solution)/shard_map/all_gather | solution.py:84
  126.4 1.0 fusion.6
  128.5 0.7 copy.37
  (46 shorter events, 6.0 us)
Async XLA Ops:
  7.2 19.2 %copy-start = (f32[256,256]{1,0:T(8,128)S(1)}, f32[256,256]{1,0:T(8,128)}, u32[]{:S(2)}) copy-start(f32[256,256]{1,0:T(8,128)} %param.9) | copy-start | bytes 786436
  7.2 1.1 copy-start.7
  7.2 56.1 %reduce-scatter.3.cloned.1.call-start = ((), (), s32[]{:S(2)}) async-start(), calls=%async_computation.4 | async-start | bytes 655360 | tf_op jit(solution)/shard_map/reduce_scatter | solution.py:69
  28.9 3.6 %copy-start.3 = (f32[256,128]{1,0:T(8,128)S(1)}, f32[256,128]{1,0:T(8,128)}, u32[]{:S(2)}) copy-start(f32[256,128]{1,0:T(8,128)} %param.13) | copy-start | bytes 393220
  28.9 21.9 %all-to-all-start = ((f32[256,4,128]{0,2,1:T(8,128)}), f32[256,4,128]{0,2,1:T(8,128)S(1)}, u32[]{:S(2)}, u32[]{:S(2)}) async-start(f32[256,4,128]{0,2,1:T(8,128)} %bitcast.3), calls=%async_computation.1 | async-start | bytes 1048576 | tf_op jit(solution)/shard_map/all_to_all | solution.py:74
  32.5 0.7 copy-start.8
  50.8 12.3 %all-to-all-start.1 = ((f32[256,4,128]{0,2,1:T(8,128)}), f32[256,4,128]{0,2,1:T(8,128)S(1)}, u32[]{:S(2)}, u32[]{:S(2)}) async-start(f32[256,4,128]{0,2,1:T(8,128)} %bitcast.19), calls=%async_computation.3 | async-start | bytes 1048576 | tf_op jit(solution)/shard_map/all_to_all | solution.py:75
  54.3 27.1 %reduce-scatter.5.cloned.1.call-start = ((), (), s32[]{:S(2)}) async-start(), calls=%async_computation.5 | async-start | bytes 655360 | tf_op jit(solution)/shard_map/reduce_scatter | solution.py:70
  56.8 2.0 %copy-start.1 = (f32[128,128]{1,0:T(8,128)S(1)}, f32[128,128]{1,0:T(8,128)}, u32[]{:S(2)}) copy-start(f32[128,128]{1,0:T(8,128)} %param.16) | copy-start | bytes 196612
  56.8 62.1 %all-reduce.3.cloned.1.call-start = ((), (), s32[]{:S(2)}) async-start(), calls=%async_computation.6 | async-start | bytes 262144 | tf_op jit(solution)/shard_map/psum | solution.py:79
  56.9 0.7 copy-start.9
  82.3 0.9 copy-start.2
  84.1 0.8 copy-start.5
  85.0 0.8 copy-start.6
  127.4 0.8 copy-start.4
Sparse Core Ops, SparseCore 0:
  29.0 23.5 reduce-scatter.2
  57.7 23.5 reduce-scatter.4
  84.3 34.5 all-reduce.2
where the time goes:
time: 136 us
  blocking collectives  47.9 us (35%)
  waiting for transfers between devices  44.6 us (33%)
  between operations  14 us (10%)
  matrix products  9.6 us (7%)
  local copies, waits for them, and re-layouts  9.05 us (7%)
  starting transfers between devices  7.21 us (5%)
  other arithmetic  3.42 us (3%)
    psum x1, waiting for transfers between devices, on_device(): diag_first = dinv_first - lax.psum(first_terms, 'row')  31.5 us
    all_gather x1, blocking collectives, on_device(): lax.all_gather(first, 'row', axis=1, tiled=True)  18 us
    all_gather x1, blocking collectives, on_device(): lax.all_gather(second, 'row', axis=1, tiled=True)  17.5 us
    reduce_scatter x1, waiting for transfers between devices, on_device(): lax.psum_scatter(second_part, 'col', scatter_dimension=1, tiled=True)  9.09 us
    unnamed x28, local copies, waits for them, and re-layouts  7.68 us
    all_gather x1, blocking collectives, on_device(): lax.all_gather(inverse_first, 'col', axis=1, tiled=True)  6.58 us
    all_gather x1, blocking collectives, on_device(): lax.all_gather(diag_first, 'col', axis=1, tiled=True)  5.77 us
    all_to_all x1, waiting for transfers between devices, on_device(): lax.all_to_all(second_full, 'col', split_axis=1, concat_axis=0, tiled=True)  4 us
  transfers between devices with their start and end apart: 5, of which 3 were waited for; matrix products, arithmetic and copies ran while one was open for 6% of the time, Pallas kernels for 0%

commit v1 on v0

v1 whole, which is shorter than its diff:
```python
import functools

import jax
import jax.numpy as jnp
from jax import lax
from jax.experimental import pallas as pl
from jax.experimental.pallas import tpu as pltpu
from jax.sharding import PartitionSpec as P

VMEM = pl.BlockSpec(memory_space=pltpu.VMEM)
SMEM = pl.BlockSpec(memory_space=pltpu.SMEM)
NN = ((1,), (0,))
TN = ((0,), (0,))


def split(x):
    high = x.astype(jnp.bfloat16)
    return high, (x - high.astype(jnp.float32)).astype(jnp.bfloat16)


def dot_split(a, b, dims):
    def one(left, right):
        return lax.dot_general(left, right, (dims, ((), ())), preferred_element_type=jnp.float32)

    return one(a[0], b[0]) + (one(a[0], b[1]) + one(a[1], b[0]))


def dot3(a, b, dims=NN):
    return dot_split(split(a), split(b), dims)


def slots(nrow, ncol):
    q = ncol // nrow
    r, c = lax.axis_index("row"), lax.axis_index("col")
    own = [(r * q + i) ^ c for i in range(q)]
    return (r * q + c % q) ^ c, own, c


def first_kernel(nrow, ncol, *refs):
    r_refs, f_refs = refs[:ncol], refs[ncol : 2 * ncol]
    dinv_ref, x_ref, z_ref, rh_ref, rl_ref, fh_ref, fl_ref = refs[2 * ncol :]
    base, own, _ = slots(nrow, ncol)
    depth = f_refs[0].shape[0]
    for t in range(ncol):
        slot = base ^ t
        fh_ref[slot], fl_ref[slot] = split(f_refs[t][...])
    total = None
    for j in range(ncol):
        parts = split(r_refs[j][...])
        rh_ref[j], rl_ref[j] = parts
        term = dot_split(parts, (fh_ref[j], fl_ref[j]), NN)
        total = term if total is None else total + term
    x = -total
    x_ref[...] = x
    rows = x.shape[0]
    z_ref[:rows] = x
    diag = None
    for i, slot in enumerate(own):
        term = dot_split(
            (fh_ref[slot], fl_ref[slot]), split(total[i * depth : (i + 1) * depth]), TN
        )
        diag = term if diag is None else diag + term
    block = diag.shape[0]
    z_ref[rows : rows + block] = diag
    z_ref[rows + block :] = dinv_ref[...]


def parent_kernel(nrow, ncol, *refs):
    z_refs = refs[:ncol]
    parent_ref, lower_ref, dinv_ref, c_ref, t_ref, e_ref, sel_ref = refs[ncol:]
    c = lax.axis_index("col")
    slot = parent_ref[c] ^ c
    for j in range(ncol):

        @pl.when(slot == j)
        def _(j=j):
            sel_ref[...] = z_refs[j][...]

    lower = split(lower_ref[...])
    block = lower_ref.shape[0]
    rows = c_ref.shape[0]
    product = dot_split(split(sel_ref[...]), lower, NN)
    c_ref[...] = product[:rows]
    t_ref[...] = dot_split(lower, split(product[rows : rows + block]), TN)
    e_ref[...] = dinv_ref[...] + dot_split(lower, split(product[rows + block :]), TN)


def second_kernel(nrow, ncol, *refs):
    s_refs = refs[:ncol]
    rh_ref, rl_ref, c_ref, t_ref, z_ref, y_ref, m_ref, sh_ref, sl_ref = refs[ncol:]
    base, own, _ = slots(nrow, ncol)
    depth = s_refs[0].shape[0]
    for t in range(ncol):
        slot = base ^ t
        sh_ref[slot], sl_ref[slot] = split(s_refs[t][...])
    total = c_ref[...]
    for j in range(ncol):
        total += dot_split((rh_ref[j], rl_ref[j]), (sh_ref[j], sl_ref[j]), NN)
    y_ref[...] = -total
    coupling = c_ref[...]
    diag = t_ref[...]
    for i, slot in enumerate(own):
        mine = (sh_ref[slot], sl_ref[slot])
        here = slice(i * depth, (i + 1) * depth)
        diag += dot_split(mine, split(total[here]), TN)
        diag += dot_split(split(coupling[here]), mine, TN)
    rows = c_ref.shape[0]
    block = diag.shape[0]
    across = lax.broadcasted_iota(jnp.int32, diag.shape, 1)
    down = lax.broadcasted_iota(jnp.int32, diag.shape, 0)
    m_ref[:block] = jnp.where(down <= across, z_ref[rows : rows + block], diag)
    line = jnp.sum(jnp.where(down == across, diag, 0.0), axis=0, keepdims=True)
    m_ref[block:] = jnp.broadcast_to(line, (m_ref.shape[0] - block, line.shape[1]))


def last_kernel(m_ref, dinv_ref, e_ref, one_ref, two_ref):
    block = dinv_ref.shape[0]
    m = m_ref[:block]
    across = lax.broadcasted_iota(jnp.int32, m.shape, 1)
    down = lax.broadcasted_iota(jnp.int32, m.shape, 0)
    turned = m.T
    one_ref[...] = dinv_ref[...] + jnp.where(down <= across, m, turned)
    line = jnp.broadcast_to(m_ref[block : block + 1], m.shape)
    two_ref[...] = e_ref[...] + jnp.where(
        down == across, line, jnp.where(down > across, m, turned)
    )


def call(kernel, outs, scratch, *args):
    size = 0
    for shape, dtype in [(a.shape, a.dtype) for a in args] + outs + scratch:
        if len(shape) > 1:
            count = 1
            for extent in shape:
                count *= extent
            size += count * jnp.dtype(dtype).itemsize
    limit = min(56 << 20, 3 * size + (4 << 20))
    return pl.pallas_call(
        kernel,
        out_shape=[jax.ShapeDtypeStruct(shape, dtype) for shape, dtype in outs],
        in_specs=[SMEM if a.ndim == 1 else VMEM for a in args],
        out_specs=[VMEM] * len(outs),
        scratch_shapes=[pltpu.VMEM(shape, dtype) for shape, dtype in scratch],
        compiler_params=pltpu.CompilerParams(vmem_limit_bytes=limit),
        cost_estimate=pl.CostEstimate(flops=4 * size * 64, bytes_accessed=size, transcendentals=0),
    )(*args)


def masked(values, pattern):
    rows, cols = pattern.shape
    grid = values.reshape(rows, values.shape[0] // rows, cols, values.shape[1] // cols)
    return (grid * pattern.astype(jnp.float32)[:, None, :, None]).reshape(values.shape)


def swap(x, axis, size, bit):
    return lax.ppermute(x, axis, [(i, i ^ bit) for i in range(size)])


def gather_xor(x, axis, size):
    blocks = {0: x}
    bit = size // 2
    while bit:
        for j in sorted(blocks):
            blocks[j ^ bit] = swap(blocks[j], axis, size, bit)
        bit //= 2
    return [blocks[j] for j in range(size)]


def turn(values, nrow, ncol, block):
    q = ncol // nrow
    out = []
    for t in range(ncol):
        pairs = []
        for r in range(nrow):
            for c in range(ncol):
                k = (r * q + c % q) ^ t
                pairs.append(((c // q) * ncol + k, r * ncol + c))
        part = values
        if q > 1:
            which = (lax.axis_index("col") ^ t) % q
            part = lax.dynamic_slice_in_dim(values, which * block, block, 1)
        out.append(lax.ppermute(part, ("row", "col"), pairs))
    return out


def on_device(
    nrow,
    ncol,
    inverse_root,
    lower_first,
    mask_first,
    dinv_first,
    lower_second,
    mask_second,
    parent,
    lower_parent,
    dinv_second,
):
    f32, bf16 = jnp.float32, jnp.bfloat16
    block = dinv_first.shape[0]
    rows, depth = inverse_root.shape
    first = masked(lower_first, mask_first)
    second = masked(lower_second, mask_second)
    f_parts = turn(first, nrow, ncol, block)
    r_parts = gather_xor(inverse_root, "col", ncol)
    s_parts = turn(second, nrow, ncol, block)
    halves = [((ncol, rows, depth), bf16)] * 2
    pieces = [((ncol, depth, block), bf16)] * 2
    inverse_first, z, r_high, r_low = call(
        functools.partial(first_kernel, nrow, ncol),
        [((rows, block), f32), ((rows + 2 * block, block), f32)] + halves,
        pieces,
        *r_parts,
        *f_parts,
        dinv_first,
    )
    z_parts = gather_xor(z, "col", ncol)
    coupling, parent_diag, start = call(
        functools.partial(parent_kernel, nrow, ncol),
        [((rows, block), f32), ((block, block), f32), ((block, block), f32)],
        [(z.shape, f32)],
        *z_parts,
        parent,
        lower_parent,
        dinv_second,
    )
    inverse_second, packed = call(
        functools.partial(second_kernel, nrow, ncol),
        [((rows, block), f32), ((block + 8, block), f32)],
        pieces,
        *s_parts,
        r_high,
        r_low,
        coupling,
        parent_diag,
        z,
    )
    bit = 1
    while bit < nrow:
        packed = packed + swap(packed, "row", nrow, bit)
        bit *= 2
    diag_first, diag_second = call(
        last_kernel, [((block, block), f32)] * 2, [], packed, dinv_first, start
    )
    return (inverse_first, diag_first, inverse_second, diag_second)


def solution(mesh):
    in_specs = (
        P(("pole", "row"), "col"),
        P(("pole", "col"), "row"),
        P("col", "row"),
        P("pole", "col"),
        P(("pole", "col"), "row"),
        P("col", "row"),
        P(),
        P("pole", "col"),
        P("pole", "col"),
    )
    out_specs = (
        P(("pole", "row"), "col"),
        P("pole", "col"),
        P(("pole", "row"), "col"),
        P("pole", "col"),
    )
    return jax.shard_map(
        functools.partial(on_device, mesh.shape["row"], mesh.shape["col"]),
        mesh=mesh,
        in_specs=in_specs,
        out_specs=out_specs,
        check_vma=False,
    )
```

time: 136 us -> 66.6 us (0.49)
  blocking collectives: 47.9 us -> 0 us
  starting transfers between devices: 7.21 us -> 39.5 us
  waiting for transfers between devices: 44.6 us -> 18.1 us
  between operations: 14 us -> 0.75 us
  matrix products: 9.6 us -> 0 us
  local copies, waits for them, and re-layouts: 9.05 us -> 1.01 us
  Pallas kernels: 0 us -> 4.5 us
  other arithmetic: 3.42 us -> 1.77 us
    all_gather x4 -> x0, blocking collectives: 47.9 us -> none  [the longest x1 18 us: on_device(): lax.all_gather(first, 'row', axis=1, tiled=True)]
    ppermute x0 -> x16, starting transfers between devices: none -> 39.5 us  [the longest x8 21.3 us: swap(): return lax.ppermute(x, axis, [(i, i ^ bit) for i in range(size)])]
    psum x1 -> x0, waiting for transfers between devices: 31.5 us -> none  [on_device(): diag_first = dinv_first - lax.psum(first_terms, 'row')]
    ppermute x0 -> x16, waiting for transfers between devices: none -> 18.1 us  [the longest x8 11.4 us: swap(): return lax.ppermute(x, axis, [(i, i ^ bit) for i in range(size)])]
    dot_general x9 -> x0, matrix products: 9.6 us -> none  [the longest x4 2.49 us: diag_blocks(): jnp.einsum('rkb,rkc->bkc', left_cube, right_cube, precision=highest)]
    reduce_scatter x2 -> x0, waiting for transfers between devices: 9.11 us -> none  [the longest x1 9.09 us: on_device(): lax.psum_scatter(second_part, 'col', scatter_dimension=1, tiled=True)]
    all_to_all x2 -> x0, starting transfers between devices: 7.08 us -> none  [the longest x1 3.61 us: on_device(): lax.all_to_all(first_full, 'col', split_axis=1, concat_axis=0, tiled=True)]
    unnamed x28 -> x14, local copies, waits for them, and re-layouts: 7.68 us -> 0.86 us
  transfers between devices with their start and end apart: 5 -> 16, of which waited for: 3 -> 7; matrix products, arithmetic and copies ran while one was open for 6% -> 3% of each run, Pallas kernels for 0% -> 2%
where the time goes in v1:
time: 66.6 us; the launch traced here: 65.6 us
  starting transfers between devices  39.5 us (59%)
  waiting for transfers between devices  18.1 us (27%)
  Pallas kernels  4.5 us (7%)
  other arithmetic  1.77 us (3%)
  local copies, waits for them, and re-layouts  1.01 us (2%)
  between operations  0.75 us (1%)
    ppermute x8, starting transfers between devices, swap(): return lax.ppermute(x, axis, [(i, i ^ bit) for i in range(size)])  21.3 us
    ppermute x8, starting transfers between devices, turn(): out.append(lax.ppermute(part, ('row', 'col'), pairs))  18.2 us
    ppermute x8, waiting for transfers between devices, swap(): return lax.ppermute(x, axis, [(i, i ^ bit) for i in range(size)])  11.4 us
    ppermute x8, waiting for transfers between devices, turn(): out.append(lax.ppermute(part, ('row', 'col'), pairs))  6.71 us
    pallas_call x4, Pallas kernels, call(): pl.pallas_call(kernel, out_shape=[jax.ShapeDtypeStruct(shape, dtype) for...  4.5 us
    mul x4, other arithmetic, masked(): grid * pattern.astype(jnp.float32)[:, None, :, None]  1.75 us
  transfers between devices with their start and end apart: 16, of which 7 were waited for; matrix products, arithmetic and copies ran while one was open for 3% of the time, Pallas kernels for 2%

profile of v1, /device:TPU:0, one launch (start us, length us, event | category | flops | bytes accessed | tf_op | source)
XLA Modules:
  0.0 65.6 jit_solution(6142443945863706170)
XLA Ops:
  0.6 3.0 %collective-permute-start.1 = (f32[256,256]{1,0:T(8,128)}, f32[256,256]{1,0:T(8,128)S(1)}, u32[]{:S(2)}, u32[]{:S(2)}) collective-permute-start(f32[256,256]{1,0:T(8,128)} %refs_0_.1), channel_id=1, source_target_pairs={{0,2},{1,3},{2,0},{3,1},{4,6},{5,7},{6,4},{7,5},{8,10},{9,11},{10,... | collective-permute-start | bytes 786440 | tf_op jit(solution)/shard_map/ppermute | solution.py:156
  4.4 1.0 %broadcast_multiply_fusion.1 = f32[256,128]{1,0:T(8,128)S(1)} fusion(f32[256,128]{1,0:T(8,128)} %param.10, f32[256]{0:T(256)S(1)} %broadcast_bitcast_fusion.1), kind=kLoop, calls=%fused_computation.1 | loop fusion | flops 32768 | bytes 263168 | tf_op jit(solution)/shard_map/mul | solution.py:152
  6.1 3.0 %collective-permute-start = (f32[256,256]{1,0:T(8,128)S(1)}, f32[256,256]{1,0:T(8,128)S(1)}, u32[]{:S(2)}, u32[]{:S(2)}) collective-permute-start(f32[256,256]{1,0:T(8,128)S(1)} %copy-done), channel_id=1, source_target_pairs={{0,1},{1,0},{2,3},{3,2},{4,5},{5,4},{6,7},{7,6},{8,9},{9,8},{10,11... | collective-permute-start | bytes 786440 | tf_op jit(solution)/shard_map/ppermute | solution.py:156
  9.1 1.1 %collective-permute-done.1.refs_2_ = f32[256,256]{1,0:T(8,128)S(1)} collective-permute-done((f32[256,256]{1,0:T(8,128)}, f32[256,256]{1,0:T(8,128)S(1)}, u32[]{:S(2)}, u32[]{:S(2)}) %collective-permute-start.1) | collective-permute-done | bytes 262176 | tf_op jit(solution)/shard_map/ppermute | solution.py:156
  10.2 1.8 %collective-permute-start.4 = (f32[256,128]{1,0:T(8,128)S(1)}, f32[256,128]{1,0:T(8,128)S(1)}, u32[]{:S(2)}, u32[]{:S(2)}) collective-permute-start(f32[256,128]{1,0:T(8,128)S(1)} %broadcast_multiply_fusion.1), channel_id=1, source_target_pairs={{1,0},{5,1},{9,2},{13,3},{0,4},{4,5},{8,6},{12,7},{3,8},{7,9},{11,... | collective-permute-start | bytes 393224 | tf_op jit(solution)/shard_map/ppermute | solution.py:182
  12.0 3.8 %collective-permute-start.5 = (f32[256,128]{1,0:T(8,128)S(1)}, f32[256,128]{1,0:T(8,128)S(1)}, u32[]{:S(2)}, u32[]{:S(2)}) collective-permute-start(f32[256,128]{1,0:T(8,128)S(1)} %broadcast_multiply_fusion.1), channel_id=1, source_target_pairs={{2,0},{6,1},{10,2},{14,3},{3,4},{7,5},{11,6},{15,7},{0,8},{4,9},{8... | collective-permute-start | bytes 393224 | tf_op jit(solution)/shard_map/ppermute | solution.py:182
  15.8 3.3 %collective-permute-start.6 = (f32[256,128]{1,0:T(8,128)S(1)}, f32[256,128]{1,0:T(8,128)S(1)}, u32[]{:S(2)}, u32[]{:S(2)}) collective-permute-start(f32[256,128]{1,0:T(8,128)S(1)} %broadcast_multiply_fusion.1), channel_id=1, source_target_pairs={{3,0},{7,1},{11,2},{15,3},{2,4},{6,5},{10,6},{14,7},{1,8},{5,9},{9... | collective-permute-start | bytes 393224 | tf_op jit(solution)/shard_map/ppermute | solution.py:182
  19.1 1.7 %collective-permute-done.5.refs_6_ = f32[256,128]{1,0:T(8,128)S(1)} collective-permute-done((f32[256,128]{1,0:T(8,128)S(1)}, f32[256,128]{1,0:T(8,128)S(1)}, u32[]{:S(2)}, u32[]{:S(2)}) %collective-permute-start.5) | collective-permute-done | bytes 131104 | tf_op jit(solution)/shard_map/ppermute | solution.py:182
  20.8 1.7 %collective-permute-done.6.refs_7_ = f32[256,128]{1,0:T(8,128)S(1)} collective-permute-done((f32[256,128]{1,0:T(8,128)S(1)}, f32[256,128]{1,0:T(8,128)S(1)}, u32[]{:S(2)}, u32[]{:S(2)}) %collective-permute-start.6) | collective-permute-done | bytes 131104 | tf_op jit(solution)/shard_map/ppermute | solution.py:182
  22.5 0.8 %copy-done.3 = f32[128,128]{1,0:T(8,128)S(1)} copy-done((f32[128,128]{1,0:T(8,128)S(1)}, f32[128,128]{1,0:T(8,128)}, u32[]{:S(2)}) %copy-start.3) | copy-done | bytes 65560
  23.4 1.3 %shard_map.120 = (f32[256,128]{1,0:T(8,128)}, f32[512,128]{1,0:T(8,128)S(1)}, bf16[4,256,256]{2,1,0:T(8,128)(2,1)S(1)}, bf16[4,256,256]{2,1,0:T(8,128)(2,1)S(1)}) custom-call(f32[256,256]{1,0:T(8,128)S(1)} %copy-done, f32[256,256]{1,0:T(8,128)S(1)} %collective-permute-done.refs_1_, f32[256,256]{1,0:T(8,128)S(1)} %collective-permute-done.1.refs_2_, ...), custom_call_target="tpu_custom_call" | custom-call | flops 922746880 | bytes 3604480 | tf_op jit(solution)/shard_map/pallas_call | solution.py:138
  24.7 7.0 %collective-permute-start.12 = (f32[512,128]{1,0:T(8,128)S(1)}, f32[512,128]{1,0:T(8,128)S(1)}, u32[]{:S(2)}, u32[]{:S(2)}) collective-permute-start(f32[512,128]{1,0:T(8,128)S(1)} %get-tuple-element.18.refs_0_.refs_8_), channel_id=1, source_target_pairs={{0,2},{1,3},{2,0},{3,1},{4,6},{5,7},{6,4},{7,5},{8,10},{9,11},{10,... | collective-permute-start | bytes 786440 | tf_op jit(solution)/shard_map/ppermute | solution.py:156
  31.8 4.3 %collective-permute-done.12.refs_2_ = f32[512,128]{1,0:T(8,128)S(1)} collective-permute-done((f32[512,128]{1,0:T(8,128)S(1)}, f32[512,128]{1,0:T(8,128)S(1)}, u32[]{:S(2)}, u32[]{:S(2)}) %collective-permute-start.12) | collective-permute-done | bytes 262176 | tf_op jit(solution)/shard_map/ppermute | solution.py:156
  36.2 2.0 %collective-permute-start.10 = (f32[256,128]{1,0:T(8,128)S(1)}, f32[256,128]{1,0:T(8,128)S(1)}, u32[]{:S(2)}, u32[]{:S(2)}) collective-permute-start(f32[256,128]{1,0:T(8,128)S(1)} %broadcast_multiply_fusion), channel_id=1, source_target_pairs={{3,0},{7,1},{11,2},{15,3},{2,4},{6,5},{10,6},{14,7},{1,8},{5,9},{9... | collective-permute-start | bytes 393224 | tf_op jit(solution)/shard_map/ppermute | solution.py:182
  38.9 3.4 %collective-permute-start.8 = (f32[256,128]{1,0:T(8,128)S(1)}, f32[256,128]{1,0:T(8,128)S(1)}, u32[]{:S(2)}, u32[]{:S(2)}) collective-permute-start(f32[256,128]{1,0:T(8,128)S(1)} %broadcast_multiply_fusion), channel_id=1, source_target_pairs={{1,0},{5,1},{9,2},{13,3},{0,4},{4,5},{8,6},{12,7},{3,8},{7,9},{11,... | collective-permute-start | bytes 393224 | tf_op jit(solution)/shard_map/ppermute | solution.py:182
  42.2 2.5 %collective-permute-start.9 = (f32[256,128]{1,0:T(8,128)S(1)}, f32[256,128]{1,0:T(8,128)S(1)}, u32[]{:S(2)}, u32[]{:S(2)}) collective-permute-start(f32[256,128]{1,0:T(8,128)S(1)} %broadcast_multiply_fusion), channel_id=1, source_target_pairs={{2,0},{6,1},{10,2},{14,3},{3,4},{7,5},{11,6},{15,7},{0,8},{4,9},{8... | collective-permute-start | bytes 393224 | tf_op jit(solution)/shard_map/ppermute | solution.py:182
  44.8 1.1 %shard_map.121 = (f32[256,128]{1,0:T(8,128)S(1)}, f32[128,128]{1,0:T(8,128)S(1)}, f32[128,128]{1,0:T(8,128)S(1)}) custom-call(f32[512,128]{1,0:T(8,128)S(1)} %get-tuple-element.18.refs_0_.refs_8_, f32[512,128]{1,0:T(8,128)S(1)} %collective-permute-done.11.refs_1_, f32[512,128]{1,0:T(8,128)S(1)} %collective-permute-done.12.refs_2_, ...), custom_call_target="tpu_custom_call" | custom-call | flops 436207616 | bytes 1703936 | tf_op jit(solution)/shard_map/pallas_call | solution.py:138
  45.9 3.2 %collective-permute-done.9.refs_2_ = f32[256,128]{1,0:T(8,128)S(1)} collective-permute-done((f32[256,128]{1,0:T(8,128)S(1)}, f32[256,128]{1,0:T(8,128)S(1)}, u32[]{:S(2)}, u32[]{:S(2)}) %collective-permute-start.9) | collective-permute-done | bytes 131104 | tf_op jit(solution)/shard_map/ppermute | solution.py:182
  49.2 1.4 %shard_map.122 = (f32[256,128]{1,0:T(8,128)}, f32[136,128]{1,0:T(8,128)S(1)}) custom-call(f32[256,128]{1,0:T(8,128)S(1)} %collective-permute-done.7.refs_0_, f32[256,128]{1,0:T(8,128)S(1)} %collective-permute-done.8.refs_1_, f32[256,128]{1,0:T(8,128)S(1)} %collective-permute-done.9.refs_2_, f32[256,128]{1,0:T(8,128)S(1)} %collective-permute-done.10.refs_3_, ...), custom_call_target="tpu_custom_call" | custom-call | flops 705691648 | bytes 2756608 | tf_op jit(solution)/shard_map/pallas_call | solution.py:138
  50.5 3.0 %collective-permute-start.14 = (f32[136,128]{1,0:T(8,128)S(1)}, f32[136,128]{1,0:T(8,128)S(1)}, u32[]{:S(2)}, u32[]{:S(2)}) collective-permute-start(f32[136,128]{1,0:T(8,128)S(1)} %get-tuple-element.21), channel_id=1, source_target_pairs={{0,4},{4,0},{8,12},{12,8},{1,5},{5,1},{9,13},{13,9},{2,6},{6,2},{1... | collective-permute-start | bytes 208904 | tf_op jit(solution)/shard_map/ppermute | solution.py:156
  53.6 2.3 %collective-permute-done.14 = f32[136,128]{1,0:T(8,128)S(1)} collective-permute-done((f32[136,128]{1,0:T(8,128)S(1)}, f32[136,128]{1,0:T(8,128)S(1)}, u32[]{:S(2)}, u32[]{:S(2)}) %collective-permute-start.14) | collective-permute-done | bytes 69664 | tf_op jit(solution)/shard_map/ppermute | solution.py:156
  55.9 5.3 %collective-permute-start.15 = (f32[136,128]{1,0:T(8,128)S(1)}, f32[136,128]{1,0:T(8,128)S(1)}, u32[]{:S(2)}, u32[]{:S(2)}) collective-permute-start(f32[136,128]{1,0:T(8,128)S(1)} %add.6), channel_id=1, source_target_pairs={{0,8},{4,12},{8,0},{12,4},{1,9},{5,13},{9,1},{13,5},{2,10},{6,14},... | collective-permute-start | bytes 208904 | tf_op jit(solution)/shard_map/ppermute | solution.py:156
  61.2 3.7 %collective-permute-done.15 = f32[136,128]{1,0:T(8,128)S(1)} collective-permute-done((f32[136,128]{1,0:T(8,128)S(1)}, f32[136,128]{1,0:T(8,128)S(1)}, u32[]{:S(2)}, u32[]{:S(2)}) %collective-permute-start.15) | collective-permute-done | bytes 69664 | tf_op jit(solution)/shard_map/ppermute | solution.py:156
  64.9 0.8 %shard_map.123 = (f32[128,128]{1,0:T(8,128)}, f32[128,128]{1,0:T(8,128)}) custom-call(f32[136,128]{1,0:T(8,128)S(1)} %add.7.m_ref, f32[128,128]{1,0:T(8,128)S(1)} %copy-done.3, f32[128,128]{1,0:T(8,128)S(1)} %get-tuple-element.22.e_ref), custom_call_target="tpu_custom_call" | custom-call | flops 84934656 | bytes 331776 | tf_op jit(solution)/shard_map/pallas_call | solution.py:138
  (34 shorter events, 2.3 us)
Async XLA Ops:
  0.6 5.4 %copy-start = (f32[256,256]{1,0:T(8,128)S(1)}, f32[256,256]{1,0:T(8,128)}, u32[]{:S(2)}) copy-start(f32[256,256]{1,0:T(8,128)} %refs_0_.1) | copy-start | bytes 786436
  0.6 9.5 %collective-permute-start.1 = (f32[256,256]{1,0:T(8,128)}, f32[256,256]{1,0:T(8,128)S(1)}, u32[]{:S(2)}, u32[]{:S(2)}) collective-permute-start(f32[256,256]{1,0:T(8,128)} %refs_0_.1), channel_id=1, source_target_pairs={{0,2},{1,3},{2,0},{3,1},{4,6},{5,7},{6,4},{7,5},{8,10},{9,11},{10,... | collective-permute-start | bytes 786440 | tf_op jit(solution)/shard_map/ppermute | solution.py:156
  5.4 10.4 %collective-permute-start.3 = (f32[256,128]{1,0:T(8,128)S(1)}, f32[256,128]{1,0:T(8,128)S(1)}, u32[]{:S(2)}, u32[]{:S(2)}) collective-permute-start(f32[256,128]{1,0:T(8,128)S(1)} %broadcast_multiply_fusion.1), channel_id=1, source_target_pairs={{0,0},{4,1},{8,2},{12,3},{1,4},{5,5},{9,6},{13,7},{2,8},{6,9},{10,... | collective-permute-start | bytes 393224 | tf_op jit(solution)/shard_map/ppermute | solution.py:182
  6.1 16.5 %collective-permute-start = (f32[256,256]{1,0:T(8,128)S(1)}, f32[256,256]{1,0:T(8,128)S(1)}, u32[]{:S(2)}, u32[]{:S(2)}) collective-permute-start(f32[256,256]{1,0:T(8,128)S(1)} %copy-done), channel_id=1, source_target_pairs={{0,1},{1,0},{2,3},{3,2},{4,5},{5,4},{6,7},{7,6},{8,9},{9,8},{10,11... | collective-permute-start | bytes 786440 | tf_op jit(solution)/shard_map/ppermute | solution.py:156
  10.2 12.4 %collective-permute-start.2 = (f32[256,256]{1,0:T(8,128)S(1)}, f32[256,256]{1,0:T(8,128)S(1)}, u32[]{:S(2)}, u32[]{:S(2)}) collective-permute-start(f32[256,256]{1,0:T(8,128)S(1)} %collective-permute-done.1.refs_2_), channel_id=1, source_target_pairs={{0,1},{1,0},{2,3},{3,2},{4,5},{5,4},{6,7},{7,6},{8,9},{9,8},{10,11... | collective-permute-start | bytes 786440 | tf_op jit(solution)/shard_map/ppermute | solution.py:156
  10.2 8.9 %collective-permute-start.4 = (f32[256,128]{1,0:T(8,128)S(1)}, f32[256,128]{1,0:T(8,128)S(1)}, u32[]{:S(2)}, u32[]{:S(2)}) collective-permute-start(f32[256,128]{1,0:T(8,128)S(1)} %broadcast_multiply_fusion.1), channel_id=1, source_target_pairs={{1,0},{5,1},{9,2},{13,3},{0,4},{4,5},{8,6},{12,7},{3,8},{7,9},{11,... | collective-permute-start | bytes 393224 | tf_op jit(solution)/shard_map/ppermute | solution.py:182
  12.0 8.8 %collective-permute-start.5 = (f32[256,128]{1,0:T(8,128)S(1)}, f32[256,128]{1,0:T(8,128)S(1)}, u32[]{:S(2)}, u32[]{:S(2)}) collective-permute-start(f32[256,128]{1,0:T(8,128)S(1)} %broadcast_multiply_fusion.1), channel_id=1, source_target_pairs={{2,0},{6,1},{10,2},{14,3},{3,4},{7,5},{11,6},{15,7},{0,8},{4,9},{8... | collective-permute-start | bytes 393224 | tf_op jit(solution)/shard_map/ppermute | solution.py:182
  15.8 6.7 %collective-permute-start.6 = (f32[256,128]{1,0:T(8,128)S(1)}, f32[256,128]{1,0:T(8,128)S(1)}, u32[]{:S(2)}, u32[]{:S(2)}) collective-permute-start(f32[256,128]{1,0:T(8,128)S(1)} %broadcast_multiply_fusion.1), channel_id=1, source_target_pairs={{3,0},{7,1},{11,2},{15,3},{2,4},{6,5},{10,6},{14,7},{1,8},{5,9},{9... | collective-permute-start | bytes 393224 | tf_op jit(solution)/shard_map/ppermute | solution.py:182
  22.5 0.8 %copy-start.3 = (f32[128,128]{1,0:T(8,128)S(1)}, f32[128,128]{1,0:T(8,128)}, u32[]{:S(2)}) copy-start(f32[128,128]{1,0:T(8,128)} %dinv_ref.1) | copy-start | bytes 196612
  23.4 12.7 %copy-start.5 = (f32[256,128]{1,0:T(8,128)S(1)}, f32[256,128]{1,0:T(8,128)}, u32[]{:S(2)}) copy-start(f32[256,128]{1,0:T(8,128)} %param.13) | copy-start | bytes 393220
  24.7 7.0 %copy-start.6 = (s32[2,1]{0,1:T(1,128)S(1)}, s32[2,1]{0,1:T(1,128)}, u32[]{:S(2)}) copy-start(s32[2,1]{0,1:T(1,128)} %param.14) | copy-start | bytes 28
  24.7 11.4 %collective-permute-start.12 = (f32[512,128]{1,0:T(8,128)S(1)}, f32[512,128]{1,0:T(8,128)S(1)}, u32[]{:S(2)}, u32[]{:S(2)}) collective-permute-start(f32[512,128]{1,0:T(8,128)S(1)} %get-tuple-element.18.refs_0_.refs_8_), channel_id=1, source_target_pairs={{0,2},{1,3},{2,0},{3,1},{4,6},{5,7},{6,4},{7,5},{8,10},{9,11},{10,... | collective-permute-start | bytes 786440 | tf_op jit(solution)/shard_map/ppermute | solution.py:156
  31.7 10.5 %collective-permute-start.11 = (f32[512,128]{1,0:T(8,128)S(1)}, f32[512,128]{1,0:T(8,128)S(1)}, u32[]{:S(2)}, u32[]{:S(2)}) collective-permute-start(f32[512,128]{1,0:T(8,128)S(1)} %get-tuple-element.18.refs_0_.refs_8_), channel_id=1, source_target_pairs={{0,1},{1,0},{2,3},{3,2},{4,5},{5,4},{6,7},{7,6},{8,9},{9,8},{10,11... | collective-permute-start | bytes 786440 | tf_op jit(solution)/shard_map/ppermute | solution.py:156
  31.8 13.0 %copy-start.1 = (f32[128,128]{1,0:T(8,128)S(1)}, f32[128,128]{1,0:T(8,128)}, u32[]{:S(2)}) copy-start(f32[128,128]{1,0:T(8,128)} %refs_5_.1) | copy-start | bytes 196612
  31.8 13.0 %copy-start.2 = (f32[128,128]{1,0:T(8,128)S(1)}, f32[128,128]{1,0:T(8,128)}, u32[]{:S(2)}) copy-start(f32[128,128]{1,0:T(8,128)} %refs_6_.1) | copy-start | bytes 196612
  31.8 13.0 %copy-start.4 = (s32[4]{0:T(128)S(1)}, s32[4]{0:T(128)}, u32[]{:S(2)}) copy-start(s32[4]{0:T(128)} %refs_4_.1) | copy-start | bytes 52
  36.1 8.7 %collective-permute-start.13 = (f32[512,128]{1,0:T(8,128)S(1)}, f32[512,128]{1,0:T(8,128)S(1)}, u32[]{:S(2)}, u32[]{:S(2)}) collective-permute-start(f32[512,128]{1,0:T(8,128)S(1)} %collective-permute-done.12.refs_2_), channel_id=1, source_target_pairs={{0,1},{1,0},{2,3},{3,2},{4,5},{5,4},{6,7},{7,6},{8,9},{9,8},{10,11... | collective-permute-start | bytes 786440 | tf_op jit(solution)/shard_map/ppermute | solution.py:156
  36.2 9.7 %collective-permute-start.10 = (f32[256,128]{1,0:T(8,128)S(1)}, f32[256,128]{1,0:T(8,128)S(1)}, u32[]{:S(2)}, u32[]{:S(2)}) collective-permute-start(f32[256,128]{1,0:T(8,128)S(1)} %broadcast_multiply_fusion), channel_id=1, source_target_pairs={{3,0},{7,1},{11,2},{15,3},{2,4},{6,5},{10,6},{14,7},{1,8},{5,9},{9... | collective-permute-start | bytes 393224 | tf_op jit(solution)/shard_map/ppermute | solution.py:182
  38.2 7.7 %collective-permute-start.7 = (f32[256,128]{1,0:T(8,128)S(1)}, f32[256,128]{1,0:T(8,128)S(1)}, u32[]{:S(2)}, u32[]{:S(2)}) collective-permute-start(f32[256,128]{1,0:T(8,128)S(1)} %broadcast_multiply_fusion), channel_id=1, source_target_pairs={{0,0},{4,1},{8,2},{12,3},{1,4},{5,5},{9,6},{13,7},{2,8},{6,9},{10,... | collective-permute-start | bytes 393224 | tf_op jit(solution)/shard_map/ppermute | solution.py:182
  38.9 7.0 %collective-permute-start.8 = (f32[256,128]{1,0:T(8,128)S(1)}, f32[256,128]{1,0:T(8,128)S(1)}, u32[]{:S(2)}, u32[]{:S(2)}) collective-permute-start(f32[256,128]{1,0:T(8,128)S(1)} %broadcast_multiply_fusion), channel_id=1, source_target_pairs={{1,0},{5,1},{9,2},{13,3},{0,4},{4,5},{8,6},{12,7},{3,8},{7,9},{11,... | collective-permute-start | bytes 393224 | tf_op jit(solution)/shard_map/ppermute | solution.py:182
  42.2 6.9 %collective-permute-start.9 = (f32[256,128]{1,0:T(8,128)S(1)}, f32[256,128]{1,0:T(8,128)S(1)}, u32[]{:S(2)}, u32[]{:S(2)}) collective-permute-start(f32[256,128]{1,0:T(8,128)S(1)} %broadcast_multiply_fusion), channel_id=1, source_target_pairs={{2,0},{6,1},{10,2},{14,3},{3,4},{7,5},{11,6},{15,7},{0,8},{4,9},{8... | collective-permute-start | bytes 393224 | tf_op jit(solution)/shard_map/ppermute | solution.py:182
  50.5 5.4 %collective-permute-start.14 = (f32[136,128]{1,0:T(8,128)S(1)}, f32[136,128]{1,0:T(8,128)S(1)}, u32[]{:S(2)}, u32[]{:S(2)}) collective-permute-start(f32[136,128]{1,0:T(8,128)S(1)} %get-tuple-element.21), channel_id=1, source_target_pairs={{0,4},{4,0},{8,12},{12,8},{1,5},{5,1},{9,13},{13,9},{2,6},{6,2},{1... | collective-permute-start | bytes 208904 | tf_op jit(solution)/shard_map/ppermute | solution.py:156
  55.9 8.9 %collective-permute-start.15 = (f32[136,128]{1,0:T(8,128)S(1)}, f32[136,128]{1,0:T(8,128)S(1)}, u32[]{:S(2)}, u32[]{:S(2)}) collective-permute-start(f32[136,128]{1,0:T(8,128)S(1)} %add.6), channel_id=1, source_target_pairs={{0,8},{4,12},{8,0},{12,4},{1,9},{5,13},{9,1},{13,5},{2,10},{6,14},... | collective-permute-start | bytes 208904 | tf_op jit(solution)/shard_map/ppermute | solution.py:156

commit v2 on v1

--- a/solution.py
+++ b/solution.py
@@ -38,21 +38,26 @@
 
 def first_kernel(nrow, ncol, *refs):
     r_refs, f_refs = refs[:ncol], refs[ncol : 2 * ncol]
-    dinv_ref, x_ref, z_ref, rh_ref, rl_ref, fh_ref, fl_ref = refs[2 * ncol :]
-    base, own, _ = slots(nrow, ncol)
+    parent_ref, lower_ref, dinv_ref, x_ref, z_ref, e_ref, rh_ref, rl_ref, fh_ref, fl_ref, sel_ref = refs[
+        2 * ncol :
+    ]
+    base, own, c = slots(nrow, ncol)
     depth = f_refs[0].shape[0]
+    rows = x_ref.shape[0]
+    block = dinv_ref.shape[0]
+    fold = depth // block
+    chosen = parent_ref[c] ^ c
     for t in range(ncol):
         slot = base ^ t
         fh_ref[slot], fl_ref[slot] = split(f_refs[t][...])
     total = None
     for j in range(ncol):
-        parts = split(r_refs[j][...])
+        parts = split(r_refs[j][:rows])
         rh_ref[j], rl_ref[j] = parts
         term = dot_split(parts, (fh_ref[j], fl_ref[j]), NN)
         total = term if total is None else total + term
     x = -total
     x_ref[...] = x
-    rows = x.shape[0]
     z_ref[:rows] = x
     diag = None
     for i, slot in enumerate(own):
@@ -60,29 +65,29 @@
             (fh_ref[slot], fl_ref[slot]), split(total[i * depth : (i + 1) * depth]), TN
         )
         diag = term if diag is None else diag + term
-    block = diag.shape[0]
-    z_ref[rows : rows + block] = diag
-    z_ref[rows + block :] = dinv_ref[...]
-
-
-def parent_kernel(nrow, ncol, *refs):
-    z_refs = refs[:ncol]
-    parent_ref, lower_ref, dinv_ref, c_ref, t_ref, e_ref, sel_ref = refs[ncol:]
-    c = lax.axis_index("col")
-    slot = parent_ref[c] ^ c
+    z_ref[rows:] = diag
     for j in range(ncol):
 
-        @pl.when(slot == j)
+        @pl.when(chosen == j)
         def _(j=j):
-            sel_ref[...] = z_refs[j][...]
+            for i in range(fold):
+                sel_ref[i * (block // fold) : (i + 1) * (block // fold)] = r_refs[j][
+                    rows:, i * block : (i + 1) * block
+                ]
 
     lower = split(lower_ref[...])
-    block = lower_ref.shape[0]
-    rows = c_ref.shape[0]
     product = dot_split(split(sel_ref[...]), lower, NN)
+    e_ref[...] = dinv_ref[...] + dot_split(lower, split(product), TN)
+
+
+def parent_kernel(z_ref, parent_ref, lower_ref, c_ref, t_ref):
+    rows, block = c_ref.shape
+    height = rows + block
+    first = pl.multiple_of(parent_ref[lax.axis_index("col")] * height, block)
+    lower = split(lower_ref[...])
+    product = dot_split(split(z_ref[pl.ds(first, height)]), lower, NN)
     c_ref[...] = product[:rows]
-    t_ref[...] = dot_split(lower, split(product[rows : rows + block]), TN)
-    e_ref[...] = dinv_ref[...] + dot_split(lower, split(product[rows + block :]), TN)
+    t_ref[...] = dot_split(lower, split(product[rows:]), TN)
 
 
 def second_kernel(nrow, ncol, *refs):
@@ -126,7 +131,7 @@
     )
 
 
-def call(kernel, outs, scratch, *args):
+def call(kernel, outs, scratch, *args, flops=0):
     size = 0
     for shape, dtype in [(a.shape, a.dtype) for a in args] + outs + scratch:
         if len(shape) > 1:
@@ -142,7 +147,7 @@
         out_specs=[VMEM] * len(outs),
         scratch_shapes=[pltpu.VMEM(shape, dtype) for shape, dtype in scratch],
         compiler_params=pltpu.CompilerParams(vmem_limit_bytes=limit),
-        cost_estimate=pl.CostEstimate(flops=4 * size * 64, bytes_accessed=size, transcendentals=0),
+        cost_estimate=pl.CostEstimate(flops=flops, bytes_accessed=size, transcendentals=0),
     )(*args)
 
 
@@ -202,27 +207,31 @@
     first = masked(lower_first, mask_first)
     second = masked(lower_second, mask_second)
     f_parts = turn(first, nrow, ncol, block)
-    r_parts = gather_xor(inverse_root, "col", ncol)
+    fold = depth // block
+    folded = jnp.concatenate(
+        [dinv_first[i * (block // fold) : (i + 1) * (block // fold)] for i in range(fold)], 1
+    )
+    r_parts = gather_xor(jnp.concatenate([inverse_root, folded], 0), "col", ncol)
     s_parts = turn(second, nrow, ncol, block)
     halves = [((ncol, rows, depth), bf16)] * 2
     pieces = [((ncol, depth, block), bf16)] * 2
-    inverse_first, z, r_high, r_low = call(
+    inverse_first, z, start, r_high, r_low = call(
         functools.partial(first_kernel, nrow, ncol),
-        [((rows, block), f32), ((rows + 2 * block, block), f32)] + halves,
-        pieces,
+        [((rows, block), f32), ((rows + block, block), f32), ((block, block), f32)] + halves,
+        pieces + [((block, block), f32)],
         *r_parts,
         *f_parts,
-        dinv_first,
-    )
-    z_parts = gather_xor(z, "col", ncol)
-    coupling, parent_diag, start = call(
-        functools.partial(parent_kernel, nrow, ncol),
-        [((rows, block), f32), ((block, block), f32), ((block, block), f32)],
-        [(z.shape, f32)],
-        *z_parts,
         parent,
         lower_parent,
         dinv_second,
+    )
+    coupling, parent_diag = call(
+        parent_kernel,
+        [((rows, block), f32), ((block, block), f32)],
+        [],
+        lax.all_gather(z, "col", axis=0, tiled=True),
+        parent,
+        lower_parent,
     )
     inverse_second, packed = call(
         functools.partial(second_kernel, nrow, ncol),

time: 66.6 us -> 57.3 us (0.86); the launches traced: 65.6 us -> 57 us
  waiting for transfers between devices: 18.1 us -> 7.12 us
  blocking collectives: 0 us -> 7.34 us
  starting transfers between devices: 39.5 us -> 34.5 us
    ppermute x8 -> x5, starting transfers between devices: 21.3 us -> 9.74 us  [swap(): return lax.ppermute(x, axis, [(i, i ^ bit) for i in range(size)])]
    all_gather x0 -> x1, blocking collectives: none -> 7.34 us  [on_device(): lax.all_gather(z, 'col', axis=0, tiled=True)]
    ppermute x8, starting transfers between devices: 18.2 us -> 24.8 us  [turn(): out.append(lax.ppermute(part, ('row', 'col'), pairs))]
    ppermute x8, waiting for transfers between devices: 6.71 us -> 0.43 us  [turn(): out.append(lax.ppermute(part, ('row', 'col'), pairs))]
    ppermute x8 -> x5, waiting for transfers between devices: 11.4 us -> 6.69 us  [swap(): return lax.ppermute(x, axis, [(i, i ^ bit) for i in range(size)])]
    mul x4, other arithmetic: 1.75 us -> 0.19 us  [masked(): grid * pattern.astype(jnp.float32)[:, None, :, None]]
    concatenate x0 -> x1, other arithmetic: none -> 1.01 us  [on_device(): jnp.concatenate([inverse_root, folded], 0)]
    unnamed x14 -> x16, local copies, waits for them, and re-layouts: 0.86 us -> 0.03 us
  transfers between devices with their start and end apart: 16 -> 13, of which waited for: 7 -> 4; matrix products, arithmetic and copies ran while one was open for 3% -> 1% of each run, Pallas kernels for 2% -> 5%
where the time goes in v2:
time: 57.3 us; the launch traced here: 57 us
  starting transfers between devices  34.5 us (60%)
  blocking collectives  7.34 us (13%)
  waiting for transfers between devices  7.12 us (12%)
  Pallas kernels  5.14 us (9%)
  other arithmetic  1.23 us (2%)
  local copies, waits for them, and re-layouts  0.95 us (2%)
  between operations  0.77 us (1%)
    ppermute x8, starting transfers between devices, turn(): out.append(lax.ppermute(part, ('row', 'col'), pairs))  24.8 us
    ppermute x5, starting transfers between devices, swap(): return lax.ppermute(x, axis, [(i, i ^ bit) for i in range(size)])  9.74 us
    all_gather x1, blocking collectives, on_device(): lax.all_gather(z, 'col', axis=0, tiled=True)  7.34 us
    ppermute x5, waiting for transfers between devices, swap(): return lax.ppermute(x, axis, [(i, i ^ bit) for i in range(size)])  6.69 us
    pallas_call x4, Pallas kernels, call(): pl.pallas_call(kernel, out_shape=[jax.ShapeDtypeStruct(shape, dtype) for...  5.14 us
  transfers between devices with their start and end apart: 13, of which 4 were waited for; matrix products, arithmetic and copies ran while one was open for 1% of the time, Pallas kernels for 5%

profile of v2, /device:TPU:0, one launch (start us, length us, event | category | flops | bytes accessed | tf_op | source)
XLA Modules:
  0.0 57.0 jit_solution(6886750981170534792)
XLA Ops:
  0.6 0.8 %fusion = (f32[64,128]{1,0:T(8,128)S(1)}, f32[64,128]{1,0:T(8,128)S(1)}) fusion(f32[128,128]{1,0:T(8,128)} %dinv_ref.1), kind=kLoop, calls=%fused_computation.7 | loop fusion | bytes 131072 | tf_op jit(solution)/shard_map/slice | solution.py:212
  1.4 1.0 %maximum_maximum_fusion.refs_0_ = f32[320,256]{1,0:T(8,128)S(1)} fusion(f32[64,128]{1,0:T(8,128)S(1)} %get-tuple-element.27, f32[64,128]{1,0:T(8,128)S(1)} %get-tuple-element.26, f32[256,256]{1,0:T(8,128)} %param.9), kind=kLoop, calls=%fused_computation | loop fusion | flops 163840 | bytes 655360 | tf_op jit(solution)/shard_map/concatenate | solution.py:214
  2.4 3.0 %collective-permute-start.1 = (f32[320,256]{1,0:T(8,128)S(1)}, f32[320,256]{1,0:T(8,128)S(1)}, u32[]{:S(2)}, u32[]{:S(2)}) collective-permute-start(f32[320,256]{1,0:T(8,128)S(1)} %maximum_maximum_fusion.refs_0_), channel_id=1, source_target_pairs={{0,2},{1,3},{2,0},{3,1},{4,6},{5,7},{6,4},{7,5},{8,10},{9,11},{10,... | collective-permute-start | bytes 983048 | tf_op jit(solution)/shard_map/ppermute | solution.py:161
  5.5 0.1 broadcast_multiply_fusion.1
  5.6 0.7 %collective-permute-start.3 = (f32[256,128]{1,0:T(8,128)S(1)}, f32[256,128]{1,0:T(8,128)S(1)}, u32[]{:S(2)}, u32[]{:S(2)}) collective-permute-start(f32[256,128]{1,0:T(8,128)S(1)} %broadcast_multiply_fusion.1), channel_id=1, source_target_pairs={{0,0},{4,1},{8,2},{12,3},{1,4},{5,5},{9,6},{13,7},{2,8},{6,9},{10,... | collective-permute-start | bytes 393224 | tf_op jit(solution)/shard_map/ppermute | solution.py:187
  6.3 3.4 %collective-permute-start.4 = (f32[256,128]{1,0:T(8,128)S(1)}, f32[256,128]{1,0:T(8,128)S(1)}, u32[]{:S(2)}, u32[]{:S(2)}) collective-permute-start(f32[256,128]{1,0:T(8,128)S(1)} %broadcast_multiply_fusion.1), channel_id=1, source_target_pairs={{1,0},{5,1},{9,2},{13,3},{0,4},{4,5},{8,6},{12,7},{3,8},{7,9},{11,... | collective-permute-start | bytes 393224 | tf_op jit(solution)/shard_map/ppermute | solution.py:187
  9.7 3.5 %collective-permute-start.5 = (f32[256,128]{1,0:T(8,128)S(1)}, f32[256,128]{1,0:T(8,128)S(1)}, u32[]{:S(2)}, u32[]{:S(2)}) collective-permute-start(f32[256,128]{1,0:T(8,128)S(1)} %broadcast_multiply_fusion.1), channel_id=1, source_target_pairs={{2,0},{6,1},{10,2},{14,3},{3,4},{7,5},{11,6},{15,7},{0,8},{4,9},{8... | collective-permute-start | bytes 393224 | tf_op jit(solution)/shard_map/ppermute | solution.py:187
  13.2 0.6 %collective-permute-done.1.refs_2_ = f32[320,256]{1,0:T(8,128)S(1)} collective-permute-done((f32[320,256]{1,0:T(8,128)S(1)}, f32[320,256]{1,0:T(8,128)S(1)}, u32[]{:S(2)}, u32[]{:S(2)}) %collective-permute-start.1) | collective-permute-done | bytes 327712 | tf_op jit(solution)/shard_map/ppermute | solution.py:161
  13.8 1.2 %collective-permute-start.2 = (f32[320,256]{1,0:T(8,128)S(1)}, f32[320,256]{1,0:T(8,128)S(1)}, u32[]{:S(2)}, u32[]{:S(2)}) collective-permute-start(f32[320,256]{1,0:T(8,128)S(1)} %collective-permute-done.1.refs_2_), channel_id=1, source_target_pairs={{0,1},{1,0},{2,3},{3,2},{4,5},{5,4},{6,7},{7,6},{8,9},{9,8},{10,11... | collective-permute-start | bytes 983048 | tf_op jit(solution)/shard_map/ppermute | solution.py:161
  15.1 4.5 %collective-permute-start.6 = (f32[256,128]{1,0:T(8,128)S(1)}, f32[256,128]{1,0:T(8,128)S(1)}, u32[]{:S(2)}, u32[]{:S(2)}) collective-permute-start(f32[256,128]{1,0:T(8,128)S(1)} %broadcast_multiply_fusion.1), channel_id=1, source_target_pairs={{3,0},{7,1},{11,2},{15,3},{2,4},{6,5},{10,6},{14,7},{1,8},{5,9},{9... | collective-permute-start | bytes 393224 | tf_op jit(solution)/shard_map/ppermute | solution.py:187
  19.8 2.0 %collective-permute-start.10 = (f32[256,128]{1,0:T(8,128)S(1)}, f32[256,128]{1,0:T(8,128)S(1)}, u32[]{:S(2)}, u32[]{:S(2)}) collective-permute-start(f32[256,128]{1,0:T(8,128)S(1)} %broadcast_multiply_fusion), channel_id=1, source_target_pairs={{3,0},{7,1},{11,2},{15,3},{2,4},{6,5},{10,6},{14,7},{1,8},{5,9},{9... | collective-permute-start | bytes 393224 | tf_op jit(solution)/shard_map/ppermute | solution.py:187
  21.7 0.7 %collective-permute-start.7 = (f32[256,128]{1,0:T(8,128)S(1)}, f32[256,128]{1,0:T(8,128)S(1)}, u32[]{:S(2)}, u32[]{:S(2)}) collective-permute-start(f32[256,128]{1,0:T(8,128)S(1)} %broadcast_multiply_fusion), channel_id=1, source_target_pairs={{0,0},{4,1},{8,2},{12,3},{1,4},{5,5},{9,6},{13,7},{2,8},{6,9},{10,... | collective-permute-start | bytes 393224 | tf_op jit(solution)/shard_map/ppermute | solution.py:187
  22.4 0.4 collective-permute-done.6.refs_7_
  22.8 7.2 %collective-permute-start.8 = (f32[256,128]{1,0:T(8,128)S(1)}, f32[256,128]{1,0:T(8,128)S(1)}, u32[]{:S(2)}, u32[]{:S(2)}) collective-permute-start(f32[256,128]{1,0:T(8,128)S(1)} %broadcast_multiply_fusion), channel_id=1, source_target_pairs={{1,0},{5,1},{9,2},{13,3},{0,4},{4,5},{8,6},{12,7},{3,8},{7,9},{11,... | collective-permute-start | bytes 393224 | tf_op jit(solution)/shard_map/ppermute | solution.py:187
  30.0 2.9 %collective-permute-start.9 = (f32[256,128]{1,0:T(8,128)S(1)}, f32[256,128]{1,0:T(8,128)S(1)}, u32[]{:S(2)}, u32[]{:S(2)}) collective-permute-start(f32[256,128]{1,0:T(8,128)S(1)} %broadcast_multiply_fusion), channel_id=1, source_target_pairs={{2,0},{6,1},{10,2},{14,3},{3,4},{7,5},{11,6},{15,7},{0,8},{4,9},{8... | collective-permute-start | bytes 393224 | tf_op jit(solution)/shard_map/ppermute | solution.py:187
  32.9 2.1 %shard_map.120 = (f32[256,128]{1,0:T(8,128)}, f32[384,128]{1,0:T(8,128)S(1)}, f32[128,128]{1,0:T(8,128)S(1)}, bf16[4,256,256]{2,1,0:T(8,128)(2,1)S(1)}, bf16[4,256,256]{2,1,0:T(8,128)(2,1)S(1)}) custom-call(f32[320,256]{1,0:T(8,128)S(1)} %maximum_maximum_fusion.refs_0_, f32[320,256]{1,0:T(8,128)S(1)} %collective-permute-done.refs_1_, ...), custom_call_target="tpu_custom_call" | custom-call | bytes 3997696 | tf_op jit(solution)/shard_map/pallas_call | solution.py:143
  34.9 7.3 %all_gather.3.z_ref = f32[1536,128]{1,0:T(8,128)S(1)} all-gather(f32[384,128]{1,0:T(8,128)S(1)} %get-tuple-element.18.refs_8_), channel_id=1, replica_groups=mesh['pole'=2,'row'=4,'col'=4] {'col'}, dimensions={0}, use_global_device_ids=true | all-gather | bytes 983040 | tf_op jit(solution)/shard_map/all_gather | solution.py:232
  42.3 1.0 %shard_map.121 = (f32[256,128]{1,0:T(8,128)S(1)}, f32[128,128]{1,0:T(8,128)S(1)}) custom-call(f32[1536,128]{1,0:T(8,128)S(1)} %all_gather.3.z_ref, s32[4]{0:T(128)S(1)} %copy-done.3, f32[128,128]{1,0:T(8,128)S(1)} %copy-done), custom_call_target="tpu_custom_call" | custom-call | bytes 1048576 | tf_op jit(solution)/shard_map/pallas_call | solution.py:143
  43.3 1.4 %shard_map.122 = (f32[256,128]{1,0:T(8,128)}, f32[136,128]{1,0:T(8,128)S(1)}) custom-call(f32[256,128]{1,0:T(8,128)S(1)} %collective-permute-done.7.refs_0_, f32[256,128]{1,0:T(8,128)S(1)} %collective-permute-done.8.refs_1_, f32[256,128]{1,0:T(8,128)S(1)} %collective-permute-done.9.refs_2_, f32[256,128]{1,0:T(8,128)S(1)} %collective-permute-done.10.refs_3_, ...), custom_call_target="tpu_custom_call" | custom-call | bytes 2691072 | tf_op jit(solution)/shard_map/pallas_call | solution.py:143
  44.6 1.9 %collective-permute-start.11 = (f32[136,128]{1,0:T(8,128)S(1)}, f32[136,128]{1,0:T(8,128)S(1)}, u32[]{:S(2)}, u32[]{:S(2)}) collective-permute-start(f32[136,128]{1,0:T(8,128)S(1)} %get-tuple-element.21), channel_id=1, source_target_pairs={{0,4},{4,0},{8,12},{12,8},{1,5},{5,1},{9,13},{13,9},{2,6},{6,2},{1... | collective-permute-start | bytes 208904 | tf_op jit(solution)/shard_map/ppermute | solution.py:161
  46.5 2.7 %collective-permute-done.11 = f32[136,128]{1,0:T(8,128)S(1)} collective-permute-done((f32[136,128]{1,0:T(8,128)S(1)}, f32[136,128]{1,0:T(8,128)S(1)}, u32[]{:S(2)}, u32[]{:S(2)}) %collective-permute-start.11) | collective-permute-done | bytes 69664 | tf_op jit(solution)/shard_map/ppermute | solution.py:161
  49.3 3.6 %collective-permute-start.12 = (f32[136,128]{1,0:T(8,128)S(1)}, f32[136,128]{1,0:T(8,128)S(1)}, u32[]{:S(2)}, u32[]{:S(2)}) collective-permute-start(f32[136,128]{1,0:T(8,128)S(1)} %add.6), channel_id=1, source_target_pairs={{0,8},{4,12},{8,0},{12,4},{1,9},{5,13},{9,1},{13,5},{2,10},{6,14},... | collective-permute-start | bytes 208904 | tf_op jit(solution)/shard_map/ppermute | solution.py:161
  52.9 3.4 %collective-permute-done.12 = f32[136,128]{1,0:T(8,128)S(1)} collective-permute-done((f32[136,128]{1,0:T(8,128)S(1)}, f32[136,128]{1,0:T(8,128)S(1)}, u32[]{:S(2)}, u32[]{:S(2)}) %collective-permute-start.12) | collective-permute-done | bytes 69664 | tf_op jit(solution)/shard_map/ppermute | solution.py:161
  56.3 0.8 %shard_map.123 = (f32[128,128]{1,0:T(8,128)}, f32[128,128]{1,0:T(8,128)}) custom-call(f32[136,128]{1,0:T(8,128)S(1)} %add.7.m_ref, f32[128,128]{1,0:T(8,128)S(1)} %copy-done.1, f32[128,128]{1,0:T(8,128)S(1)} %get-tuple-element.22.e_ref), custom_call_target="tpu_custom_call" | custom-call | bytes 331776 | tf_op jit(solution)/shard_map/pallas_call | solution.py:143
  (33 shorter events, 0.3 us)
Async XLA Ops:
  1.4 4.0 %copy-start.6 = (s32[2,1]{0,1:T(1,128)S(1)}, s32[2,1]{0,1:T(1,128)}, u32[]{:S(2)}) copy-start(s32[2,1]{0,1:T(1,128)} %param.11) | copy-start | bytes 28
  1.4 4.1 %copy-start.4 = (f32[256,128]{1,0:T(8,128)S(1)}, f32[256,128]{1,0:T(8,128)}, u32[]{:S(2)}) copy-start(f32[256,128]{1,0:T(8,128)} %param.10) | copy-start | bytes 393220
  2.4 11.4 %collective-permute-start.1 = (f32[320,256]{1,0:T(8,128)S(1)}, f32[320,256]{1,0:T(8,128)S(1)}, u32[]{:S(2)}, u32[]{:S(2)}) collective-permute-start(f32[320,256]{1,0:T(8,128)S(1)} %maximum_maximum_fusion.refs_0_), channel_id=1, source_target_pairs={{0,2},{1,3},{2,0},{3,1},{4,6},{5,7},{6,4},{7,5},{8,10},{9,11},{10,... | collective-permute-start | bytes 983048 | tf_op jit(solution)/shard_map/ppermute | solution.py:161
  5.4 24.6 %collective-permute-start = (f32[320,256]{1,0:T(8,128)S(1)}, f32[320,256]{1,0:T(8,128)S(1)}, u32[]{:S(2)}, u32[]{:S(2)}) collective-permute-start(f32[320,256]{1,0:T(8,128)S(1)} %maximum_maximum_fusion.refs_0_), channel_id=1, source_target_pairs={{0,1},{1,0},{2,3},{3,2},{4,5},{5,4},{6,7},{7,6},{8,9},{9,8},{10,11... | collective-permute-start | bytes 983048 | tf_op jit(solution)/shard_map/ppermute | solution.py:161
  5.5 7.7 %copy-start.7 = (s32[2,1]{0,1:T(1,128)S(1)}, s32[2,1]{0,1:T(1,128)}, u32[]{:S(2)}) copy-start(s32[2,1]{0,1:T(1,128)} %param.14) | copy-start | bytes 28
  5.5 14.1 %copy-start.5 = (f32[256,128]{1,0:T(8,128)S(1)}, f32[256,128]{1,0:T(8,128)}, u32[]{:S(2)}) copy-start(f32[256,128]{1,0:T(8,128)} %param.13) | copy-start | bytes 393220
  5.6 9.5 %collective-permute-start.3 = (f32[256,128]{1,0:T(8,128)S(1)}, f32[256,128]{1,0:T(8,128)S(1)}, u32[]{:S(2)}, u32[]{:S(2)}) collective-permute-start(f32[256,128]{1,0:T(8,128)S(1)} %broadcast_multiply_fusion.1), channel_id=1, source_target_pairs={{0,0},{4,1},{8,2},{12,3},{1,4},{5,5},{9,6},{13,7},{2,8},{6,9},{10,... | collective-permute-start | bytes 393224 | tf_op jit(solution)/shard_map/ppermute | solution.py:187
  6.3 13.4 %collective-permute-start.4 = (f32[256,128]{1,0:T(8,128)S(1)}, f32[256,128]{1,0:T(8,128)S(1)}, u32[]{:S(2)}, u32[]{:S(2)}) collective-permute-start(f32[256,128]{1,0:T(8,128)S(1)} %broadcast_multiply_fusion.1), channel_id=1, source_target_pairs={{1,0},{5,1},{9,2},{13,3},{0,4},{4,5},{8,6},{12,7},{3,8},{7,9},{11,... | collective-permute-start | bytes 393224 | tf_op jit(solution)/shard_map/ppermute | solution.py:187
  9.7 12.0 %collective-permute-start.5 = (f32[256,128]{1,0:T(8,128)S(1)}, f32[256,128]{1,0:T(8,128)S(1)}, u32[]{:S(2)}, u32[]{:S(2)}) collective-permute-start(f32[256,128]{1,0:T(8,128)S(1)} %broadcast_multiply_fusion.1), channel_id=1, source_target_pairs={{2,0},{6,1},{10,2},{14,3},{3,4},{7,5},{11,6},{15,7},{0,8},{4,9},{8... | collective-permute-start | bytes 393224 | tf_op jit(solution)/shard_map/ppermute | solution.py:187
  13.8 19.0 %collective-permute-start.2 = (f32[320,256]{1,0:T(8,128)S(1)}, f32[320,256]{1,0:T(8,128)S(1)}, u32[]{:S(2)}, u32[]{:S(2)}) collective-permute-start(f32[320,256]{1,0:T(8,128)S(1)} %collective-permute-done.1.refs_2_), channel_id=1, source_target_pairs={{0,1},{1,0},{2,3},{3,2},{4,5},{5,4},{6,7},{7,6},{8,9},{9,8},{10,11... | collective-permute-start | bytes 983048 | tf_op jit(solution)/shard_map/ppermute | solution.py:161
  15.1 17.7 %copy-start = (f32[128,128]{1,0:T(8,128)S(1)}, f32[128,128]{1,0:T(8,128)}, u32[]{:S(2)}) copy-start(f32[128,128]{1,0:T(8,128)} %lower_ref.1) | copy-start | bytes 196612
  15.1 17.7 %copy-start.2 = (f32[128,128]{1,0:T(8,128)S(1)}, f32[128,128]{1,0:T(8,128)}, u32[]{:S(2)}) copy-start(f32[128,128]{1,0:T(8,128)} %refs_10_.1) | copy-start | bytes 196612
  15.1 17.7 %copy-start.3 = (s32[4]{0:T(128)S(1)}, s32[4]{0:T(128)}, u32[]{:S(2)}) copy-start(s32[4]{0:T(128)} %parent_ref.1) | copy-start | bytes 52
  15.1 7.7 %collective-permute-start.6 = (f32[256,128]{1,0:T(8,128)S(1)}, f32[256,128]{1,0:T(8,128)S(1)}, u32[]{:S(2)}, u32[]{:S(2)}) collective-permute-start(f32[256,128]{1,0:T(8,128)S(1)} %broadcast_multiply_fusion.1), channel_id=1, source_target_pairs={{3,0},{7,1},{11,2},{15,3},{2,4},{6,5},{10,6},{14,7},{1,8},{5,9},{9... | collective-permute-start | bytes 393224 | tf_op jit(solution)/shard_map/ppermute | solution.py:187
  19.8 23.5 %collective-permute-start.10 = (f32[256,128]{1,0:T(8,128)S(1)}, f32[256,128]{1,0:T(8,128)S(1)}, u32[]{:S(2)}, u32[]{:S(2)}) collective-permute-start(f32[256,128]{1,0:T(8,128)S(1)} %broadcast_multiply_fusion), channel_id=1, source_target_pairs={{3,0},{7,1},{11,2},{15,3},{2,4},{6,5},{10,6},{14,7},{1,8},{5,9},{9... | collective-permute-start | bytes 393224 | tf_op jit(solution)/shard_map/ppermute | solution.py:187
  21.7 21.5 %collective-permute-start.7 = (f32[256,128]{1,0:T(8,128)S(1)}, f32[256,128]{1,0:T(8,128)S(1)}, u32[]{:S(2)}, u32[]{:S(2)}) collective-permute-start(f32[256,128]{1,0:T(8,128)S(1)} %broadcast_multiply_fusion), channel_id=1, source_target_pairs={{0,0},{4,1},{8,2},{12,3},{1,4},{5,5},{9,6},{13,7},{2,8},{6,9},{10,... | collective-permute-start | bytes 393224 | tf_op jit(solution)/shard_map/ppermute | solution.py:187
  22.8 20.5 %collective-permute-start.8 = (f32[256,128]{1,0:T(8,128)S(1)}, f32[256,128]{1,0:T(8,128)S(1)}, u32[]{:S(2)}, u32[]{:S(2)}) collective-permute-start(f32[256,128]{1,0:T(8,128)S(1)} %broadcast_multiply_fusion), channel_id=1, source_target_pairs={{1,0},{5,1},{9,2},{13,3},{0,4},{4,5},{8,6},{12,7},{3,8},{7,9},{11,... | collective-permute-start | bytes 393224 | tf_op jit(solution)/shard_map/ppermute | solution.py:187
  30.0 13.3 %collective-permute-start.9 = (f32[256,128]{1,0:T(8,128)S(1)}, f32[256,128]{1,0:T(8,128)S(1)}, u32[]{:S(2)}, u32[]{:S(2)}) collective-permute-start(f32[256,128]{1,0:T(8,128)S(1)} %broadcast_multiply_fusion), channel_id=1, source_target_pairs={{2,0},{6,1},{10,2},{14,3},{3,4},{7,5},{11,6},{15,7},{0,8},{4,9},{8... | collective-permute-start | bytes 393224 | tf_op jit(solution)/shard_map/ppermute | solution.py:187
  44.6 4.6 %collective-permute-start.11 = (f32[136,128]{1,0:T(8,128)S(1)}, f32[136,128]{1,0:T(8,128)S(1)}, u32[]{:S(2)}, u32[]{:S(2)}) collective-permute-start(f32[136,128]{1,0:T(8,128)S(1)} %get-tuple-element.21), channel_id=1, source_target_pairs={{0,4},{4,0},{8,12},{12,8},{1,5},{5,1},{9,13},{13,9},{2,6},{6,2},{1... | collective-permute-start | bytes 208904 | tf_op jit(solution)/shard_map/ppermute | solution.py:161
  49.2 7.0 %copy-start.1 = (f32[128,128]{1,0:T(8,128)S(1)}, f32[128,128]{1,0:T(8,128)}, u32[]{:S(2)}) copy-start(f32[128,128]{1,0:T(8,128)} %dinv_ref.1) | copy-start | bytes 196612
  49.3 7.0 %collective-permute-start.12 = (f32[136,128]{1,0:T(8,128)S(1)}, f32[136,128]{1,0:T(8,128)S(1)}, u32[]{:S(2)}, u32[]{:S(2)}) collective-permute-start(f32[136,128]{1,0:T(8,128)S(1)} %add.6), channel_id=1, source_target_pairs={{0,8},{4,12},{8,0},{12,4},{1,9},{5,13},{9,1},{13,5},{2,10},{6,14},... | collective-permute-start | bytes 208904 | tf_op jit(solution)/shard_map/ppermute | solution.py:161

commit v3 on v2

--- a/solution.py
+++ b/solution.py
@@ -11,6 +11,8 @@
 SMEM = pl.BlockSpec(memory_space=pltpu.SMEM)
 NN = ((1,), (0,))
 TN = ((0,), (0,))
+BLOCK = 128
+PIECES = 2
 
 
 def split(x):
@@ -36,25 +38,70 @@
     return (r * q + c % q) ^ c, own, c
 
 
+def prepare_kernel(
+    root_ref, dinv_ref, first_ref, second_ref, one_ref, two_ref, panel_ref, both_ref, raw_ref, sems
+):
+    rows, depth = root_ref.shape
+    block = dinv_ref.shape[0]
+    fold = depth // block
+    part = block // fold
+    high, width = first_ref.shape
+    across = width // BLOCK
+    loads = [(first_ref, raw_ref.at[:high]), (second_ref, raw_ref.at[high:])]
+    loads.append((root_ref, panel_ref.at[:rows]))
+    for i in range(fold):
+        cols = pl.ds(i * block, block)
+        loads.append((dinv_ref.at[pl.ds(i * part, part)], panel_ref.at[pl.ds(rows, part), cols]))
+    copies = [pltpu.make_async_copy(src, dst, sems.at[i]) for i, (src, dst) in enumerate(loads)]
+    for copy in copies:
+        copy.start()
+    for level, pattern_ref in enumerate((one_ref, two_ref)):
+        copies[level].wait()
+        for i in range(high // BLOCK):
+            here = slice(level * high + i * BLOCK, level * high + (i + 1) * BLOCK)
+            for j in range(across):
+                cols = slice(j * BLOCK, (j + 1) * BLOCK)
+                factor = pattern_ref[i * across + j].astype(jnp.float32)
+                both_ref[here, cols] = raw_ref[here, cols] * factor
+    for copy in copies[2:]:
+        copy.wait()
+
+
+def pair_kernel(level, own_ref, other_ref, *refs):
+    out_ref = refs[-1]
+    depth = own_ref.shape[0] // 2
+    here = slice(level * depth, (level + 1) * depth)
+    out_ref[:depth] = own_ref[here]
+    out_ref[depth:] = other_ref[here]
+
+
 def first_kernel(nrow, ncol, *refs):
-    r_refs, f_refs = refs[:ncol], refs[ncol : 2 * ncol]
+    pairs = ncol // 2
+    count = pairs * (1 + PIECES)
+    r_refs, f_refs = refs[:count], refs[count : count + pairs]
     parent_ref, lower_ref, dinv_ref, x_ref, z_ref, e_ref, rh_ref, rl_ref, fh_ref, fl_ref, sel_ref = refs[
-        2 * ncol :
+        count + pairs :
     ]
     base, own, c = slots(nrow, ncol)
-    depth = f_refs[0].shape[0]
+    depth = f_refs[0].shape[0] // 2
     rows = x_ref.shape[0]
     block = dinv_ref.shape[0]
     fold = depth // block
     chosen = parent_ref[c] ^ c
     for t in range(ncol):
         slot = base ^ t
-        fh_ref[slot], fl_ref[slot] = split(f_refs[t][...])
+        part = f_refs[t // 2][t % 2 * depth : (t % 2 + 1) * depth]
+        fh_ref[slot], fl_ref[slot] = split(part)
     total = None
     for j in range(ncol):
-        parts = split(r_refs[j][:rows])
-        rh_ref[j], rl_ref[j] = parts
-        term = dot_split(parts, (fh_ref[j], fl_ref[j]), NN)
+        first = j // 2 * (1 + PIECES)
+        start = 0
+        for ref in r_refs[first + 1 : first + 1 + PIECES] if j % 2 else r_refs[first : first + 1]:
+            stop = min(start + ref.shape[0], rows)
+            if start < stop:
+                rh_ref[j, start:stop], rl_ref[j, start:stop] = split(ref[: stop - start])
+            start = stop
+        term = dot_split((rh_ref[j], rl_ref[j]), (fh_ref[j], fl_ref[j]), NN)
         total = term if total is None else total + term
     x = -total
     x_ref[...] = x
@@ -71,9 +118,9 @@
         @pl.when(chosen == j)
         def _(j=j):
             for i in range(fold):
-                sel_ref[i * (block // fold) : (i + 1) * (block // fold)] = r_refs[j][
-                    rows:, i * block : (i + 1) * block
-                ]
+                sel_ref[i * (block // fold) : (i + 1) * (block // fold)] = r_refs[
+                    j // 2 * (1 + PIECES) + j % 2 * PIECES
+                ][-(block // fold) :, i * block : (i + 1) * block]
 
     lower = split(lower_ref[...])
     product = dot_split(split(sel_ref[...]), lower, NN)
@@ -91,13 +138,15 @@
 
 
 def second_kernel(nrow, ncol, *refs):
-    s_refs = refs[:ncol]
-    rh_ref, rl_ref, c_ref, t_ref, z_ref, y_ref, m_ref, sh_ref, sl_ref = refs[ncol:]
+    pairs = ncol // 2
+    s_refs = refs[:pairs]
+    rh_ref, rl_ref, c_ref, t_ref, z_ref, y_ref, m_ref, sh_ref, sl_ref = refs[pairs:]
     base, own, _ = slots(nrow, ncol)
-    depth = s_refs[0].shape[0]
+    depth = s_refs[0].shape[0] // 2
     for t in range(ncol):
         slot = base ^ t
-        sh_ref[slot], sl_ref[slot] = split(s_refs[t][...])
+        part = s_refs[t // 2][t % 2 * depth : (t % 2 + 1) * depth]
+        sh_ref[slot], sl_ref[slot] = split(part)
     total = c_ref[...]
     for j in range(ncol):
         total += dot_split((rh_ref[j], rl_ref[j]), (sh_ref[j], sl_ref[j]), NN)
@@ -151,12 +200,6 @@
     )(*args)
 
 
-def masked(values, pattern):
-    rows, cols = pattern.shape
-    grid = values.reshape(rows, values.shape[0] // rows, cols, values.shape[1] // cols)
-    return (grid * pattern.astype(jnp.float32)[:, None, :, None]).reshape(values.shape)
-
-
 def swap(x, axis, size, bit):
     return lax.ppermute(x, axis, [(i, i ^ bit) for i in range(size)])
 
@@ -166,15 +209,23 @@
     bit = size // 2
     while bit:
         for j in sorted(blocks):
-            blocks[j ^ bit] = swap(blocks[j], axis, size, bit)
+            if bit > 1:
+                blocks[j ^ bit] = swap(blocks[j], axis, size, bit)
         bit //= 2
-    return [blocks[j] for j in range(size)]
+    parts = []
+    for j in range(0, size, 2):
+        parts.append(blocks[j])
+        count = blocks[j].shape[0] // PIECES
+        parts += [
+            swap(blocks[j][i * count : (i + 1) * count], axis, size, 1) for i in range(PIECES)
+        ]
+    return parts
 
 
 def turn(values, nrow, ncol, block):
     q = ncol // nrow
     out = []
-    for t in range(ncol):
+    for t in range(0, ncol, 2):
         pairs = []
         for r in range(nrow):
             for c in range(ncol):
@@ -204,14 +255,33 @@
     f32, bf16 = jnp.float32, jnp.bfloat16
     block = dinv_first.shape[0]
     rows, depth = inverse_root.shape
-    first = masked(lower_first, mask_first)
-    second = masked(lower_second, mask_second)
+    fold = depth // block
+    tall = (2 * lower_first.shape[0], lower_first.shape[1])
+    anywhere = pl.BlockSpec(memory_space=pl.ANY)
+    panel, both = pl.pallas_call(
+        prepare_kernel,
+        out_shape=[
+            jax.ShapeDtypeStruct((rows + block // fold, depth), f32),
+            jax.ShapeDtypeStruct(tall, f32),
+        ],
+        in_specs=[anywhere] * 4 + [SMEM] * 2,
+        out_specs=[VMEM] * 2,
+        scratch_shapes=[pltpu.VMEM(tall, f32), pltpu.SemaphoreType.DMA((3 + fold,))],
+    )(
+        inverse_root,
+        dinv_first,
+        lower_first,
+        lower_second,
+        mask_first.reshape(-1),
+        mask_second.reshape(-1),
+    )
+    other = swap(both, "col", ncol, 1)
+    first = call(functools.partial(pair_kernel, 0), [(both.shape, f32)], [], both, other)[0]
     f_parts = turn(first, nrow, ncol, block)
-    fold = depth // block
-    folded = jnp.concatenate(
-        [dinv_first[i * (block // fold) : (i + 1) * (block // fold)] for i in range(fold)], 1
-    )
-    r_parts = gather_xor(jnp.concatenate([inverse_root, folded], 0), "col", ncol)
+    r_parts = gather_xor(panel, "col", ncol)
+    second = call(
+        functools.partial(pair_kernel, 1), [(both.shape, f32)], [], both, other
+    )[0]
     s_parts = turn(second, nrow, ncol, block)
     halves = [((ncol, rows, depth), bf16)] * 2
     pieces = [((ncol, depth, block), bf16)] * 2

time: 57.3 us -> 51.9 us (0.906)
  starting transfers between devices: 34.5 us -> 16.4 us
  blocking collectives: 7.34 us -> 15.1 us
  waiting for transfers between devices: 7.12 us -> 10.5 us
  Pallas kernels: 5.14 us -> 7.81 us
  other arithmetic: 1.23 us -> 0.02 us
    ppermute x8 -> x4, starting transfers between devices: 24.8 us -> 6.84 us  [turn(): out.append(lax.ppermute(part, ('row', 'col'), pairs))]
    all_gather x1, blocking collectives: 7.34 us -> 15.1 us  [on_device(): lax.all_gather(z, 'col', axis=0, tiled=True)]
    ppermute x5 -> x8, waiting for transfers between devices: 6.69 us -> 10.5 us  [swap(): return lax.ppermute(x, axis, [(i, i ^ bit) for i in range(size)])]
    pallas_call x0 -> x1, Pallas kernels: none -> 2.63 us  [on_device(): pl.pallas_call(prepare_kernel, out_shape=[jax.ShapeDtypeStruct((rows + bl...]
    concatenate x1 -> x0, other arithmetic: 1.01 us -> none  [on_device(): jnp.concatenate([inverse_root, folded], 0)]
    ppermute x5 -> x8, starting transfers between devices: 9.74 us -> 9.52 us  [swap(): return lax.ppermute(x, axis, [(i, i ^ bit) for i in range(size)])]
    pallas_call x4 -> x6, Pallas kernels: 5.14 us -> 5.18 us  [call(): pl.pallas_call(kernel, out_shape=[jax.ShapeDtypeStruct(shape, dtype) for...]
  transfers between devices with their start and end apart: 13 -> 12, of which waited for: 4 -> 4; matrix products, arithmetic and copies ran while one was open for 1% -> 2% of each run, Pallas kernels for 5% -> 6%
where the time goes in v3:
time: 51.9 us; the launch traced here: 51.7 us
  starting transfers between devices  16.4 us (32%)
  blocking collectives  15.1 us (29%)
  waiting for transfers between devices  10.5 us (20%)
  Pallas kernels  7.81 us (15%)
  local copies, waits for them, and re-layouts  1.11 us (2%)
  between operations  0.83 us (2%)
    all_gather x1, blocking collectives, on_device(): lax.all_gather(z, 'col', axis=0, tiled=True)  15.1 us
    ppermute x8, waiting for transfers between devices, swap(): return lax.ppermute(x, axis, [(i, i ^ bit) for i in range(size)])  10.5 us
    ppermute x8, starting transfers between devices, swap(): return lax.ppermute(x, axis, [(i, i ^ bit) for i in range(size)])  9.52 us
    ppermute x4, starting transfers between devices, turn(): out.append(lax.ppermute(part, ('row', 'col'), pairs))  6.84 us
    pallas_call x6, Pallas kernels, call(): pl.pallas_call(kernel, out_shape=[jax.ShapeDtypeStruct(shape, dtype) for...  5.18 us
    pallas_call x1, Pallas kernels, on_device(): pl.pallas_call(prepare_kernel, out_shape=[jax.ShapeDtypeStruct((rows + bl...  2.63 us
    slice x2, local copies, waits for them, and re-layouts, gather_xor(): blocks[j][i * count:(i + 1) * count]  1.08 us
  transfers between devices with their start and end apart: 12, of which 4 were waited for; matrix products, arithmetic and copies ran while one was open for 2% of the time, Pallas kernels for 6%

profile of v3, /device:TPU:0, one launch (start us, length us, event | category | flops | bytes accessed | tf_op | source)
XLA Modules:
  0.0 51.7 jit_solution(6402545893587201196)
XLA Ops:
  0.6 2.6 %shard_map.120 = (f32[320,256]{1,0:T(8,128)}, f32[512,128]{1,0:T(8,128)}) custom-call(f32[256,256]{1,0:T(8,128)} %root_ref.1, f32[128,128]{1,0:T(8,128)} %dinv_ref.3, f32[256,128]{1,0:T(8,128)} %first_ref.1, f32[256,128]{1,0:T(8,128)} %second_ref.1, s32[2]{0:T(128)} %bitcast.2, s32[2]{0:T(128)} %bitcast.3), custom_call_target="tpu_custom_call" | custom-call | tf_op jit(solution)/shard_map/pallas_call | solution.py:261
  3.3 3.0 %collective-permute-start.2 = (f32[320,256]{1,0:T(8,128)}, f32[320,256]{1,0:T(8,128)S(1)}, u32[]{:S(2)}, u32[]{:S(2)}) collective-permute-start(f32[320,256]{1,0:T(8,128)} %get-tuple-element.17.refs_0_), channel_id=1, source_target_pairs={{0,2},{1,3},{2,0},{3,1},{4,6},{5,7},{6,4},{7,5},{8,10},{9,11},{10,... | collective-permute-start | bytes 983048 | tf_op jit(solution)/shard_map/ppermute | solution.py:204
  6.3 1.1 %fusion.1 = (f32[160,256]{1,0:T(8,128)S(1)}, f32[160,256]{1,0:T(8,128)S(1)}) fusion(f32[320,256]{1,0:T(8,128)} %get-tuple-element.17.refs_0_), kind=kLoop, calls=%fused_computation.1 | loop fusion | bytes 655360 | tf_op jit(solution)/shard_map/slice | solution.py:220
  7.3 0.5 %collective-permute-start.1 = (f32[160,256]{1,0:T(8,128)S(1)}, f32[160,256]{1,0:T(8,128)S(1)}, u32[]{:S(2)}, u32[]{:S(2)}) collective-permute-start(f32[160,256]{1,0:T(8,128)S(1)} %get-tuple-element.32), channel_id=1, source_target_pairs={{0,1},{1,0},{2,3},{3,2},{4,5},{5,4},{6,7},{7,6},{8,9},{9,8},{10,11... | collective-permute-start | bytes 491528 | tf_op jit(solution)/shard_map/ppermute | solution.py:204
  7.9 0.1 collective-permute-start
  8.0 0.1 collective-permute-done.5.other_ref
  8.0 2.6 %collective-permute-start.7 = (f32[512,128]{1,0:T(8,128)S(1)}, f32[512,128]{1,0:T(8,128)S(1)}, u32[]{:S(2)}, u32[]{:S(2)}) collective-permute-start(f32[512,128]{1,0:T(8,128)S(1)} %shard_map.121), channel_id=1, source_target_pairs={{2,0},{6,1},{10,2},{14,3},{3,4},{7,5},{11,6},{15,7},{0,8},{4,9},{8... | collective-permute-start | bytes 786440 | tf_op jit(solution)/shard_map/ppermute | solution.py:238
  10.7 0.7 %collective-permute-start.6 = (f32[512,128]{1,0:T(8,128)S(1)}, f32[512,128]{1,0:T(8,128)S(1)}, u32[]{:S(2)}, u32[]{:S(2)}) collective-permute-start(f32[512,128]{1,0:T(8,128)S(1)} %shard_map.121), channel_id=1, source_target_pairs={{0,0},{4,1},{8,2},{12,3},{1,4},{5,5},{9,6},{13,7},{2,8},{6,9},{10,... | collective-permute-start | bytes 786440 | tf_op jit(solution)/shard_map/ppermute | solution.py:238
  11.4 4.8 %collective-permute-done.2.refs_3_ = f32[320,256]{1,0:T(8,128)S(1)} collective-permute-done((f32[320,256]{1,0:T(8,128)}, f32[320,256]{1,0:T(8,128)S(1)}, u32[]{:S(2)}, u32[]{:S(2)}) %collective-permute-start.2) | collective-permute-done | bytes 327712 | tf_op jit(solution)/shard_map/ppermute | solution.py:204
  16.2 0.1 collective-permute-start.4
  16.3 0.0 copy-start.2
  16.3 0.0 copy-start.4
  16.3 0.5 %collective-permute-start.3 = (f32[160,256]{1,0:T(8,128)S(1)}, f32[160,256]{1,0:T(8,128)S(1)}, u32[]{:S(2)}, u32[]{:S(2)}) collective-permute-start(f32[160,256]{1,0:T(8,128)S(1)} %get-tuple-element.31), channel_id=1, source_target_pairs={{0,1},{1,0},{2,3},{3,2},{4,5},{5,4},{6,7},{7,6},{8,9},{9,8},{10,11... | collective-permute-start | bytes 491528 | tf_op jit(solution)/shard_map/ppermute | solution.py:204
  16.9 2.9 %collective-permute-start.9 = (f32[512,128]{1,0:T(8,128)S(1)}, f32[512,128]{1,0:T(8,128)S(1)}, u32[]{:S(2)}, u32[]{:S(2)}) collective-permute-start(f32[512,128]{1,0:T(8,128)S(1)} %shard_map.123), channel_id=1, source_target_pairs={{2,0},{6,1},{10,2},{14,3},{3,4},{7,5},{11,6},{15,7},{0,8},{4,9},{8... | collective-permute-start | bytes 786440 | tf_op jit(solution)/shard_map/ppermute | solution.py:238
  19.7 0.7 %collective-permute-start.8 = (f32[512,128]{1,0:T(8,128)S(1)}, f32[512,128]{1,0:T(8,128)S(1)}, u32[]{:S(2)}, u32[]{:S(2)}) collective-permute-start(f32[512,128]{1,0:T(8,128)S(1)} %shard_map.123), channel_id=1, source_target_pairs={{0,0},{4,1},{8,2},{12,3},{1,4},{5,5},{9,6},{13,7},{2,8},{6,9},{10,... | collective-permute-start | bytes 786440 | tf_op jit(solution)/shard_map/ppermute | solution.py:238
  20.5 2.1 %shard_map.122 = (f32[256,128]{1,0:T(8,128)}, f32[384,128]{1,0:T(8,128)S(1)}, f32[128,128]{1,0:T(8,128)S(1)}, bf16[4,256,256]{2,1,0:T(8,128)(2,1)S(1)}, bf16[4,256,256]{2,1,0:T(8,128)(2,1)S(1)}) custom-call(f32[320,256]{1,0:T(8,128)S(1)} %copy-done, f32[160,256]{1,0:T(8,128)S(1)} %collective-permute-done.refs_1_, ...), custom_call_target="tpu_custom_call" | custom-call | bytes 3997696 | tf_op jit(solution)/shard_map/pallas_call | solution.py:192
  22.6 15.1 %all_gather.3.z_ref = f32[1536,128]{1,0:T(8,128)S(1)} all-gather(f32[384,128]{1,0:T(8,128)S(1)} %get-tuple-element.22.refs_6_), channel_id=1, replica_groups=mesh['pole'=2,'row'=4,'col'=4] {'col'}, dimensions={0}, use_global_device_ids=true | all-gather | bytes 983040 | tf_op jit(solution)/shard_map/all_gather | solution.py:302
  37.7 1.0 %shard_map.124 = (f32[256,128]{1,0:T(8,128)S(1)}, f32[128,128]{1,0:T(8,128)S(1)}) custom-call(f32[1536,128]{1,0:T(8,128)S(1)} %all_gather.3.z_ref, s32[4]{0:T(128)S(1)} %copy-done.5, f32[128,128]{1,0:T(8,128)S(1)} %copy-done.2), custom_call_target="tpu_custom_call" | custom-call | bytes 1048576 | tf_op jit(solution)/shard_map/pallas_call | solution.py:192
  38.7 1.4 %shard_map.125 = (f32[256,128]{1,0:T(8,128)}, f32[136,128]{1,0:T(8,128)S(1)}) custom-call(f32[512,128]{1,0:T(8,128)S(1)} %collective-permute-done.8.refs_0_, f32[512,128]{1,0:T(8,128)S(1)} %collective-permute-done.9.refs_1_, bf16[4,256,256]{2,1,0:T(8,128)(2,1)S(1)} %get-tuple-element.20.refs_2_, bf16[4,256,256]{2,1,0:T(8,128)(2,1)S(1)} %get-tuple-element.21.refs_3_, ...), custom_call_target="tpu_custom_call" | custom-call | bytes 2691072 | tf_op jit(solution)/shard_map/pallas_call | solution.py:192
  40.0 2.4 %collective-permute-start.10 = (f32[136,128]{1,0:T(8,128)S(1)}, f32[136,128]{1,0:T(8,128)S(1)}, u32[]{:S(2)}, u32[]{:S(2)}) collective-permute-start(f32[136,128]{1,0:T(8,128)S(1)} %get-tuple-element.25), channel_id=1, source_target_pairs={{0,4},{4,0},{8,12},{12,8},{1,5},{5,1},{9,13},{13,9},{2,6},{6,2},{1... | collective-permute-start | bytes 208904 | tf_op jit(solution)/shard_map/ppermute | solution.py:204
  42.5 2.7 %collective-permute-done.10 = f32[136,128]{1,0:T(8,128)S(1)} collective-permute-done((f32[136,128]{1,0:T(8,128)S(1)}, f32[136,128]{1,0:T(8,128)S(1)}, u32[]{:S(2)}, u32[]{:S(2)}) %collective-permute-start.10) | collective-permute-done | bytes 69664 | tf_op jit(solution)/shard_map/ppermute | solution.py:204
  45.2 2.9 %collective-permute-start.11 = (f32[136,128]{1,0:T(8,128)S(1)}, f32[136,128]{1,0:T(8,128)S(1)}, u32[]{:S(2)}, u32[]{:S(2)}) collective-permute-start(f32[136,128]{1,0:T(8,128)S(1)} %add.6), channel_id=1, source_target_pairs={{0,8},{4,12},{8,0},{12,4},{1,9},{5,13},{9,1},{13,5},{2,10},{6,14},... | collective-permute-start | bytes 208904 | tf_op jit(solution)/shard_map/ppermute | solution.py:204
  48.1 2.9 %collective-permute-done.11 = f32[136,128]{1,0:T(8,128)S(1)} collective-permute-done((f32[136,128]{1,0:T(8,128)S(1)}, f32[136,128]{1,0:T(8,128)S(1)}, u32[]{:S(2)}, u32[]{:S(2)}) %collective-permute-start.11) | collective-permute-done | bytes 69664 | tf_op jit(solution)/shard_map/ppermute | solution.py:204
  51.0 0.8 %shard_map.126 = (f32[128,128]{1,0:T(8,128)}, f32[128,128]{1,0:T(8,128)}) custom-call(f32[136,128]{1,0:T(8,128)S(1)} %add.7.m_ref, f32[128,128]{1,0:T(8,128)S(1)} %copy-done.3, f32[128,128]{1,0:T(8,128)S(1)} %get-tuple-element.26.e_ref), custom_call_target="tpu_custom_call" | custom-call | bytes 331776 | tf_op jit(solution)/shard_map/pallas_call | solution.py:192
  (24 shorter events, 0.1 us)
Async XLA Ops:
  3.3 12.9 %collective-permute-start.2 = (f32[320,256]{1,0:T(8,128)}, f32[320,256]{1,0:T(8,128)S(1)}, u32[]{:S(2)}, u32[]{:S(2)}) collective-permute-start(f32[320,256]{1,0:T(8,128)} %get-tuple-element.17.refs_0_), channel_id=1, source_target_pairs={{0,2},{1,3},{2,0},{3,1},{4,6},{5,7},{6,4},{7,5},{8,10},{9,11},{10,... | collective-permute-start | bytes 983048 | tf_op jit(solution)/shard_map/ppermute | solution.py:204
  6.3 1.8 %copy-start.1 = (f32[512,128]{1,0:T(8,128)S(1)}, f32[512,128]{1,0:T(8,128)}, u32[]{:S(2)}) copy-start(f32[512,128]{1,0:T(8,128)} %get-tuple-element.18.own_ref) | copy-start | bytes 786436
  6.3 1.7 %collective-permute-start.5 = (f32[512,128]{1,0:T(8,128)}, f32[512,128]{1,0:T(8,128)S(1)}, u32[]{:S(2)}, u32[]{:S(2)}) collective-permute-start(f32[512,128]{1,0:T(8,128)} %get-tuple-element.18.own_ref), channel_id=1, source_target_pairs={{0,1},{1,0},{2,3},{3,2},{4,5},{5,4},{6,7},{7,6},{8,9},{9,8},{10,11... | collective-permute-start | bytes 786440 | tf_op jit(solution)/shard_map/ppermute | solution.py:204
  7.3 8.9 %collective-permute-start.1 = (f32[160,256]{1,0:T(8,128)S(1)}, f32[160,256]{1,0:T(8,128)S(1)}, u32[]{:S(2)}, u32[]{:S(2)}) collective-permute-start(f32[160,256]{1,0:T(8,128)S(1)} %get-tuple-element.32), channel_id=1, source_target_pairs={{0,1},{1,0},{2,3},{3,2},{4,5},{5,4},{6,7},{7,6},{8,9},{9,8},{10,11... | collective-permute-start | bytes 491528 | tf_op jit(solution)/shard_map/ppermute | solution.py:204
  7.9 9.0 %collective-permute-start = (f32[160,256]{1,0:T(8,128)S(1)}, f32[160,256]{1,0:T(8,128)S(1)}, u32[]{:S(2)}, u32[]{:S(2)}) collective-permute-start(f32[160,256]{1,0:T(8,128)S(1)} %get-tuple-element.33), channel_id=1, source_target_pairs={{0,1},{1,0},{2,3},{3,2},{4,5},{5,4},{6,7},{7,6},{8,9},{9,8},{10,11... | collective-permute-start | bytes 491528 | tf_op jit(solution)/shard_map/ppermute | solution.py:204
  8.0 12.4 %collective-permute-start.7 = (f32[512,128]{1,0:T(8,128)S(1)}, f32[512,128]{1,0:T(8,128)S(1)}, u32[]{:S(2)}, u32[]{:S(2)}) collective-permute-start(f32[512,128]{1,0:T(8,128)S(1)} %shard_map.121), channel_id=1, source_target_pairs={{2,0},{6,1},{10,2},{14,3},{3,4},{7,5},{11,6},{15,7},{0,8},{4,9},{8... | collective-permute-start | bytes 786440 | tf_op jit(solution)/shard_map/ppermute | solution.py:238
  10.7 9.7 %collective-permute-start.6 = (f32[512,128]{1,0:T(8,128)S(1)}, f32[512,128]{1,0:T(8,128)S(1)}, u32[]{:S(2)}, u32[]{:S(2)}) collective-permute-start(f32[512,128]{1,0:T(8,128)S(1)} %shard_map.121), channel_id=1, source_target_pairs={{0,0},{4,1},{8,2},{12,3},{1,4},{5,5},{9,6},{13,7},{2,8},{6,9},{10,... | collective-permute-start | bytes 786440 | tf_op jit(solution)/shard_map/ppermute | solution.py:238
  16.2 3.6 %collective-permute-start.4 = (f32[160,256]{1,0:T(8,128)S(1)}, f32[160,256]{1,0:T(8,128)S(1)}, u32[]{:S(2)}, u32[]{:S(2)}) collective-permute-start(f32[160,256]{1,0:T(8,128)S(1)} %get-tuple-element.30), channel_id=1, source_target_pairs={{0,1},{1,0},{2,3},{3,2},{4,5},{5,4},{6,7},{7,6},{8,9},{9,8},{10,11... | collective-permute-start | bytes 491528 | tf_op jit(solution)/shard_map/ppermute | solution.py:204
  16.3 4.2 %copy-start = (f32[320,256]{1,0:T(8,128)S(1)}, f32[320,256]{1,0:T(8,128)}, u32[]{:S(2)}) copy-start(f32[320,256]{1,0:T(8,128)} %get-tuple-element.17.refs_0_) | copy-start | bytes 983044
  16.3 4.2 %copy-start.2 = (f32[128,128]{1,0:T(8,128)S(1)}, f32[128,128]{1,0:T(8,128)}, u32[]{:S(2)}) copy-start(f32[128,128]{1,0:T(8,128)} %lower_ref.1) | copy-start | bytes 196612
  16.3 4.2 %copy-start.4 = (f32[128,128]{1,0:T(8,128)S(1)}, f32[128,128]{1,0:T(8,128)}, u32[]{:S(2)}) copy-start(f32[128,128]{1,0:T(8,128)} %refs_10_.1) | copy-start | bytes 196612
  16.3 4.2 %copy-start.5 = (s32[4]{0:T(128)S(1)}, s32[4]{0:T(128)}, u32[]{:S(2)}) copy-start(s32[4]{0:T(128)} %parent_ref.1) | copy-start | bytes 52
  16.3 4.1 %collective-permute-start.3 = (f32[160,256]{1,0:T(8,128)S(1)}, f32[160,256]{1,0:T(8,128)S(1)}, u32[]{:S(2)}, u32[]{:S(2)}) collective-permute-start(f32[160,256]{1,0:T(8,128)S(1)} %get-tuple-element.31), channel_id=1, source_target_pairs={{0,1},{1,0},{2,3},{3,2},{4,5},{5,4},{6,7},{7,6},{8,9},{9,8},{10,11... | collective-permute-start | bytes 491528 | tf_op jit(solution)/shard_map/ppermute | solution.py:204
  16.9 21.8 %collective-permute-start.9 = (f32[512,128]{1,0:T(8,128)S(1)}, f32[512,128]{1,0:T(8,128)S(1)}, u32[]{:S(2)}, u32[]{:S(2)}) collective-permute-start(f32[512,128]{1,0:T(8,128)S(1)} %shard_map.123), channel_id=1, source_target_pairs={{2,0},{6,1},{10,2},{14,3},{3,4},{7,5},{11,6},{15,7},{0,8},{4,9},{8... | collective-permute-start | bytes 786440 | tf_op jit(solution)/shard_map/ppermute | solution.py:238
  19.7 18.9 %collective-permute-start.8 = (f32[512,128]{1,0:T(8,128)S(1)}, f32[512,128]{1,0:T(8,128)S(1)}, u32[]{:S(2)}, u32[]{:S(2)}) collective-permute-start(f32[512,128]{1,0:T(8,128)S(1)} %shard_map.123), channel_id=1, source_target_pairs={{0,0},{4,1},{8,2},{12,3},{1,4},{5,5},{9,6},{13,7},{2,8},{6,9},{10,... | collective-permute-start | bytes 786440 | tf_op jit(solution)/shard_map/ppermute | solution.py:238
  40.0 5.1 %collective-permute-start.10 = (f32[136,128]{1,0:T(8,128)S(1)}, f32[136,128]{1,0:T(8,128)S(1)}, u32[]{:S(2)}, u32[]{:S(2)}) collective-permute-start(f32[136,128]{1,0:T(8,128)S(1)} %get-tuple-element.25), channel_id=1, source_target_pairs={{0,4},{4,0},{8,12},{12,8},{1,5},{5,1},{9,13},{13,9},{2,6},{6,2},{1... | collective-permute-start | bytes 208904 | tf_op jit(solution)/shard_map/ppermute | solution.py:204
  45.2 5.8 %copy-start.3 = (f32[128,128]{1,0:T(8,128)S(1)}, f32[128,128]{1,0:T(8,128)}, u32[]{:S(2)}) copy-start(f32[128,128]{1,0:T(8,128)} %dinv_ref.3) | copy-start | bytes 196612
  45.2 5.8 %collective-permute-start.11 = (f32[136,128]{1,0:T(8,128)S(1)}, f32[136,128]{1,0:T(8,128)S(1)}, u32[]{:S(2)}, u32[]{:S(2)}) collective-permute-start(f32[136,128]{1,0:T(8,128)S(1)} %add.6), channel_id=1, source_target_pairs={{0,8},{4,12},{8,0},{12,4},{1,9},{5,13},{9,1},{13,5},{2,10},{6,14},... | collective-permute-start | bytes 208904 | tf_op jit(solution)/shard_map/ppermute | solution.py:204

commit v4 on v3

--- a/solution.py
+++ b/solution.py
@@ -75,36 +75,57 @@
     out_ref[depth:] = other_ref[here]
 
 
-def first_kernel(nrow, ncol, *refs):
-    pairs = ncol // 2
-    count = pairs * (1 + PIECES)
-    r_refs, f_refs = refs[:count], refs[count : count + pairs]
-    parent_ref, lower_ref, dinv_ref, x_ref, z_ref, e_ref, rh_ref, rl_ref, fh_ref, fl_ref, sel_ref = refs[
-        count + pairs :
-    ]
-    base, own, c = slots(nrow, ncol)
-    depth = f_refs[0].shape[0] // 2
-    rows = x_ref.shape[0]
+def panel_kernel(nrow, ncol, *refs):
+    count = ncol // 2 * (1 + PIECES)
+    r_refs = refs[:count]
+    parent_ref, lower_ref, dinv_ref, e_ref, rh_ref, rl_ref, sel_ref = refs[count:]
+    _, rows, depth = rh_ref.shape
     block = dinv_ref.shape[0]
     fold = depth // block
+    part = block // fold
+    c = lax.axis_index("col")
     chosen = parent_ref[c] ^ c
-    for t in range(ncol):
-        slot = base ^ t
-        part = f_refs[t // 2][t % 2 * depth : (t % 2 + 1) * depth]
-        fh_ref[slot], fl_ref[slot] = split(part)
-    total = None
     for j in range(ncol):
         first = j // 2 * (1 + PIECES)
+        here = r_refs[first + 1 : first + 1 + PIECES] if j % 2 else r_refs[first : first + 1]
         start = 0
-        for ref in r_refs[first + 1 : first + 1 + PIECES] if j % 2 else r_refs[first : first + 1]:
+        for ref in here:
             stop = min(start + ref.shape[0], rows)
             if start < stop:
                 rh_ref[j, start:stop], rl_ref[j, start:stop] = split(ref[: stop - start])
             start = stop
+
+        @pl.when(chosen == j)
+        def _(last=here[-1]):
+            for i in range(fold):
+                sel_ref[i * part : (i + 1) * part] = last[-part:, i * block : (i + 1) * block]
+
+    lower = split(lower_ref[...])
+    product = dot_split(split(sel_ref[...]), lower, NN)
+    e_ref[...] = dinv_ref[...] + dot_split(lower, split(product), TN)
+
+
+def spread(nrow, ncol, refs, high_ref, low_ref):
+    base, own, _ = slots(nrow, ncol)
+    depth = refs[0].shape[0] // 2
+    for t in range(ncol):
+        slot = base ^ t
+        part = refs[-1 - t // 2][t % 2 * depth : (t % 2 + 1) * depth]
+        high_ref[slot], low_ref[slot] = split(part)
+    return own, depth
+
+
+def first_kernel(nrow, ncol, *refs):
+    f_refs = refs[: ncol // 2]
+    rh_ref, rl_ref, x_ref, z_ref, fh_ref, fl_ref = refs[ncol // 2 :]
+    own, depth = spread(nrow, ncol, f_refs, fh_ref, fl_ref)
+    total = None
+    for j in range(ncol):
         term = dot_split((rh_ref[j], rl_ref[j]), (fh_ref[j], fl_ref[j]), NN)
         total = term if total is None else total + term
     x = -total
     x_ref[...] = x
+    rows = x.shape[0]
     z_ref[:rows] = x
     diag = None
     for i, slot in enumerate(own):
@@ -113,53 +134,31 @@
         )
         diag = term if diag is None else diag + term
     z_ref[rows:] = diag
-    for j in range(ncol):
-
-        @pl.when(chosen == j)
-        def _(j=j):
-            for i in range(fold):
-                sel_ref[i * (block // fold) : (i + 1) * (block // fold)] = r_refs[
-                    j // 2 * (1 + PIECES) + j % 2 * PIECES
-                ][-(block // fold) :, i * block : (i + 1) * block]
-
-    lower = split(lower_ref[...])
-    product = dot_split(split(sel_ref[...]), lower, NN)
-    e_ref[...] = dinv_ref[...] + dot_split(lower, split(product), TN)
-
-
-def parent_kernel(z_ref, parent_ref, lower_ref, c_ref, t_ref):
-    rows, block = c_ref.shape
+
+
+def second_kernel(nrow, ncol, *refs):
+    s_refs = refs[: ncol // 2]
+    rh_ref, rl_ref, all_ref, parent_ref, lower_ref, z_ref, y_ref, m_ref, sh_ref, sl_ref = refs[
+        ncol // 2 :
+    ]
+    own, depth = spread(nrow, ncol, s_refs, sh_ref, sl_ref)
+    rows = y_ref.shape[0]
+    block = lower_ref.shape[0]
     height = rows + block
     first = pl.multiple_of(parent_ref[lax.axis_index("col")] * height, block)
     lower = split(lower_ref[...])
-    product = dot_split(split(z_ref[pl.ds(first, height)]), lower, NN)
-    c_ref[...] = product[:rows]
-    t_ref[...] = dot_split(lower, split(product[rows:]), TN)
-
-
-def second_kernel(nrow, ncol, *refs):
-    pairs = ncol // 2
-    s_refs = refs[:pairs]
-    rh_ref, rl_ref, c_ref, t_ref, z_ref, y_ref, m_ref, sh_ref, sl_ref = refs[pairs:]
-    base, own, _ = slots(nrow, ncol)
-    depth = s_refs[0].shape[0] // 2
-    for t in range(ncol):
-        slot = base ^ t
-        part = s_refs[t // 2][t % 2 * depth : (t % 2 + 1) * depth]
-        sh_ref[slot], sl_ref[slot] = split(part)
-    total = c_ref[...]
+    product = dot_split(split(all_ref[pl.ds(first, height)]), lower, NN)
+    coupling = product[:rows]
+    diag = dot_split(lower, split(product[rows:]), TN)
+    total = coupling
     for j in range(ncol):
         total += dot_split((rh_ref[j], rl_ref[j]), (sh_ref[j], sl_ref[j]), NN)
     y_ref[...] = -total
-    coupling = c_ref[...]
-    diag = t_ref[...]
     for i, slot in enumerate(own):
         mine = (sh_ref[slot], sl_ref[slot])
         here = slice(i * depth, (i + 1) * depth)
         diag += dot_split(mine, split(total[here]), TN)
         diag += dot_split(split(coupling[here]), mine, TN)
-    rows = c_ref.shape[0]
-    block = diag.shape[0]
     across = lax.broadcasted_iota(jnp.int32, diag.shape, 1)
     down = lax.broadcasted_iota(jnp.int32, diag.shape, 0)
     m_ref[:block] = jnp.where(down <= across, z_ref[rows : rows + block], diag)
@@ -167,14 +166,18 @@
     m_ref[block:] = jnp.broadcast_to(line, (m_ref.shape[0] - block, line.shape[1]))
 
 
-def last_kernel(m_ref, dinv_ref, e_ref, one_ref, two_ref):
+def last_kernel(dinv_ref, e_ref, *refs):
+    one_ref, two_ref = refs[-2:]
     block = dinv_ref.shape[0]
-    m = m_ref[:block]
+    total = refs[0][...]
+    for ref in refs[1:-2]:
+        total += ref[...]
+    m = total[:block]
     across = lax.broadcasted_iota(jnp.int32, m.shape, 1)
     down = lax.broadcasted_iota(jnp.int32, m.shape, 0)
     turned = m.T
     one_ref[...] = dinv_ref[...] + jnp.where(down <= across, m, turned)
-    line = jnp.broadcast_to(m_ref[block : block + 1], m.shape)
+    line = jnp.broadcast_to(total[block : block + 1], m.shape)
     two_ref[...] = e_ref[...] + jnp.where(
         down == across, line, jnp.where(down > across, m, turned)
     )
@@ -285,41 +288,43 @@
     s_parts = turn(second, nrow, ncol, block)
     halves = [((ncol, rows, depth), bf16)] * 2
     pieces = [((ncol, depth, block), bf16)] * 2
-    inverse_first, z, start, r_high, r_low = call(
-        functools.partial(first_kernel, nrow, ncol),
-        [((rows, block), f32), ((rows + block, block), f32), ((block, block), f32)] + halves,
-        pieces + [((block, block), f32)],
+    start, r_high, r_low = call(
+        functools.partial(panel_kernel, nrow, ncol),
+        [((block, block), f32)] + halves,
+        [((block, block), f32)],
         *r_parts,
-        *f_parts,
         parent,
         lower_parent,
         dinv_second,
     )
-    coupling, parent_diag = call(
-        parent_kernel,
-        [((rows, block), f32), ((block, block), f32)],
-        [],
-        lax.all_gather(z, "col", axis=0, tiled=True),
-        parent,
-        lower_parent,
+    inverse_first, z = call(
+        functools.partial(first_kernel, nrow, ncol),
+        [((rows, block), f32), ((rows + block, block), f32)],
+        pieces,
+        *f_parts[::-1],
+        r_high,
+        r_low,
     )
     inverse_second, packed = call(
         functools.partial(second_kernel, nrow, ncol),
         [((rows, block), f32), ((block + 8, block), f32)],
         pieces,
-        *s_parts,
+        *s_parts[::-1],
         r_high,
         r_low,
-        coupling,
-        parent_diag,
+        lax.all_gather(z, "col", axis=0, tiled=True),
+        parent,
+        lower_parent,
         z,
     )
-    bit = 1
-    while bit < nrow:
-        packed = packed + swap(packed, "row", nrow, bit)
-        bit *= 2
     diag_first, diag_second = call(
-        last_kernel, [((block, block), f32)] * 2, [], packed, dinv_first, start
+        last_kernel,
+        [((block, block), f32)] * 2,
+        [],
+        dinv_first,
+        start,
+        packed,
+        *[swap(packed, "row", nrow, j) for j in range(nrow - 1, 0, -1)],
     )
     return (inverse_first, diag_first, inverse_second, diag_second)
 

time: 51.9 us -> 51.4 us (level)
    ppermute x8 -> x9, waiting for transfers between devices: 10.5 us -> 10.1 us  [swap(): return lax.ppermute(x, axis, [(i, i ^ bit) for i in range(size)])]
    ppermute x8 -> x9, starting transfers between devices: 9.52 us -> 9.27 us  [swap(): return lax.ppermute(x, axis, [(i, i ^ bit) for i in range(size)])]
  transfers between devices with their start and end apart: 12 -> 13, of which waited for: 4 -> 4; matrix products, arithmetic and copies ran while one was open for 2% -> 2% of each run, Pallas kernels for 6% -> 5%
where the time goes in v4:
time: 51.4 us; the launch traced here: 51.2 us
  starting transfers between devices  16.1 us (31%)
  blocking collectives  15 us (29%)
  waiting for transfers between devices  10.1 us (20%)
  Pallas kernels  8.01 us (16%)
  local copies, waits for them, and re-layouts  1.11 us (2%)
  between operations  0.8 us (2%)
    all_gather x1, blocking collectives, on_device(): lax.all_gather(z, 'col', axis=0, tiled=True)  15 us
    ppermute x9, waiting for transfers between devices, swap(): return lax.ppermute(x, axis, [(i, i ^ bit) for i in range(size)])  10.1 us
    ppermute x9, starting transfers between devices, swap(): return lax.ppermute(x, axis, [(i, i ^ bit) for i in range(size)])  9.27 us
    ppermute x4, starting transfers between devices, turn(): out.append(lax.ppermute(part, ('row', 'col'), pairs))  6.84 us
    pallas_call x6, Pallas kernels, call(): pl.pallas_call(kernel, out_shape=[jax.ShapeDtypeStruct(shape, dtype) for...  5.37 us
    pallas_call x1, Pallas kernels, on_device(): pl.pallas_call(prepare_kernel, out_shape=[jax.ShapeDtypeStruct((rows + bl...  2.64 us
    slice x2, local copies, waits for them, and re-layouts, gather_xor(): blocks[j][i * count:(i + 1) * count]  1.08 us
  transfers between devices with their start and end apart: 13, of which 4 were waited for; matrix products, arithmetic and copies ran while one was open for 2% of the time, Pallas kernels for 5%

profile of v4, /device:TPU:0, one launch (start us, length us, event | category | flops | bytes accessed | tf_op | source)
XLA Modules:
  0.0 51.2 jit_solution(16296094009373221663)
XLA Ops:
  0.6 2.6 %shard_map.120 = (f32[320,256]{1,0:T(8,128)}, f32[512,128]{1,0:T(8,128)}) custom-call(f32[256,256]{1,0:T(8,128)} %root_ref.1, f32[128,128]{1,0:T(8,128)} %dinv_ref.3, f32[256,128]{1,0:T(8,128)} %first_ref.1, f32[256,128]{1,0:T(8,128)} %second_ref.1, s32[2]{0:T(128)} %bitcast.2, s32[2]{0:T(128)} %bitcast.3), custom_call_target="tpu_custom_call" | custom-call | tf_op jit(solution)/shard_map/pallas_call | solution.py:264
  3.3 3.0 %collective-permute-start.5 = (f32[320,256]{1,0:T(8,128)}, f32[320,256]{1,0:T(8,128)S(1)}, u32[]{:S(2)}, u32[]{:S(2)}) collective-permute-start(f32[320,256]{1,0:T(8,128)} %get-tuple-element.16.refs_0_), channel_id=1, source_target_pairs={{0,2},{1,3},{2,0},{3,1},{4,6},{5,7},{6,4},{7,5},{8,10},{9,11},{10,... | collective-permute-start | bytes 983048 | tf_op jit(solution)/shard_map/ppermute | solution.py:207
  6.3 1.1 %fusion.1 = (f32[160,256]{1,0:T(8,128)S(1)}, f32[160,256]{1,0:T(8,128)S(1)}) fusion(f32[320,256]{1,0:T(8,128)} %get-tuple-element.16.refs_0_), kind=kLoop, calls=%fused_computation.1 | loop fusion | bytes 655360 | tf_op jit(solution)/shard_map/slice | solution.py:223
  7.4 0.5 %collective-permute-start.3 = (f32[160,256]{1,0:T(8,128)S(1)}, f32[160,256]{1,0:T(8,128)S(1)}, u32[]{:S(2)}, u32[]{:S(2)}) collective-permute-start(f32[160,256]{1,0:T(8,128)S(1)} %get-tuple-element.29), channel_id=1, source_target_pairs={{0,1},{1,0},{2,3},{3,2},{4,5},{5,4},{6,7},{7,6},{8,9},{9,8},{10,11... | collective-permute-start | bytes 491528 | tf_op jit(solution)/shard_map/ppermute | solution.py:207
  7.9 0.1 collective-permute-start.4
  8.0 0.1 collective-permute-done.other_ref
  8.1 2.6 %collective-permute-start.1 = (f32[512,128]{1,0:T(8,128)S(1)}, f32[512,128]{1,0:T(8,128)S(1)}, u32[]{:S(2)}, u32[]{:S(2)}) collective-permute-start(f32[512,128]{1,0:T(8,128)S(1)} %shard_map.121), channel_id=1, source_target_pairs={{2,0},{6,1},{10,2},{14,3},{3,4},{7,5},{11,6},{15,7},{0,8},{4,9},{8... | collective-permute-start | bytes 786440 | tf_op jit(solution)/shard_map/ppermute | solution.py:241
  10.7 0.7 %collective-permute-start.2 = (f32[512,128]{1,0:T(8,128)S(1)}, f32[512,128]{1,0:T(8,128)S(1)}, u32[]{:S(2)}, u32[]{:S(2)}) collective-permute-start(f32[512,128]{1,0:T(8,128)S(1)} %shard_map.121), channel_id=1, source_target_pairs={{0,0},{4,1},{8,2},{12,3},{1,4},{5,5},{9,6},{13,7},{2,8},{6,9},{10,... | collective-permute-start | bytes 786440 | tf_op jit(solution)/shard_map/ppermute | solution.py:241
  11.4 4.8 %collective-permute-done.5.refs_3_ = f32[320,256]{1,0:T(8,128)S(1)} collective-permute-done((f32[320,256]{1,0:T(8,128)}, f32[320,256]{1,0:T(8,128)S(1)}, u32[]{:S(2)}, u32[]{:S(2)}) %collective-permute-start.5) | collective-permute-done | bytes 327712 | tf_op jit(solution)/shard_map/ppermute | solution.py:207
  16.2 0.1 collective-permute-start.6
  16.3 0.0 copy-start.3
  16.3 0.0 copy-start.4
  16.3 0.5 %collective-permute-start.7 = (f32[160,256]{1,0:T(8,128)S(1)}, f32[160,256]{1,0:T(8,128)S(1)}, u32[]{:S(2)}, u32[]{:S(2)}) collective-permute-start(f32[160,256]{1,0:T(8,128)S(1)} %get-tuple-element.26), channel_id=1, source_target_pairs={{0,1},{1,0},{2,3},{3,2},{4,5},{5,4},{6,7},{7,6},{8,9},{9,8},{10,11... | collective-permute-start | bytes 491528 | tf_op jit(solution)/shard_map/ppermute | solution.py:207
  16.9 2.9 %collective-permute-start.8 = (f32[512,128]{1,0:T(8,128)S(1)}, f32[512,128]{1,0:T(8,128)S(1)}, u32[]{:S(2)}, u32[]{:S(2)}) collective-permute-start(f32[512,128]{1,0:T(8,128)S(1)} %shard_map.124), channel_id=1, source_target_pairs={{2,0},{6,1},{10,2},{14,3},{3,4},{7,5},{11,6},{15,7},{0,8},{4,9},{8... | collective-permute-start | bytes 786440 | tf_op jit(solution)/shard_map/ppermute | solution.py:241
  19.8 0.7 %collective-permute-start.9 = (f32[512,128]{1,0:T(8,128)S(1)}, f32[512,128]{1,0:T(8,128)S(1)}, u32[]{:S(2)}, u32[]{:S(2)}) collective-permute-start(f32[512,128]{1,0:T(8,128)S(1)} %shard_map.124), channel_id=1, source_target_pairs={{0,0},{4,1},{8,2},{12,3},{1,4},{5,5},{9,6},{13,7},{2,8},{6,9},{10,... | collective-permute-start | bytes 786440 | tf_op jit(solution)/shard_map/ppermute | solution.py:241
  20.5 1.0 %shard_map.122 = (f32[128,128]{1,0:T(8,128)S(1)}, bf16[4,256,256]{2,1,0:T(8,128)(2,1)S(1)}, bf16[4,256,256]{2,1,0:T(8,128)(2,1)S(1)}) custom-call(f32[320,256]{1,0:T(8,128)S(1)} %copy-done, f32[160,256]{1,0:T(8,128)S(1)} %collective-permute-done.3.refs_1_, f32[160,256]{1,0:T(8,128)S(1)} %collective-permute-done.4.refs_2_, ...), custom_call_target="tpu_custom_call" | custom-call | bytes 2621440 | tf_op jit(solution)/shard_map/pallas_call | solution.py:195
  21.5 1.3 %shard_map.123 = (f32[256,128]{1,0:T(8,128)}, f32[384,128]{1,0:T(8,128)S(1)}) custom-call(f32[512,128]{1,0:T(8,128)S(1)} %collective-permute-done.1.refs_0_, f32[512,128]{1,0:T(8,128)S(1)} %collective-permute-done.2.refs_1_, bf16[4,256,256]{2,1,0:T(8,128)(2,1)S(1)} %get-tuple-element.17.refs_2_, bf16[4,256,256]{2,1,0:T(8,128)(2,1)S(1)} %get-tuple-element.18.refs_3_), custom_call_target="tpu_custom_call" | custom-call | bytes 2424832 | tf_op jit(solution)/shard_map/pallas_call | solution.py:195
  22.9 15.0 %all_gather.3.refs_4_ = f32[1536,128]{1,0:T(8,128)S(1)} all-gather(f32[384,128]{1,0:T(8,128)S(1)} %get-tuple-element.21.refs_7_), channel_id=1, replica_groups=mesh['pole'=2,'row'=4,'col'=4] {'col'}, dimensions={0}, use_global_device_ids=true | all-gather | bytes 983040 | tf_op jit(solution)/shard_map/all_gather | solution.py:315
  37.9 2.2 %shard_map.125 = (f32[256,128]{1,0:T(8,128)}, f32[136,128]{1,0:T(8,128)S(1)}) custom-call(f32[512,128]{1,0:T(8,128)S(1)} %collective-permute-done.8.refs_0_, f32[512,128]{1,0:T(8,128)S(1)} %collective-permute-done.9.refs_1_, bf16[4,256,256]{2,1,0:T(8,128)(2,1)S(1)} %get-tuple-element.17.refs_2_, bf16[4,256,256]{2,1,0:T(8,128)(2,1)S(1)} %get-tuple-element.18.refs_3_, ...), custom_call_target="tpu_custom_call" | custom-call | bytes 3346432 | tf_op jit(solution)/shard_map/pallas_call | solution.py:195
  40.1 4.5 %collective-permute-start.10 = (f32[136,128]{1,0:T(8,128)S(1)}, f32[136,128]{1,0:T(8,128)S(1)}, u32[]{:S(2)}, u32[]{:S(2)}) collective-permute-start(f32[136,128]{1,0:T(8,128)S(1)} %get-tuple-element.22.refs_0_), channel_id=1, source_target_pairs={{0,12},{4,8},{8,4},{12,0},{1,13},{5,9},{9,5},{13,1},{2,14},{6,10},... | collective-permute-start | bytes 208904 | tf_op jit(solution)/shard_map/ppermute | solution.py:207
  44.6 0.6 %collective-permute-start.12 = (f32[136,128]{1,0:T(8,128)S(1)}, f32[136,128]{1,0:T(8,128)S(1)}, u32[]{:S(2)}, u32[]{:S(2)}) collective-permute-start(f32[136,128]{1,0:T(8,128)S(1)} %get-tuple-element.22.refs_0_), channel_id=1, source_target_pairs={{0,4},{4,0},{8,12},{12,8},{1,5},{5,1},{9,13},{13,9},{2,6},{6,2},{1... | collective-permute-start | bytes 208904 | tf_op jit(solution)/shard_map/ppermute | solution.py:207
  45.1 2.4 %collective-permute-done.10.refs_1_ = f32[136,128]{1,0:T(8,128)S(1)} collective-permute-done((f32[136,128]{1,0:T(8,128)S(1)}, f32[136,128]{1,0:T(8,128)S(1)}, u32[]{:S(2)}, u32[]{:S(2)}) %collective-permute-start.10) | collective-permute-done | bytes 69664 | tf_op jit(solution)/shard_map/ppermute | solution.py:207
  47.5 2.9 %collective-permute-done.11.refs_2_ = f32[136,128]{1,0:T(8,128)S(1)} collective-permute-done((f32[136,128]{1,0:T(8,128)S(1)}, f32[136,128]{1,0:T(8,128)S(1)}, u32[]{:S(2)}, u32[]{:S(2)}) %collective-permute-start.11) | collective-permute-done | bytes 69664 | tf_op jit(solution)/shard_map/ppermute | solution.py:207
  50.4 0.8 %shard_map.126 = (f32[128,128]{1,0:T(8,128)}, f32[128,128]{1,0:T(8,128)}) custom-call(f32[128,128]{1,0:T(8,128)S(1)} %copy-done.2, f32[128,128]{1,0:T(8,128)S(1)} %get-tuple-element.20.e_ref, f32[136,128]{1,0:T(8,128)S(1)} %get-tuple-element.22.refs_0_, f32[136,128]{1,0:T(8,128)S(1)} %collective-permute-done.10.refs_1_, ...), custom_call_target="tpu_custom_call" | custom-call | bytes 540672 | tf_op jit(solution)/shard_map/pallas_call | solution.py:195
  (24 shorter events, 0.1 us)
Async XLA Ops:
  3.3 12.9 %collective-permute-start.5 = (f32[320,256]{1,0:T(8,128)}, f32[320,256]{1,0:T(8,128)S(1)}, u32[]{:S(2)}, u32[]{:S(2)}) collective-permute-start(f32[320,256]{1,0:T(8,128)} %get-tuple-element.16.refs_0_), channel_id=1, source_target_pairs={{0,2},{1,3},{2,0},{3,1},{4,6},{5,7},{6,4},{7,5},{8,10},{9,11},{10,... | collective-permute-start | bytes 983048 | tf_op jit(solution)/shard_map/ppermute | solution.py:207
  6.3 1.8 %copy-start.1 = (f32[512,128]{1,0:T(8,128)S(1)}, f32[512,128]{1,0:T(8,128)}, u32[]{:S(2)}) copy-start(f32[512,128]{1,0:T(8,128)} %get-tuple-element.15.own_ref) | copy-start | bytes 786436
  6.3 1.7 %collective-permute-start = (f32[512,128]{1,0:T(8,128)}, f32[512,128]{1,0:T(8,128)S(1)}, u32[]{:S(2)}, u32[]{:S(2)}) collective-permute-start(f32[512,128]{1,0:T(8,128)} %get-tuple-element.15.own_ref), channel_id=1, source_target_pairs={{0,1},{1,0},{2,3},{3,2},{4,5},{5,4},{6,7},{7,6},{8,9},{9,8},{10,11... | collective-permute-start | bytes 786440 | tf_op jit(solution)/shard_map/ppermute | solution.py:207
  7.4 8.9 %collective-permute-start.3 = (f32[160,256]{1,0:T(8,128)S(1)}, f32[160,256]{1,0:T(8,128)S(1)}, u32[]{:S(2)}, u32[]{:S(2)}) collective-permute-start(f32[160,256]{1,0:T(8,128)S(1)} %get-tuple-element.29), channel_id=1, source_target_pairs={{0,1},{1,0},{2,3},{3,2},{4,5},{5,4},{6,7},{7,6},{8,9},{9,8},{10,11... | collective-permute-start | bytes 491528 | tf_op jit(solution)/shard_map/ppermute | solution.py:207
  7.9 9.0 %collective-permute-start.4 = (f32[160,256]{1,0:T(8,128)S(1)}, f32[160,256]{1,0:T(8,128)S(1)}, u32[]{:S(2)}, u32[]{:S(2)}) collective-permute-start(f32[160,256]{1,0:T(8,128)S(1)} %get-tuple-element.28), channel_id=1, source_target_pairs={{0,1},{1,0},{2,3},{3,2},{4,5},{5,4},{6,7},{7,6},{8,9},{9,8},{10,11... | collective-permute-start | bytes 491528 | tf_op jit(solution)/shard_map/ppermute | solution.py:207
  8.1 13.5 %collective-permute-start.1 = (f32[512,128]{1,0:T(8,128)S(1)}, f32[512,128]{1,0:T(8,128)S(1)}, u32[]{:S(2)}, u32[]{:S(2)}) collective-permute-start(f32[512,128]{1,0:T(8,128)S(1)} %shard_map.121), channel_id=1, source_target_pairs={{2,0},{6,1},{10,2},{14,3},{3,4},{7,5},{11,6},{15,7},{0,8},{4,9},{8... | collective-permute-start | bytes 786440 | tf_op jit(solution)/shard_map/ppermute | solution.py:241
  10.7 10.8 %collective-permute-start.2 = (f32[512,128]{1,0:T(8,128)S(1)}, f32[512,128]{1,0:T(8,128)S(1)}, u32[]{:S(2)}, u32[]{:S(2)}) collective-permute-start(f32[512,128]{1,0:T(8,128)S(1)} %shard_map.121), channel_id=1, source_target_pairs={{0,0},{4,1},{8,2},{12,3},{1,4},{5,5},{9,6},{13,7},{2,8},{6,9},{10,... | collective-permute-start | bytes 786440 | tf_op jit(solution)/shard_map/ppermute | solution.py:241
  16.2 3.6 %collective-permute-start.6 = (f32[160,256]{1,0:T(8,128)S(1)}, f32[160,256]{1,0:T(8,128)S(1)}, u32[]{:S(2)}, u32[]{:S(2)}) collective-permute-start(f32[160,256]{1,0:T(8,128)S(1)} %get-tuple-element.27), channel_id=1, source_target_pairs={{0,1},{1,0},{2,3},{3,2},{4,5},{5,4},{6,7},{7,6},{8,9},{9,8},{10,11... | collective-permute-start | bytes 491528 | tf_op jit(solution)/shard_map/ppermute | solution.py:207
  16.3 4.2 %copy-start = (f32[320,256]{1,0:T(8,128)S(1)}, f32[320,256]{1,0:T(8,128)}, u32[]{:S(2)}) copy-start(f32[320,256]{1,0:T(8,128)} %get-tuple-element.16.refs_0_) | copy-start | bytes 983044
  16.3 4.2 %copy-start.3 = (f32[128,128]{1,0:T(8,128)S(1)}, f32[128,128]{1,0:T(8,128)}, u32[]{:S(2)}) copy-start(f32[128,128]{1,0:T(8,128)} %refs_6_.3) | copy-start | bytes 196612
  16.3 4.2 %copy-start.4 = (f32[128,128]{1,0:T(8,128)S(1)}, f32[128,128]{1,0:T(8,128)}, u32[]{:S(2)}) copy-start(f32[128,128]{1,0:T(8,128)} %refs_8_.1) | copy-start | bytes 196612
  16.3 4.2 %copy-start.5 = (s32[4]{0:T(128)S(1)}, s32[4]{0:T(128)}, u32[]{:S(2)}) copy-start(s32[4]{0:T(128)} %refs_5_.1) | copy-start | bytes 52
  16.3 4.1 %collective-permute-start.7 = (f32[160,256]{1,0:T(8,128)S(1)}, f32[160,256]{1,0:T(8,128)S(1)}, u32[]{:S(2)}, u32[]{:S(2)}) collective-permute-start(f32[160,256]{1,0:T(8,128)S(1)} %get-tuple-element.26), channel_id=1, source_target_pairs={{0,1},{1,0},{2,3},{3,2},{4,5},{5,4},{6,7},{7,6},{8,9},{9,8},{10,11... | collective-permute-start | bytes 491528 | tf_op jit(solution)/shard_map/ppermute | solution.py:207
  16.9 21.0 %collective-permute-start.8 = (f32[512,128]{1,0:T(8,128)S(1)}, f32[512,128]{1,0:T(8,128)S(1)}, u32[]{:S(2)}, u32[]{:S(2)}) collective-permute-start(f32[512,128]{1,0:T(8,128)S(1)} %shard_map.124), channel_id=1, source_target_pairs={{2,0},{6,1},{10,2},{14,3},{3,4},{7,5},{11,6},{15,7},{0,8},{4,9},{8... | collective-permute-start | bytes 786440 | tf_op jit(solution)/shard_map/ppermute | solution.py:241
  19.8 18.1 %collective-permute-start.9 = (f32[512,128]{1,0:T(8,128)S(1)}, f32[512,128]{1,0:T(8,128)S(1)}, u32[]{:S(2)}, u32[]{:S(2)}) collective-permute-start(f32[512,128]{1,0:T(8,128)S(1)} %shard_map.124), channel_id=1, source_target_pairs={{0,0},{4,1},{8,2},{12,3},{1,4},{5,5},{9,6},{13,7},{2,8},{6,9},{10,... | collective-permute-start | bytes 786440 | tf_op jit(solution)/shard_map/ppermute | solution.py:241
  37.9 12.5 %copy-start.2 = (f32[128,128]{1,0:T(8,128)S(1)}, f32[128,128]{1,0:T(8,128)}, u32[]{:S(2)}) copy-start(f32[128,128]{1,0:T(8,128)} %dinv_ref.3) | copy-start | bytes 196612
  40.1 7.4 %collective-permute-start.10 = (f32[136,128]{1,0:T(8,128)S(1)}, f32[136,128]{1,0:T(8,128)S(1)}, u32[]{:S(2)}, u32[]{:S(2)}) collective-permute-start(f32[136,128]{1,0:T(8,128)S(1)} %get-tuple-element.22.refs_0_), channel_id=1, source_target_pairs={{0,12},{4,8},{8,4},{12,0},{1,13},{5,9},{9,5},{13,1},{2,14},{6,10},... | collective-permute-start | bytes 208904 | tf_op jit(solution)/shard_map/ppermute | solution.py:207
  44.6 5.8 %collective-permute-start.11 = (f32[136,128]{1,0:T(8,128)S(1)}, f32[136,128]{1,0:T(8,128)S(1)}, u32[]{:S(2)}, u32[]{:S(2)}) collective-permute-start(f32[136,128]{1,0:T(8,128)S(1)} %get-tuple-element.22.refs_0_), channel_id=1, source_target_pairs={{0,8},{4,12},{8,0},{12,4},{1,9},{5,13},{9,1},{13,5},{2,10},{6,14},... | collective-permute-start | bytes 208904 | tf_op jit(solution)/shard_map/ppermute | solution.py:207
  44.6 5.8 %collective-permute-start.12 = (f32[136,128]{1,0:T(8,128)S(1)}, f32[136,128]{1,0:T(8,128)S(1)}, u32[]{:S(2)}, u32[]{:S(2)}) collective-permute-start(f32[136,128]{1,0:T(8,128)S(1)} %get-tuple-element.22.refs_0_), channel_id=1, source_target_pairs={{0,4},{4,0},{8,12},{12,8},{1,5},{5,1},{9,13},{13,9},{2,6},{6,2},{1... | collective-permute-start | bytes 208904 | tf_op jit(solution)/shard_map/ppermute | solution.py:207

commit v5 on v4

v5 whole, which is shorter than its diff:
```python
import functools

import jax
import jax.numpy as jnp
from jax import lax
from jax.experimental import pallas as pl
from jax.experimental.pallas import tpu as pltpu
from jax.sharding import PartitionSpec as P

VMEM = pl.BlockSpec(memory_space=pltpu.VMEM)
SMEM = pl.BlockSpec(memory_space=pltpu.SMEM)
NN = ((1,), (0,))
TN = ((0,), (0,))
BLOCK = 128
PIECES = 2


def split(x):
    high = x.astype(jnp.bfloat16)
    return high, (x - high.astype(jnp.float32)).astype(jnp.bfloat16)


def dot_split(a, b, dims):
    def one(left, right):
        return lax.dot_general(left, right, (dims, ((), ())), preferred_element_type=jnp.float32)

    return one(a[0], b[0]) + (one(a[0], b[1]) + one(a[1], b[0]))


def dot3(a, b, dims=NN):
    return dot_split(split(a), split(b), dims)


def slots(nrow, ncol):
    q = ncol // nrow
    r, c = lax.axis_index("row"), lax.axis_index("col")
    own = [(r * q + i) ^ c for i in range(q)]
    return (r * q + c % q) ^ (c // q % 2 * (ncol // 2)) ^ c, own, c


def prepare_kernel(
    lower_ref, dinv_ref, first_ref, second_ref, one_ref, two_ref, side_ref, out1_ref, out2_ref, raw_ref, sems
):
    block = dinv_ref.shape[0]
    high, width = first_ref.shape
    across = width // BLOCK
    loads = [(first_ref, raw_ref.at[0]), (second_ref, raw_ref.at[1])]
    loads += [(lower_ref, side_ref.at[:block]), (dinv_ref, side_ref.at[block:])]
    copies = [pltpu.make_async_copy(src, dst, sems.at[i]) for i, (src, dst) in enumerate(loads)]
    for copy in copies:
        copy.start()
    for level, (pattern_ref, out_ref) in enumerate(((one_ref, out1_ref), (two_ref, out2_ref))):
        copies[level].wait()
        for i in range(high // BLOCK):
            rows = slice(i * BLOCK, (i + 1) * BLOCK)
            for j in range(across):
                cols = slice(j * BLOCK, (j + 1) * BLOCK)
                factor = pattern_ref[i * across + j].astype(jnp.float32)
                out_ref[rows, cols] = raw_ref[level, rows, cols] * factor
    for copy in copies[2:]:
        copy.wait()


def child_kernel(nrow, ncol, *refs):
    f_refs = refs[:nrow]
    second_ref, side_ref, parent_ref, sorted_ref, child_ref, held_ref = refs[nrow:]
    q = ncol // nrow
    depth = second_ref.shape[0]
    block = child_ref.shape[1] // q
    r, c = lax.axis_index("row"), lax.axis_index("col")
    for m in range(nrow):
        for j in range(q):
            held_ref[m * q + j] = f_refs[m][:, j * block : (j + 1) * block]
    for j in range(ncol):
        target = c ^ j
        sorted_ref[j * depth : (j + 1) * depth] = held_ref[((target // q) ^ r) * q + target % q]
    for j in range(q):
        mine = r * q + j
        above = parent_ref[mine]
        factor = held_ref[((above // q) ^ r) * q + above % q]
        lower = side_ref[pl.ds(pl.multiple_of(mine * 2 * block, block), block)]
        cols = slice(j * block, (j + 1) * block)
        child_ref[:, cols] = second_ref[:, cols] - dot3(factor, lower)


def pair_kernel(own_ref, other_ref, out_ref):
    depth = own_ref.shape[0]
    out_ref[:depth] = own_ref[...]
    out_ref[depth:] = other_ref[...]


def panel_kernel(nrow, ncol, *refs):
    count = ncol // 2 * (1 + PIECES)
    r_refs = refs[:count]
    side_ref, parent_ref, lower_ref, dinv_ref, e_ref, rh_ref, rl_ref = refs[count:]
    block = dinv_ref.shape[0]
    for j in range(ncol):
        first = j // 2 * (1 + PIECES)
        start = 0
        for ref in r_refs[first + 1 : first + 1 + PIECES] if j % 2 else r_refs[first : first + 1]:
            stop = start + ref.shape[0]
            rh_ref[j, start:stop], rl_ref[j, start:stop] = split(ref[...])
            start = stop
    above = parent_ref[lax.axis_index("col")]
    lower = split(lower_ref[...])
    dinv = side_ref[pl.ds(pl.multiple_of(above * 2 * block + block, block), block)]
    product = dot_split(split(dinv), lower, NN)
    e_ref[...] = dinv_ref[...] + dot_split(lower, split(product), TN)


def spread(nrow, ncol, refs, high_ref, low_ref):
    base, own, _ = slots(nrow, ncol)
    depth = refs[0].shape[0] // 2
    for t in range(ncol):
        slot = base ^ t
        part = refs[-1 - t // 2][t % 2 * depth : (t % 2 + 1) * depth]
        high_ref[slot], low_ref[slot] = split(part)
    return own, depth


def products(nrow, ncol, own, depth, r_refs, w_refs):
    total = None
    for j in range(ncol):
        term = dot_split((r_refs[0][j], r_refs[1][j]), (w_refs[0][j], w_refs[1][j]), NN)
        total = term if total is None else total + term
    diag = None
    for i, slot in enumerate(own):
        part = split(total[i * depth : (i + 1) * depth])
        term = dot_split((w_refs[0][slot], w_refs[1][slot]), part, TN)
        diag = term if diag is None else diag + term
    return total, diag


def first_kernel(nrow, ncol, *refs):
    rh_ref, rl_ref, x_ref, d_ref, fh_ref, fl_ref = refs[ncol:]
    own = slots(nrow, ncol)[1]
    depth = refs[0].shape[0]
    for j in range(ncol):
        fh_ref[j], fl_ref[j] = split(refs[j][...])
    total, diag = products(nrow, ncol, own, depth, (rh_ref, rl_ref), (fh_ref, fl_ref))
    x_ref[...] = -total
    d_ref[...] = diag


def second_kernel(nrow, ncol, *refs):
    rh_ref, rl_ref, d_ref, y_ref, m_ref, sh_ref, sl_ref = refs[ncol // 2 :]
    own, depth = spread(nrow, ncol, refs[: ncol // 2], sh_ref, sl_ref)
    total, diag = products(nrow, ncol, own, depth, (rh_ref, rl_ref), (sh_ref, sl_ref))
    y_ref[...] = -total
    block = diag.shape[0]
    across = lax.broadcasted_iota(jnp.int32, diag.shape, 1)
    down = lax.broadcasted_iota(jnp.int32, diag.shape, 0)
    m_ref[:block] = jnp.where(down <= across, d_ref[...], diag)
    line = jnp.sum(jnp.where(down == across, diag, 0.0), axis=0, keepdims=True)
    m_ref[block:] = jnp.broadcast_to(line, (m_ref.shape[0] - block, line.shape[1]))


def last_kernel(dinv_ref, e_ref, *refs):
    one_ref, two_ref = refs[-2:]
    block = dinv_ref.shape[0]
    total = refs[0][...]
    for ref in refs[1:-2]:
        total += ref[...]
    m = total[:block]
    across = lax.broadcasted_iota(jnp.int32, m.shape, 1)
    down = lax.broadcasted_iota(jnp.int32, m.shape, 0)
    turned = m.T
    one_ref[...] = dinv_ref[...] + jnp.where(down <= across, m, turned)
    line = jnp.broadcast_to(total[block : block + 1], m.shape)
    two_ref[...] = e_ref[...] + jnp.where(
        down == across, line, jnp.where(down > across, m, turned)
    )


def call(kernel, outs, scratch, *args, flops=0):
    size = 0
    for shape, dtype in [(a.shape, a.dtype) for a in args] + outs + scratch:
        if len(shape) > 1:
            count = 1
            for extent in shape:
                count *= extent
            size += count * jnp.dtype(dtype).itemsize
    limit = min(56 << 20, 3 * size + (4 << 20))
    return pl.pallas_call(
        kernel,
        out_shape=[jax.ShapeDtypeStruct(shape, dtype) for shape, dtype in outs],
        in_specs=[SMEM if a.ndim == 1 else VMEM for a in args],
        out_specs=[VMEM] * len(outs),
        scratch_shapes=[pltpu.VMEM(shape, dtype) for shape, dtype in scratch],
        compiler_params=pltpu.CompilerParams(vmem_limit_bytes=limit),
        cost_estimate=pl.CostEstimate(flops=flops, bytes_accessed=size, transcendentals=0),
    )(*args)


def swap(x, axis, size, bit):
    return lax.ppermute(x, axis, [(i, i ^ bit) for i in range(size)])


def gather_xor(x, axis, size):
    blocks = {0: x}
    bit = size // 2
    while bit:
        for j in sorted(blocks):
            if bit > 1:
                blocks[j ^ bit] = swap(blocks[j], axis, size, bit)
        bit //= 2
    parts = []
    for j in range(0, size, 2):
        parts.append(blocks[j])
        count = blocks[j].shape[0] // PIECES
        parts += [
            swap(blocks[j][i * count : (i + 1) * count], axis, size, 1) for i in range(PIECES)
        ]
    return parts


def after_kernel(value_ref, after_ref, out_ref):
    out_ref[...] = value_ref[...]


def after(value, other):
    return call(after_kernel, [(value.shape, jnp.float32)], [], value, other)[0]


def turn(values, nrow, ncol, block):
    q = ncol // nrow
    out = []
    for t in range(0, ncol, 2):
        pairs = []
        for r in range(nrow):
            for c in range(ncol):
                k = (r * q + c % q) ^ (c // q % 2 * (ncol // 2)) ^ t
                pairs.append(((c // q) * ncol + k, r * ncol + c))
        part = values
        if q > 1:
            which = (lax.axis_index("col") ^ t) % q
            part = lax.dynamic_slice_in_dim(values, which * block, block, 1)
        out.append(lax.ppermute(part, ("row", "col"), pairs))
    return out


def on_device(
    nrow,
    ncol,
    inverse_root,
    lower_first,
    mask_first,
    dinv_first,
    lower_second,
    mask_second,
    parent,
    lower_parent,
    dinv_second,
):
    f32, bf16 = jnp.float32, jnp.bfloat16
    block = dinv_first.shape[0]
    rows, depth = inverse_root.shape
    wide = lower_first.shape
    anywhere = pl.BlockSpec(memory_space=pl.ANY)
    side, first, second = pl.pallas_call(
        prepare_kernel,
        out_shape=[
            jax.ShapeDtypeStruct((2 * block, block), f32),
            jax.ShapeDtypeStruct(wide, f32),
            jax.ShapeDtypeStruct(wide, f32),
        ],
        in_specs=[anywhere] * 4 + [SMEM] * 2,
        out_specs=[VMEM] * 3,
        scratch_shapes=[pltpu.VMEM((2, *wide), f32), pltpu.SemaphoreType.DMA((4,))],
    )(
        lower_parent,
        dinv_first,
        lower_first,
        lower_second,
        mask_first.reshape(-1),
        mask_second.reshape(-1),
    )
    f_row = [first] + [swap(first, "row", nrow, m) for m in range(1, nrow)]
    sides = lax.all_gather(side, "col", axis=0, tiled=True)
    r_parts = gather_xor(after(inverse_root, sides), "col", ncol)
    ordered, child = call(
        functools.partial(child_kernel, nrow, ncol),
        [((ncol * depth, block), f32), (wide, f32)],
        [((ncol, depth, block), f32)],
        *f_row,
        second,
        sides,
        parent,
    )
    pair = call(
        pair_kernel, [((2 * depth, wide[1]), f32)], [], child, swap(child, "col", ncol, 1)
    )[0]
    g_parts = turn(pair, nrow, ncol, block)
    f_parts = {0: ordered}
    bit = ncol // 2
    while bit:
        for j in sorted(f_parts):
            here = f_parts[j]
            f_parts[j] = here[: bit * depth]
            sent = here[bit * depth :]
            f_parts[j ^ bit] = swap(after(sent, pair) if 2 * bit == ncol else sent, "col", ncol, bit)
        bit //= 2
    halves = [((ncol, rows, depth), bf16)] * 2
    pieces = [((ncol, depth, block), bf16)] * 2
    start, r_high, r_low = call(
        functools.partial(panel_kernel, nrow, ncol),
        [((block, block), f32)] + halves,
        [],
        *r_parts,
        sides,
        parent,
        lower_parent,
        dinv_second,
    )
    inverse_first, terms = call(
        functools.partial(first_kernel, nrow, ncol),
        [((rows, block), f32), ((block, block), f32)],
        pieces,
        *[f_parts[j] for j in range(ncol)],
        r_high,
        r_low,
    )
    inverse_second, packed = call(
        functools.partial(second_kernel, nrow, ncol),
        [((rows, block), f32), ((block + 8, block), f32)],
        pieces,
        *g_parts[::-1],
        r_high,
        r_low,
        terms,
    )
    diag_first, diag_second = call(
        last_kernel,
        [((block, block), f32)] * 2,
        [],
        dinv_first,
        start,
        packed,
        *[swap(packed, "row", nrow, j) for j in range(1, nrow)],
    )
    return (inverse_first, diag_first, inverse_second, diag_second)


def solution(mesh):
    in_specs = (
        P(("pole", "row"), "col"),
        P(("pole", "col"), "row"),
        P("col", "row"),
        P("pole", "col"),
        P(("pole", "col"), "row"),
        P("col", "row"),
        P(),
        P("pole", "col"),
        P("pole", "col"),
    )
    out_specs = (
        P(("pole", "row"), "col"),
        P("pole", "col"),
        P(("pole", "row"), "col"),
        P("pole", "col"),
    )
    return jax.shard_map(
        functools.partial(on_device, mesh.shape["row"], mesh.shape["col"]),
        mesh=mesh,
        in_specs=in_specs,
        out_specs=out_specs,
        check_vma=False,
    )
```

time: 51.4 us -> 50.7 us (0.986)
  blocking collectives: 15 us -> 7.64 us
  waiting for transfers between devices: 10.1 us -> 14.7 us
  starting transfers between devices: 16.1 us -> 19.5 us
  local copies, waits for them, and re-layouts: 1.11 us -> 0.12 us
    all_gather x1, blocking collectives: 15 us -> 7.64 us  [on_device(): sides = lax.all_gather(side, 'col', axis=0, tiled=True)]
    ppermute x9 -> x15, starting transfers between devices: 9.27 us -> 14.5 us  [swap(): return lax.ppermute(x, axis, [(i, i ^ bit) for i in range(size)])]
    ppermute x9 -> x15, waiting for transfers between devices: 10.1 us -> 14.7 us  [swap(): return lax.ppermute(x, axis, [(i, i ^ bit) for i in range(size)])]
    ppermute x4 -> x2, starting transfers between devices: 6.84 us -> 5.04 us  [turn(): out.append(lax.ppermute(part, ('row', 'col'), pairs))]
    slice x2, local copies, waits for them, and re-layouts: 1.08 us -> 0.04 us  [gather_xor(): blocks[j][i * count:(i + 1) * count]]
    pallas_call x6 -> x8, Pallas kernels: 5.37 us -> 5.3 us  [call(): pl.pallas_call(kernel, out_shape=[jax.ShapeDtypeStruct(shape, dtype) for...]
  transfers between devices with their start and end apart: 13 -> 17, of which waited for: 4 -> 8; matrix products, arithmetic and copies ran while one was open for 2% -> 0% of each run, Pallas kernels for 5% -> 6%
where the time goes in v5:
time: 50.7 us; the launch traced here: 50.5 us
  starting transfers between devices  19.5 us (38%)
  waiting for transfers between devices  14.7 us (29%)
  Pallas kernels  7.74 us (15%)
  blocking collectives  7.64 us (15%)
  between operations  0.79 us (2%)
    ppermute x15, waiting for transfers between devices, swap(): return lax.ppermute(x, axis, [(i, i ^ bit) for i in range(size)])  14.7 us
    ppermute x15, starting transfers between devices, swap(): return lax.ppermute(x, axis, [(i, i ^ bit) for i in range(size)])  14.5 us
    all_gather x1, blocking collectives, on_device(): sides = lax.all_gather(side, 'col', axis=0, tiled=True)  7.64 us
    pallas_call x8, Pallas kernels, call(): pl.pallas_call(kernel, out_shape=[jax.ShapeDtypeStruct(shape, dtype) for...  5.3 us
    ppermute x2, starting transfers between devices, turn(): out.append(lax.ppermute(part, ('row', 'col'), pairs))  5.04 us
    pallas_call x1, Pallas kernels, on_device(): pl.pallas_call(prepare_kernel, out_shape=[jax.ShapeDtypeStruct((2 * block...  2.44 us
  transfers between devices with their start and end apart: 17, of which 8 were waited for; matrix products, arithmetic and copies ran while one was open for 0% of the time, Pallas kernels for 6%

profile of v5, /device:TPU:0, one launch (start us, length us, event | category | flops | bytes accessed | tf_op | source)
XLA Modules:
  0.0 50.5 jit_solution(4488326494808058894)
XLA Ops:
  0.6 2.4 %shard_map.120 = (f32[256,128]{1,0:T(8,128)}, f32[256,128]{1,0:T(8,128)}, f32[256,128]{1,0:T(8,128)}) custom-call(f32[128,128]{1,0:T(8,128)} %refs_8_.1, f32[128,128]{1,0:T(8,128)} %dinv_ref.3, f32[256,128]{1,0:T(8,128)} %first_ref.1, f32[256,128]{1,0:T(8,128)} %second_ref.1, s32[2]{0:T(128)} %bitcast.2, s32[2]{0:T(128)} %bitcast.3), custom_call_target="tpu_custom_call" | custom-call | tf_op jit(solution)/shard_map/pallas_call | solution.py:260
  3.1 5.1 %collective-permute-start.2 = (f32[256,128]{1,0:T(8,128)}, f32[256,128]{1,0:T(8,128)S(1)}, u32[]{:S(2)}, u32[]{:S(2)}) collective-permute-start(f32[256,128]{1,0:T(8,128)} %get-tuple-element.18.refs_0_), channel_id=1, source_target_pairs={{0,12},{4,8},{8,4},{12,0},{1,13},{5,9},{9,5},{13,1},{2,14},{6,10},... | collective-permute-start | bytes 393224 | tf_op jit(solution)/shard_map/ppermute | solution.py:196
  8.2 0.6 %collective-permute-start = (f32[256,128]{1,0:T(8,128)}, f32[256,128]{1,0:T(8,128)S(1)}, u32[]{:S(2)}, u32[]{:S(2)}) collective-permute-start(f32[256,128]{1,0:T(8,128)} %get-tuple-element.18.refs_0_), channel_id=1, source_target_pairs={{0,4},{4,0},{8,12},{12,8},{1,5},{5,1},{9,13},{13,9},{2,6},{6,2},{1... | collective-permute-start | bytes 393224 | tf_op jit(solution)/shard_map/ppermute | solution.py:196
  8.8 7.6 %all_gather.3.refs_5_.after_ref.refs_6_ = f32[1024,128]{1,0:T(8,128)S(1)} all-gather(f32[256,128]{1,0:T(8,128)} %get-tuple-element.20), channel_id=1, replica_groups=mesh['pole'=2,'row'=4,'col'=4] {'col'}, dimensions={0}, use_global_device_ids=true | all-gather | bytes 655360 | tf_op jit(solution)/shard_map/all_gather | solution.py:279
  16.5 0.9 %collective-permute-start.9 = (f32[256,256]{1,0:T(8,128)S(1)}, f32[256,256]{1,0:T(8,128)S(1)}, u32[]{:S(2)}, u32[]{:S(2)}) collective-permute-start(f32[256,256]{1,0:T(8,128)S(1)} %shard_map.124.refs_0_), channel_id=1, source_target_pairs={{0,2},{1,3},{2,0},{3,1},{4,6},{5,7},{6,4},{7,5},{8,10},{9,11},{10,... | collective-permute-start | bytes 786440 | tf_op jit(solution)/shard_map/ppermute | solution.py:196
  17.4 2.1 %collective-permute-done.1.refs_2_ = f32[256,128]{1,0:T(8,128)S(1)} collective-permute-done((f32[256,128]{1,0:T(8,128)}, f32[256,128]{1,0:T(8,128)S(1)}, u32[]{:S(2)}, u32[]{:S(2)}) %collective-permute-start.1) | collective-permute-done | bytes 131104 | tf_op jit(solution)/shard_map/ppermute | solution.py:196
  19.5 0.8 %shard_map.121 = (f32[1024,128]{1,0:T(8,128)S(1)}, f32[256,128]{1,0:T(8,128)S(1)}) custom-call(f32[256,128]{1,0:T(8,128)S(1)} %copy-done.3, f32[256,128]{1,0:T(8,128)S(1)} %collective-permute-done.refs_1_, f32[256,128]{1,0:T(8,128)S(1)} %collective-permute-done.1.refs_2_, f32[256,128]{1,0:T(8,128)S(1)} %collective-permute-done.2.refs_3_, ...), custom_call_target="tpu_custom_call" | custom-call | bytes 2359296 | tf_op jit(solution)/shard_map/pallas_call | solution.py:184
  20.4 0.6 %collective-permute-start.8 = (f32[128,256]{1,0:T(8,128)S(1)}, f32[128,256]{1,0:T(8,128)S(1)}, u32[]{:S(2)}, u32[]{:S(2)}) collective-permute-start(f32[128,256]{1,0:T(8,128)S(1)} %get-tuple-element.36), channel_id=1, source_target_pairs={{0,1},{1,0},{2,3},{3,2},{4,5},{5,4},{6,7},{7,6},{8,9},{9,8},{10,11... | collective-permute-start | bytes 393224 | tf_op jit(solution)/shard_map/ppermute | solution.py:196
  21.1 0.7 %collective-permute-done.4.other_ref = f32[256,128]{1,0:T(8,128)S(1)} collective-permute-done((f32[256,128]{1,0:T(8,128)S(1)}, f32[256,128]{1,0:T(8,128)S(1)}, u32[]{:S(2)}, u32[]{:S(2)}) %collective-permute-start.4) | collective-permute-done | bytes 131104 | tf_op jit(solution)/shard_map/ppermute | solution.py:196
  21.8 1.6 %collective-permute-start.5 = (f32[512,128]{1,0:T(8,128)S(1)}, f32[512,128]{1,0:T(8,128)S(1)}, u32[]{:S(2)}, u32[]{:S(2)}) collective-permute-start(f32[512,128]{1,0:T(8,128)S(1)} %shard_map.123), channel_id=1, source_target_pairs={{0,2},{1,3},{2,0},{3,1},{4,6},{5,7},{6,4},{7,5},{8,10},{9,11},{10,... | collective-permute-start | bytes 786440 | tf_op jit(solution)/shard_map/ppermute | solution.py:196
  23.3 0.7 %collective-permute-start.13 = (f32[512,128]{1,0:T(8,128)S(1)}, f32[512,128]{1,0:T(8,128)S(1)}, u32[]{:S(2)}, u32[]{:S(2)}) collective-permute-start(f32[512,128]{1,0:T(8,128)S(1)} %shard_map.122.after_ref), channel_id=1, source_target_pairs={{0,0},{6,1},{8,2},{14,3},{1,4},{7,5},{9,6},{15,7},{2,8},{4,9},{10,... | collective-permute-start | bytes 786440 | tf_op jit(solution)/shard_map/ppermute | solution.py:238
  24.0 1.7 %collective-permute-done.9.refs_3_ = f32[256,256]{1,0:T(8,128)S(1)} collective-permute-done((f32[256,256]{1,0:T(8,128)S(1)}, f32[256,256]{1,0:T(8,128)S(1)}, u32[]{:S(2)}, u32[]{:S(2)}) %collective-permute-start.9) | collective-permute-done | bytes 262176 | tf_op jit(solution)/shard_map/ppermute | solution.py:196
  25.7 4.4 %collective-permute-start.12 = (f32[512,128]{1,0:T(8,128)S(1)}, f32[512,128]{1,0:T(8,128)S(1)}, u32[]{:S(2)}, u32[]{:S(2)}) collective-permute-start(f32[512,128]{1,0:T(8,128)S(1)} %shard_map.122.after_ref), channel_id=1, source_target_pairs={{2,0},{4,1},{10,2},{12,3},{3,4},{5,5},{11,6},{13,7},{0,8},{6,9},{8... | collective-permute-start | bytes 786440 | tf_op jit(solution)/shard_map/ppermute | solution.py:238
  30.1 2.8 %collective-permute-done.5 = f32[512,128]{1,0:T(8,128)S(1)} collective-permute-done((f32[512,128]{1,0:T(8,128)S(1)}, f32[512,128]{1,0:T(8,128)S(1)}, u32[]{:S(2)}, u32[]{:S(2)}) %collective-permute-start.5) | collective-permute-done | bytes 262176 | tf_op jit(solution)/shard_map/ppermute | solution.py:196
  32.9 0.6 %collective-permute-start.10 = (f32[128,256]{1,0:T(8,128)S(1)}, f32[128,256]{1,0:T(8,128)S(1)}, u32[]{:S(2)}, u32[]{:S(2)}) collective-permute-start(f32[128,256]{1,0:T(8,128)S(1)} %get-tuple-element.35), channel_id=1, source_target_pairs={{0,1},{1,0},{2,3},{3,2},{4,5},{5,4},{6,7},{7,6},{8,9},{9,8},{10,11... | collective-permute-start | bytes 393224 | tf_op jit(solution)/shard_map/ppermute | solution.py:196
  33.6 0.7 %collective-permute-done.11.refs_5_ = f32[128,256]{1,0:T(8,128)S(1)} collective-permute-done((f32[128,256]{1,0:T(8,128)S(1)}, f32[128,256]{1,0:T(8,128)S(1)}, u32[]{:S(2)}, u32[]{:S(2)}) %collective-permute-start.11) | collective-permute-done | bytes 131104 | tf_op jit(solution)/shard_map/ppermute | solution.py:196
  34.5 1.1 %shard_map.125 = (f32[128,128]{1,0:T(8,128)S(1)}, bf16[4,256,256]{2,1,0:T(8,128)(2,1)S(1)}, bf16[4,256,256]{2,1,0:T(8,128)(2,1)S(1)}) custom-call(f32[256,256]{1,0:T(8,128)S(1)} %shard_map.124.refs_0_, f32[128,256]{1,0:T(8,128)S(1)} %collective-permute-done.7.refs_1_, f32[128,256]{1,0:T(8,128)S(1)} %collective-permute-done.8.refs_2_, ...), custom_call_target="tpu_custom_call" | custom-call | bytes 2818048 | tf_op jit(solution)/shard_map/pallas_call | solution.py:184
  35.6 1.3 %shard_map.126 = (f32[256,128]{1,0:T(8,128)}, f32[128,128]{1,0:T(8,128)S(1)}) custom-call(f32[256,128]{1,0:T(8,128)S(1)} %get-tuple-element.33.refs_0_, f32[256,128]{1,0:T(8,128)S(1)} %collective-permute-done.3.refs_1_, f32[256,128]{1,0:T(8,128)S(1)} %get-tuple-element.39.refs_2_, f32[256,128]{1,0:T(8,128)S(1)} %collective-permute-done.6.refs_3_, ...), custom_call_target="tpu_custom_call" | custom-call | bytes 2293760 | tf_op jit(solution)/shard_map/pallas_call | solution.py:184
  36.9 1.3 %shard_map.127 = (f32[256,128]{1,0:T(8,128)}, f32[136,128]{1,0:T(8,128)S(1)}) custom-call(f32[512,128]{1,0:T(8,128)S(1)} %collective-permute-done.12.refs_0_, f32[512,128]{1,0:T(8,128)S(1)} %collective-permute-done.13.refs_1_, bf16[4,256,256]{2,1,0:T(8,128)(2,1)S(1)} %get-tuple-element.23.refs_4_.refs_2_, ...), custom_call_target="tpu_custom_call" | custom-call | bytes 2363392 | tf_op jit(solution)/shard_map/pallas_call | solution.py:184
  38.2 4.2 %collective-permute-start.16 = (f32[136,128]{1,0:T(8,128)S(1)}, f32[136,128]{1,0:T(8,128)S(1)}, u32[]{:S(2)}, u32[]{:S(2)}) collective-permute-start(f32[136,128]{1,0:T(8,128)S(1)} %get-tuple-element.28.refs_0_), channel_id=1, source_target_pairs={{0,12},{4,8},{8,4},{12,0},{1,13},{5,9},{9,5},{13,1},{2,14},{6,10},... | collective-permute-start | bytes 208904 | tf_op jit(solution)/shard_map/ppermute | solution.py:196
  42.4 0.4 collective-permute-start.15
  42.9 1.8 %collective-permute-done.16.refs_3_ = f32[136,128]{1,0:T(8,128)S(1)} collective-permute-done((f32[136,128]{1,0:T(8,128)S(1)}, f32[136,128]{1,0:T(8,128)S(1)}, u32[]{:S(2)}, u32[]{:S(2)}) %collective-permute-start.16) | collective-permute-done | bytes 69664 | tf_op jit(solution)/shard_map/ppermute | solution.py:196
  44.8 4.9 %collective-permute-done.15.refs_2_ = f32[136,128]{1,0:T(8,128)S(1)} collective-permute-done((f32[136,128]{1,0:T(8,128)S(1)}, f32[136,128]{1,0:T(8,128)S(1)}, u32[]{:S(2)}, u32[]{:S(2)}) %collective-permute-start.15) | collective-permute-done | bytes 69664 | tf_op jit(solution)/shard_map/ppermute | solution.py:196
  49.7 0.8 %shard_map.128 = (f32[128,128]{1,0:T(8,128)}, f32[128,128]{1,0:T(8,128)}) custom-call(f32[128,128]{1,0:T(8,128)S(1)} %copy-done.1, f32[128,128]{1,0:T(8,128)S(1)} %get-tuple-element.26.e_ref, f32[136,128]{1,0:T(8,128)S(1)} %get-tuple-element.28.refs_0_, f32[136,128]{1,0:T(8,128)S(1)} %collective-permute-done.14.refs_1_, ...), custom_call_target="tpu_custom_call" | custom-call | bytes 540672 | tf_op jit(solution)/shard_map/pallas_call | solution.py:184
  (39 shorter events, 0.8 us)
Async XLA Ops:
  3.1 14.3 %collective-permute-start.2 = (f32[256,128]{1,0:T(8,128)}, f32[256,128]{1,0:T(8,128)S(1)}, u32[]{:S(2)}, u32[]{:S(2)}) collective-permute-start(f32[256,128]{1,0:T(8,128)} %get-tuple-element.18.refs_0_), channel_id=1, source_target_pairs={{0,12},{4,8},{8,4},{12,0},{1,13},{5,9},{9,5},{13,1},{2,14},{6,10},... | collective-permute-start | bytes 393224 | tf_op jit(solution)/shard_map/ppermute | solution.py:196
  8.2 11.3 %collective-permute-start.1 = (f32[256,128]{1,0:T(8,128)}, f32[256,128]{1,0:T(8,128)S(1)}, u32[]{:S(2)}, u32[]{:S(2)}) collective-permute-start(f32[256,128]{1,0:T(8,128)} %get-tuple-element.18.refs_0_), channel_id=1, source_target_pairs={{0,8},{4,12},{8,0},{12,4},{1,9},{5,13},{9,1},{13,5},{2,10},{6,14},... | collective-permute-start | bytes 393224 | tf_op jit(solution)/shard_map/ppermute | solution.py:196
  8.2 11.3 %collective-permute-start = (f32[256,128]{1,0:T(8,128)}, f32[256,128]{1,0:T(8,128)S(1)}, u32[]{:S(2)}, u32[]{:S(2)}) collective-permute-start(f32[256,128]{1,0:T(8,128)} %get-tuple-element.18.refs_0_), channel_id=1, source_target_pairs={{0,4},{4,0},{8,12},{12,8},{1,5},{5,1},{9,13},{13,9},{2,6},{6,2},{1... | collective-permute-start | bytes 393224 | tf_op jit(solution)/shard_map/ppermute | solution.py:196
  8.8 7.6 %copy-start.2 = (f32[256,256]{1,0:T(8,128)S(1)}, f32[256,256]{1,0:T(8,128)}, u32[]{:S(2)}) copy-start(f32[256,256]{1,0:T(8,128)} %value_ref.1) | copy-start | bytes 786436
  16.5 3.0 %copy-start.3 = (f32[256,128]{1,0:T(8,128)S(1)}, f32[256,128]{1,0:T(8,128)}, u32[]{:S(2)}) copy-start(f32[256,128]{1,0:T(8,128)} %get-tuple-element.18.refs_0_) | copy-start | bytes 393220
  16.5 3.0 %copy-start.4 = (f32[256,128]{1,0:T(8,128)S(1)}, f32[256,128]{1,0:T(8,128)}, u32[]{:S(2)}) copy-start(f32[256,128]{1,0:T(8,128)} %get-tuple-element.19.refs_4_) | copy-start | bytes 393220
  16.5 3.0 %copy-start.6 = (s32[4]{0:T(128)S(1)}, s32[4]{0:T(128)}, u32[]{:S(2)}) copy-start(s32[4]{0:T(128)} %refs_7_.1) | copy-start | bytes 52
  16.5 9.2 %collective-permute-start.9 = (f32[256,256]{1,0:T(8,128)S(1)}, f32[256,256]{1,0:T(8,128)S(1)}, u32[]{:S(2)}, u32[]{:S(2)}) collective-permute-start(f32[256,256]{1,0:T(8,128)S(1)} %shard_map.124.refs_0_), channel_id=1, source_target_pairs={{0,2},{1,3},{2,0},{3,1},{4,6},{5,7},{6,4},{7,5},{8,10},{9,11},{10,... | collective-permute-start | bytes 786440 | tf_op jit(solution)/shard_map/ppermute | solution.py:196
  20.3 1.4 %collective-permute-start.4 = (f32[256,128]{1,0:T(8,128)S(1)}, f32[256,128]{1,0:T(8,128)S(1)}, u32[]{:S(2)}, u32[]{:S(2)}) collective-permute-start(f32[256,128]{1,0:T(8,128)S(1)} %get-tuple-element.22.own_ref), channel_id=1, source_target_pairs={{0,1},{1,0},{2,3},{3,2},{4,5},{5,4},{6,7},{7,6},{8,9},{9,8},{10,11... | collective-permute-start | bytes 393224 | tf_op jit(solution)/shard_map/ppermute | solution.py:196
  20.4 12.5 %collective-permute-start.8 = (f32[128,256]{1,0:T(8,128)S(1)}, f32[128,256]{1,0:T(8,128)S(1)}, u32[]{:S(2)}, u32[]{:S(2)}) collective-permute-start(f32[128,256]{1,0:T(8,128)S(1)} %get-tuple-element.36), channel_id=1, source_target_pairs={{0,1},{1,0},{2,3},{3,2},{4,5},{5,4},{6,7},{7,6},{8,9},{9,8},{10,11... | collective-permute-start | bytes 393224 | tf_op jit(solution)/shard_map/ppermute | solution.py:196
  21.0 12.5 %collective-permute-start.7 = (f32[128,256]{1,0:T(8,128)S(1)}, f32[128,256]{1,0:T(8,128)S(1)}, u32[]{:S(2)}, u32[]{:S(2)}) collective-permute-start(f32[128,256]{1,0:T(8,128)S(1)} %get-tuple-element.37), channel_id=1, source_target_pairs={{0,1},{1,0},{2,3},{3,2},{4,5},{5,4},{6,7},{7,6},{8,9},{9,8},{10,11... | collective-permute-start | bytes 393224 | tf_op jit(solution)/shard_map/ppermute | solution.py:196
  21.8 11.1 %collective-permute-start.5 = (f32[512,128]{1,0:T(8,128)S(1)}, f32[512,128]{1,0:T(8,128)S(1)}, u32[]{:S(2)}, u32[]{:S(2)}) collective-permute-start(f32[512,128]{1,0:T(8,128)S(1)} %shard_map.123), channel_id=1, source_target_pairs={{0,2},{1,3},{2,0},{3,1},{4,6},{5,7},{6,4},{7,5},{8,10},{9,11},{10,... | collective-permute-start | bytes 786440 | tf_op jit(solution)/shard_map/ppermute | solution.py:196
  23.3 13.5 %collective-permute-start.13 = (f32[512,128]{1,0:T(8,128)S(1)}, f32[512,128]{1,0:T(8,128)S(1)}, u32[]{:S(2)}, u32[]{:S(2)}) collective-permute-start(f32[512,128]{1,0:T(8,128)S(1)} %shard_map.122.after_ref), channel_id=1, source_target_pairs={{0,0},{6,1},{8,2},{14,3},{1,4},{7,5},{9,6},{15,7},{2,8},{4,9},{10,... | collective-permute-start | bytes 786440 | tf_op jit(solution)/shard_map/ppermute | solution.py:238
  25.7 11.2 %collective-permute-start.12 = (f32[512,128]{1,0:T(8,128)S(1)}, f32[512,128]{1,0:T(8,128)S(1)}, u32[]{:S(2)}, u32[]{:S(2)}) collective-permute-start(f32[512,128]{1,0:T(8,128)S(1)} %shard_map.122.after_ref), channel_id=1, source_target_pairs={{2,0},{4,1},{10,2},{12,3},{3,4},{5,5},{11,6},{13,7},{0,8},{6,9},{8... | collective-permute-start | bytes 786440 | tf_op jit(solution)/shard_map/ppermute | solution.py:238
  32.9 1.6 %copy-start = (f32[128,128]{1,0:T(8,128)S(1)}, f32[128,128]{1,0:T(8,128)}, u32[]{:S(2)}) copy-start(f32[128,128]{1,0:T(8,128)} %refs_8_.1) | copy-start | bytes 196612
  32.9 1.6 %copy-start.5 = (f32[128,128]{1,0:T(8,128)S(1)}, f32[128,128]{1,0:T(8,128)}, u32[]{:S(2)}) copy-start(f32[128,128]{1,0:T(8,128)} %refs_9_.1) | copy-start | bytes 196612
  32.9 1.3 %collective-permute-start.11 = (f32[128,256]{1,0:T(8,128)S(1)}, f32[128,256]{1,0:T(8,128)S(1)}, u32[]{:S(2)}, u32[]{:S(2)}) collective-permute-start(f32[128,256]{1,0:T(8,128)S(1)} %get-tuple-element.34), channel_id=1, source_target_pairs={{0,1},{1,0},{2,3},{3,2},{4,5},{5,4},{6,7},{7,6},{8,9},{9,8},{10,11... | collective-permute-start | bytes 393224 | tf_op jit(solution)/shard_map/ppermute | solution.py:196
  32.9 1.6 %collective-permute-start.10 = (f32[128,256]{1,0:T(8,128)S(1)}, f32[128,256]{1,0:T(8,128)S(1)}, u32[]{:S(2)}, u32[]{:S(2)}) collective-permute-start(f32[128,256]{1,0:T(8,128)S(1)} %get-tuple-element.35), channel_id=1, source_target_pairs={{0,1},{1,0},{2,3},{3,2},{4,5},{5,4},{6,7},{7,6},{8,9},{9,8},{10,11... | collective-permute-start | bytes 393224 | tf_op jit(solution)/shard_map/ppermute | solution.py:196
  33.5 2.1 %collective-permute-start.3 = (f32[256,128]{1,0:T(8,128)S(1)}, f32[256,128]{1,0:T(8,128)S(1)}, u32[]{:S(2)}, u32[]{:S(2)}) collective-permute-start(f32[256,128]{1,0:T(8,128)S(1)} %get-tuple-element.32), channel_id=1, source_target_pairs={{0,1},{1,0},{2,3},{3,2},{4,5},{5,4},{6,7},{7,6},{8,9},{9,8},{10,11... | collective-permute-start | bytes 393224 | tf_op jit(solution)/shard_map/ppermute | solution.py:196
  34.2 1.4 %collective-permute-start.6 = (f32[256,128]{1,0:T(8,128)S(1)}, f32[256,128]{1,0:T(8,128)S(1)}, u32[]{:S(2)}, u32[]{:S(2)}) collective-permute-start(f32[256,128]{1,0:T(8,128)S(1)} %get-tuple-element.38), channel_id=1, source_target_pairs={{0,1},{1,0},{2,3},{3,2},{4,5},{5,4},{6,7},{7,6},{8,9},{9,8},{10,11... | collective-permute-start | bytes 393224 | tf_op jit(solution)/shard_map/ppermute | solution.py:196
  36.9 12.8 %copy-start.1 = (f32[128,128]{1,0:T(8,128)S(1)}, f32[128,128]{1,0:T(8,128)}, u32[]{:S(2)}) copy-start(f32[128,128]{1,0:T(8,128)} %dinv_ref.3) | copy-start | bytes 196612
  38.2 6.6 %collective-permute-start.16 = (f32[136,128]{1,0:T(8,128)S(1)}, f32[136,128]{1,0:T(8,128)S(1)}, u32[]{:S(2)}, u32[]{:S(2)}) collective-permute-start(f32[136,128]{1,0:T(8,128)S(1)} %get-tuple-element.28.refs_0_), channel_id=1, source_target_pairs={{0,12},{4,8},{8,4},{12,0},{1,13},{5,9},{9,5},{13,1},{2,14},{6,10},... | collective-permute-start | bytes 208904 | tf_op jit(solution)/shard_map/ppermute | solution.py:196
  42.4 7.3 %collective-permute-start.15 = (f32[136,128]{1,0:T(8,128)S(1)}, f32[136,128]{1,0:T(8,128)S(1)}, u32[]{:S(2)}, u32[]{:S(2)}) collective-permute-start(f32[136,128]{1,0:T(8,128)S(1)} %get-tuple-element.28.refs_0_), channel_id=1, source_target_pairs={{0,8},{4,12},{8,0},{12,4},{1,9},{5,13},{9,1},{13,5},{2,10},{6,14},... | collective-permute-start | bytes 208904 | tf_op jit(solution)/shard_map/ppermute | solution.py:196
  42.8 6.9 %collective-permute-start.14 = (f32[136,128]{1,0:T(8,128)S(1)}, f32[136,128]{1,0:T(8,128)S(1)}, u32[]{:S(2)}, u32[]{:S(2)}) collective-permute-start(f32[136,128]{1,0:T(8,128)S(1)} %get-tuple-element.28.refs_0_), channel_id=1, source_target_pairs={{0,4},{4,0},{8,12},{12,8},{1,5},{5,1},{9,13},{13,9},{2,6},{6,2},{1... | collective-permute-start | bytes 208904 | tf_op jit(solution)/shard_map/ppermute | solution.py:196

commit v6 on v5

--- a/solution.py
+++ b/solution.py
@@ -38,49 +38,45 @@
     return (r * q + c % q) ^ (c // q % 2 * (ncol // 2)) ^ c, own, c
 
 
-def prepare_kernel(
-    lower_ref, dinv_ref, first_ref, second_ref, one_ref, two_ref, side_ref, out1_ref, out2_ref, raw_ref, sems
-):
-    block = dinv_ref.shape[0]
-    high, width = first_ref.shape
+def apply_mask(values_ref, pattern_ref, out_ref):
+    high, width = values_ref.shape
     across = width // BLOCK
-    loads = [(first_ref, raw_ref.at[0]), (second_ref, raw_ref.at[1])]
-    loads += [(lower_ref, side_ref.at[:block]), (dinv_ref, side_ref.at[block:])]
-    copies = [pltpu.make_async_copy(src, dst, sems.at[i]) for i, (src, dst) in enumerate(loads)]
-    for copy in copies:
-        copy.start()
-    for level, (pattern_ref, out_ref) in enumerate(((one_ref, out1_ref), (two_ref, out2_ref))):
-        copies[level].wait()
-        for i in range(high // BLOCK):
-            rows = slice(i * BLOCK, (i + 1) * BLOCK)
-            for j in range(across):
-                cols = slice(j * BLOCK, (j + 1) * BLOCK)
-                factor = pattern_ref[i * across + j].astype(jnp.float32)
-                out_ref[rows, cols] = raw_ref[level, rows, cols] * factor
-    for copy in copies[2:]:
-        copy.wait()
+    for i in range(high // BLOCK):
+        rows = slice(i * BLOCK, (i + 1) * BLOCK)
+        for j in range(across):
+            cols = slice(j * BLOCK, (j + 1) * BLOCK)
+            factor = pattern_ref[i * across + j].astype(jnp.float32)
+            out_ref[rows, cols] = values_ref[rows, cols] * factor
+
+
+def mask_kernel(values_ref, pattern_ref, out_ref, raw_ref, sem):
+    copy = pltpu.make_async_copy(values_ref, raw_ref, sem)
+    copy.start()
+    copy.wait()
+    apply_mask(raw_ref, pattern_ref, out_ref)
 
 
 def child_kernel(nrow, ncol, *refs):
     f_refs = refs[:nrow]
-    second_ref, side_ref, parent_ref, sorted_ref, child_ref, held_ref = refs[nrow:]
+    second_ref, pattern_ref, side_ref, parent_ref, sorted_ref, child_ref, held_ref = refs[nrow:]
     q = ncol // nrow
     depth = second_ref.shape[0]
     block = child_ref.shape[1] // q
     r, c = lax.axis_index("row"), lax.axis_index("col")
     for m in range(nrow):
         for j in range(q):
-            held_ref[m * q + j] = f_refs[m][:, j * block : (j + 1) * block]
+            held_ref[(nrow - m) % nrow * q + j] = f_refs[m][:, j * block : (j + 1) * block]
     for j in range(ncol):
         target = c ^ j
         sorted_ref[j * depth : (j + 1) * depth] = held_ref[((target // q) ^ r) * q + target % q]
+    apply_mask(second_ref, pattern_ref, child_ref)
     for j in range(q):
         mine = r * q + j
         above = parent_ref[mine]
         factor = held_ref[((above // q) ^ r) * q + above % q]
-        lower = side_ref[pl.ds(pl.multiple_of(mine * 2 * block, block), block)]
+        lower = side_ref[pl.ds(pl.multiple_of(mine * block, block), block)]
         cols = slice(j * block, (j + 1) * block)
-        child_ref[:, cols] = second_ref[:, cols] - dot3(factor, lower)
+        child_ref[:, cols] -= dot3(factor, lower)
 
 
 def pair_kernel(own_ref, other_ref, out_ref):
@@ -92,19 +88,29 @@
 def panel_kernel(nrow, ncol, *refs):
     count = ncol // 2 * (1 + PIECES)
     r_refs = refs[:count]
-    side_ref, parent_ref, lower_ref, dinv_ref, e_ref, rh_ref, rl_ref = refs[count:]
+    parent_ref, lower_ref, dinv_ref, e_ref, rh_ref, rl_ref, sel_ref = refs[count:]
+    _, rows, depth = rh_ref.shape
     block = dinv_ref.shape[0]
+    part = block * block // depth
+    c = lax.axis_index("col")
+    chosen = parent_ref[c] ^ c
     for j in range(ncol):
         first = j // 2 * (1 + PIECES)
+        here = r_refs[first + 1 : first + 1 + PIECES] if j % 2 else r_refs[first : first + 1]
         start = 0
-        for ref in r_refs[first + 1 : first + 1 + PIECES] if j % 2 else r_refs[first : first + 1]:
-            stop = start + ref.shape[0]
-            rh_ref[j, start:stop], rl_ref[j, start:stop] = split(ref[...])
+        for ref in here:
+            stop = min(start + ref.shape[0], rows)
+            if start < stop:
+                rh_ref[j, start:stop], rl_ref[j, start:stop] = split(ref[: stop - start])
             start = stop
-    above = parent_ref[lax.axis_index("col")]
+
+        @pl.when(chosen == j)
+        def _(last=here[-1]):
+            for i in range(depth // block):
+                sel_ref[i * part : (i + 1) * part] = last[-part:, i * block : (i + 1) * block]
+
     lower = split(lower_ref[...])
-    dinv = side_ref[pl.ds(pl.multiple_of(above * 2 * block + block, block), block)]
-    product = dot_split(split(dinv), lower, NN)
+    product = dot_split(split(sel_ref[...]), lower, NN)
     e_ref[...] = dinv_ref[...] + dot_split(lower, split(product), TN)
 
 
@@ -214,6 +220,15 @@
     return parts
 
 
+def fold_kernel(root_ref, dinv_ref, after_ref, out_ref):
+    rows, depth = root_ref.shape
+    block = dinv_ref.shape[0]
+    part = block * block // depth
+    out_ref[:rows] = root_ref[...]
+    for i in range(depth // block):
+        out_ref[rows:, i * block : (i + 1) * block] = dinv_ref[i * part : (i + 1) * part]
+
+
 def after_kernel(value_ref, after_ref, out_ref):
     out_ref[...] = value_ref[...]
 
@@ -256,34 +271,25 @@
     block = dinv_first.shape[0]
     rows, depth = inverse_root.shape
     wide = lower_first.shape
-    anywhere = pl.BlockSpec(memory_space=pl.ANY)
-    side, first, second = pl.pallas_call(
-        prepare_kernel,
-        out_shape=[
-            jax.ShapeDtypeStruct((2 * block, block), f32),
-            jax.ShapeDtypeStruct(wide, f32),
-            jax.ShapeDtypeStruct(wide, f32),
-        ],
-        in_specs=[anywhere] * 4 + [SMEM] * 2,
-        out_specs=[VMEM] * 3,
-        scratch_shapes=[pltpu.VMEM((2, *wide), f32), pltpu.SemaphoreType.DMA((4,))],
-    )(
-        lower_parent,
-        dinv_first,
-        lower_first,
-        lower_second,
-        mask_first.reshape(-1),
-        mask_second.reshape(-1),
-    )
-    f_row = [first] + [swap(first, "row", nrow, m) for m in range(1, nrow)]
-    sides = lax.all_gather(side, "col", axis=0, tiled=True)
-    r_parts = gather_xor(after(inverse_root, sides), "col", ncol)
+    first = pl.pallas_call(
+        mask_kernel,
+        out_shape=jax.ShapeDtypeStruct(wide, f32),
+        in_specs=[pl.BlockSpec(memory_space=pl.ANY), SMEM],
+        out_specs=VMEM,
+        scratch_shapes=[pltpu.VMEM(wide, f32), pltpu.SemaphoreType.DMA],
+    )(lower_first, mask_first.reshape(-1))
+    f_row = [first] + [swap(first, "row", nrow, m) for m in range(nrow - 1, 0, -1)]
+    sides = lax.all_gather(lower_parent, "col", axis=0, tiled=True)
+    tall = (rows + block * block // depth, depth)
+    folded = call(fold_kernel, [(tall, f32)], [], inverse_root, dinv_first, sides)[0]
+    r_parts = gather_xor(folded, "col", ncol)
     ordered, child = call(
         functools.partial(child_kernel, nrow, ncol),
         [((ncol * depth, block), f32), (wide, f32)],
         [((ncol, depth, block), f32)],
         *f_row,
-        second,
+        lower_second,
+        mask_second.reshape(-1),
         sides,
         parent,
     )
@@ -305,9 +311,8 @@
     start, r_high, r_low = call(
         functools.partial(panel_kernel, nrow, ncol),
         [((block, block), f32)] + halves,
-        [],
+        [((block, block), f32)],
         *r_parts,
-        sides,
         parent,
         lower_parent,
         dinv_second,

time: 50.7 us -> 50.5 us (level)
  starting transfers between devices: 19.5 us -> 24.6 us
  waiting for transfers between devices: 14.7 us -> 11.1 us
  blocking collectives: 7.64 us -> 6.09 us
    ppermute x15, starting transfers between devices: 14.5 us -> 22 us  [swap(): return lax.ppermute(x, axis, [(i, i ^ bit) for i in range(size)])]
    ppermute x15, waiting for transfers between devices: 14.7 us -> 11.1 us  [swap(): return lax.ppermute(x, axis, [(i, i ^ bit) for i in range(size)])]
    ppermute x2, starting transfers between devices: 5.04 us -> 2.59 us  [turn(): out.append(lax.ppermute(part, ('row', 'col'), pairs))]
    all_gather x1, blocking collectives: 7.64 us -> 6.09 us  [on_device(): sides = lax.all_gather(lower_parent, 'col', axis=0, tiled=True)]
  transfers between devices with their start and end apart: 17 -> 17, of which waited for: 8 -> 7; matrix products, arithmetic and copies ran while one was open for 0% -> 0% of each run, Pallas kernels for 6% -> 6%
where the time goes in v6:
time: 50.5 us; the launch traced here: 50.3 us
  starting transfers between devices  24.6 us (49%)
  waiting for transfers between devices  11.1 us (22%)
  Pallas kernels  7.61 us (15%)
  blocking collectives  6.09 us (12%)
  between operations  0.83 us (2%)
    ppermute x15, starting transfers between devices, swap(): return lax.ppermute(x, axis, [(i, i ^ bit) for i in range(size)])  22 us
    ppermute x15, waiting for transfers between devices, swap(): return lax.ppermute(x, axis, [(i, i ^ bit) for i in range(size)])  11.1 us
    all_gather x1, blocking collectives, on_device(): sides = lax.all_gather(lower_parent, 'col', axis=0, tiled=True)  6.09 us
    pallas_call x8, Pallas kernels, call(): pl.pallas_call(kernel, out_shape=[jax.ShapeDtypeStruct(shape, dtype) for...  5.23 us
    ppermute x2, starting transfers between devices, turn(): out.append(lax.ppermute(part, ('row', 'col'), pairs))  2.59 us
    pallas_call x1, Pallas kernels, on_device(): pl.pallas_call(mask_kernel, out_shape=jax.ShapeDtypeStruct(wide, f32), in...  2.37 us
  transfers between devices with their start and end apart: 17, of which 7 were waited for; matrix products, arithmetic and copies ran while one was open for 0% of the time, Pallas kernels for 6%

profile of v6, /device:TPU:0, one launch (start us, length us, event | category | flops | bytes accessed | tf_op | source)
XLA Modules:
  0.0 50.3 jit_solution(13995442843572873727)
XLA Ops:
  0.6 2.4 %shard_map.120.refs_0_ = f32[256,128]{1,0:T(8,128)} custom-call(f32[256,128]{1,0:T(8,128)} %values_ref.1, s32[2]{0:T(128)} %bitcast.3), custom_call_target="tpu_custom_call" | custom-call | tf_op jit(solution)/shard_map/pallas_call | solution.py:274
  3.0 5.1 %collective-permute-start = (f32[256,128]{1,0:T(8,128)}, f32[256,128]{1,0:T(8,128)S(1)}, u32[]{:S(2)}, u32[]{:S(2)}) collective-permute-start(f32[256,128]{1,0:T(8,128)} %shard_map.120.refs_0_), channel_id=1, source_target_pairs={{0,12},{4,8},{8,4},{12,0},{1,13},{5,9},{9,5},{13,1},{2,14},{6,10},... | collective-permute-start | bytes 393224 | tf_op jit(solution)/shard_map/ppermute | solution.py:202
  8.2 0.6 %collective-permute-start.2 = (f32[256,128]{1,0:T(8,128)}, f32[256,128]{1,0:T(8,128)S(1)}, u32[]{:S(2)}, u32[]{:S(2)}) collective-permute-start(f32[256,128]{1,0:T(8,128)} %shard_map.120.refs_0_), channel_id=1, source_target_pairs={{0,4},{4,0},{8,12},{12,8},{1,5},{5,1},{9,13},{13,9},{2,6},{6,2},{1... | collective-permute-start | bytes 393224 | tf_op jit(solution)/shard_map/ppermute | solution.py:202
  8.8 6.1 %all_gather.3.refs_6_.after_ref = f32[512,128]{1,0:T(8,128)S(1)} all-gather(f32[128,128]{1,0:T(8,128)} %refs_7_.3), channel_id=1, replica_groups=mesh['pole'=2,'row'=4,'col'=4] {'col'}, dimensions={0}, use_global_device_ids=true | all-gather | bytes 327680 | tf_op jit(solution)/shard_map/all_gather | solution.py:282
  15.0 1.6 %collective-permute-start.9 = (f32[320,256]{1,0:T(8,128)S(1)}, f32[320,256]{1,0:T(8,128)S(1)}, u32[]{:S(2)}, u32[]{:S(2)}) collective-permute-start(f32[320,256]{1,0:T(8,128)S(1)} %shard_map.124.refs_0_), channel_id=1, source_target_pairs={{0,2},{1,3},{2,0},{3,1},{4,6},{5,7},{6,4},{7,5},{8,10},{9,11},{10,... | collective-permute-start | bytes 983048 | tf_op jit(solution)/shard_map/ppermute | solution.py:202
  16.6 2.9 %collective-permute-done.1.refs_2_ = f32[256,128]{1,0:T(8,128)S(1)} collective-permute-done((f32[256,128]{1,0:T(8,128)}, f32[256,128]{1,0:T(8,128)S(1)}, u32[]{:S(2)}, u32[]{:S(2)}) %collective-permute-start.1) | collective-permute-done | bytes 131104 | tf_op jit(solution)/shard_map/ppermute | solution.py:202
  19.5 0.8 %shard_map.121 = (f32[1024,128]{1,0:T(8,128)S(1)}, f32[256,128]{1,0:T(8,128)S(1)}) custom-call(f32[256,128]{1,0:T(8,128)S(1)} %copy-done, f32[256,128]{1,0:T(8,128)S(1)} %collective-permute-done.refs_1_, f32[256,128]{1,0:T(8,128)S(1)} %collective-permute-done.1.refs_2_, f32[256,128]{1,0:T(8,128)S(1)} %collective-permute-done.2.refs_3_, ...), custom_call_target="tpu_custom_call" | custom-call | bytes 2097152 | tf_op jit(solution)/shard_map/pallas_call | solution.py:190
  20.4 0.6 %collective-permute-start.7 = (f32[160,256]{1,0:T(8,128)S(1)}, f32[160,256]{1,0:T(8,128)S(1)}, u32[]{:S(2)}, u32[]{:S(2)}) collective-permute-start(f32[160,256]{1,0:T(8,128)S(1)} %get-tuple-element.31), channel_id=1, source_target_pairs={{0,1},{1,0},{2,3},{3,2},{4,5},{5,4},{6,7},{7,6},{8,9},{9,8},{10,11... | collective-permute-start | bytes 491528 | tf_op jit(solution)/shard_map/ppermute | solution.py:202
  21.0 0.6 %collective-permute-done.4.other_ref = f32[256,128]{1,0:T(8,128)S(1)} collective-permute-done((f32[256,128]{1,0:T(8,128)S(1)}, f32[256,128]{1,0:T(8,128)S(1)}, u32[]{:S(2)}, u32[]{:S(2)}) %collective-permute-start.4) | collective-permute-done | bytes 131104 | tf_op jit(solution)/shard_map/ppermute | solution.py:202
  21.7 1.6 %collective-permute-start.5 = (f32[512,128]{1,0:T(8,128)S(1)}, f32[512,128]{1,0:T(8,128)S(1)}, u32[]{:S(2)}, u32[]{:S(2)}) collective-permute-start(f32[512,128]{1,0:T(8,128)S(1)} %shard_map.123), channel_id=1, source_target_pairs={{0,2},{1,3},{2,0},{3,1},{4,6},{5,7},{6,4},{7,5},{8,10},{9,11},{10,... | collective-permute-start | bytes 786440 | tf_op jit(solution)/shard_map/ppermute | solution.py:202
  23.3 1.9 %collective-permute-start.12 = (f32[512,128]{1,0:T(8,128)S(1)}, f32[512,128]{1,0:T(8,128)S(1)}, u32[]{:S(2)}, u32[]{:S(2)}) collective-permute-start(f32[512,128]{1,0:T(8,128)S(1)} %shard_map.122.after_ref), channel_id=1, source_target_pairs={{2,0},{4,1},{10,2},{12,3},{3,4},{5,5},{11,6},{13,7},{0,8},{6,9},{8... | collective-permute-start | bytes 786440 | tf_op jit(solution)/shard_map/ppermute | solution.py:253
  25.4 0.7 %collective-permute-start.13 = (f32[512,128]{1,0:T(8,128)S(1)}, f32[512,128]{1,0:T(8,128)S(1)}, u32[]{:S(2)}, u32[]{:S(2)}) collective-permute-start(f32[512,128]{1,0:T(8,128)S(1)} %shard_map.122.after_ref), channel_id=1, source_target_pairs={{0,0},{6,1},{8,2},{14,3},{1,4},{7,5},{9,6},{15,7},{2,8},{4,9},{10,... | collective-permute-start | bytes 786440 | tf_op jit(solution)/shard_map/ppermute | solution.py:253
  26.1 3.8 %collective-permute-start.10 = (f32[160,256]{1,0:T(8,128)S(1)}, f32[160,256]{1,0:T(8,128)S(1)}, u32[]{:S(2)}, u32[]{:S(2)}) collective-permute-start(f32[160,256]{1,0:T(8,128)S(1)} %get-tuple-element.29), channel_id=1, source_target_pairs={{0,1},{1,0},{2,3},{3,2},{4,5},{5,4},{6,7},{7,6},{8,9},{9,8},{10,11... | collective-permute-start | bytes 491528 | tf_op jit(solution)/shard_map/ppermute | solution.py:202
  29.9 0.7 %collective-permute-done.5 = f32[512,128]{1,0:T(8,128)S(1)} collective-permute-done((f32[512,128]{1,0:T(8,128)S(1)}, f32[512,128]{1,0:T(8,128)S(1)}, u32[]{:S(2)}, u32[]{:S(2)}) %collective-permute-start.5) | collective-permute-done | bytes 262176 | tf_op jit(solution)/shard_map/ppermute | solution.py:202
  30.6 0.6 %collective-permute-start.3 = (f32[256,128]{1,0:T(8,128)S(1)}, f32[256,128]{1,0:T(8,128)S(1)}, u32[]{:S(2)}, u32[]{:S(2)}) collective-permute-start(f32[256,128]{1,0:T(8,128)S(1)} %get-tuple-element.26), channel_id=1, source_target_pairs={{0,1},{1,0},{2,3},{3,2},{4,5},{5,4},{6,7},{7,6},{8,9},{9,8},{10,11... | collective-permute-start | bytes 393224 | tf_op jit(solution)/shard_map/ppermute | solution.py:202
  31.3 0.7 %collective-permute-done.11.refs_5_ = f32[160,256]{1,0:T(8,128)S(1)} collective-permute-done((f32[160,256]{1,0:T(8,128)S(1)}, f32[160,256]{1,0:T(8,128)S(1)}, u32[]{:S(2)}, u32[]{:S(2)}) %collective-permute-start.11) | collective-permute-done | bytes 163872 | tf_op jit(solution)/shard_map/ppermute | solution.py:202
  32.0 1.0 %shard_map.125 = (f32[128,128]{1,0:T(8,128)S(1)}, bf16[4,256,256]{2,1,0:T(8,128)(2,1)S(1)}, bf16[4,256,256]{2,1,0:T(8,128)(2,1)S(1)}) custom-call(f32[320,256]{1,0:T(8,128)S(1)} %shard_map.124.refs_0_, f32[160,256]{1,0:T(8,128)S(1)} %collective-permute-done.7.refs_1_, f32[160,256]{1,0:T(8,128)S(1)} %collective-permute-done.8.refs_2_, ...), custom_call_target="tpu_custom_call" | custom-call | bytes 2621440 | tf_op jit(solution)/shard_map/pallas_call | solution.py:190
  33.1 1.3 %shard_map.126 = (f32[256,128]{1,0:T(8,128)}, f32[128,128]{1,0:T(8,128)S(1)}) custom-call(f32[256,128]{1,0:T(8,128)S(1)} %get-tuple-element.27.refs_0_, f32[256,128]{1,0:T(8,128)S(1)} %collective-permute-done.3.refs_1_, f32[256,128]{1,0:T(8,128)S(1)} %get-tuple-element.33.refs_2_, f32[256,128]{1,0:T(8,128)S(1)} %collective-permute-done.6.refs_3_, ...), custom_call_target="tpu_custom_call" | custom-call | bytes 2293760 | tf_op jit(solution)/shard_map/pallas_call | solution.py:190
  34.3 1.3 %shard_map.127 = (f32[256,128]{1,0:T(8,128)}, f32[136,128]{1,0:T(8,128)S(1)}) custom-call(f32[512,128]{1,0:T(8,128)S(1)} %collective-permute-done.12.refs_0_, f32[512,128]{1,0:T(8,128)S(1)} %collective-permute-done.13.refs_1_, bf16[4,256,256]{2,1,0:T(8,128)(2,1)S(1)} %get-tuple-element.17.refs_4_.refs_2_, ...), custom_call_target="tpu_custom_call" | custom-call | bytes 2363392 | tf_op jit(solution)/shard_map/pallas_call | solution.py:190
  35.6 4.7 %collective-permute-start.14 = (f32[136,128]{1,0:T(8,128)S(1)}, f32[136,128]{1,0:T(8,128)S(1)}, u32[]{:S(2)}, u32[]{:S(2)}) collective-permute-start(f32[136,128]{1,0:T(8,128)S(1)} %get-tuple-element.22.refs_0_), channel_id=1, source_target_pairs={{0,4},{4,0},{8,12},{12,8},{1,5},{5,1},{9,13},{13,9},{2,6},{6,2},{1... | collective-permute-start | bytes 208904 | tf_op jit(solution)/shard_map/ppermute | solution.py:202
  40.3 3.0 %collective-permute-start.15 = (f32[136,128]{1,0:T(8,128)S(1)}, f32[136,128]{1,0:T(8,128)S(1)}, u32[]{:S(2)}, u32[]{:S(2)}) collective-permute-start(f32[136,128]{1,0:T(8,128)S(1)} %get-tuple-element.22.refs_0_), channel_id=1, source_target_pairs={{0,8},{4,12},{8,0},{12,4},{1,9},{5,13},{9,1},{13,5},{2,10},{6,14},... | collective-permute-start | bytes 208904 | tf_op jit(solution)/shard_map/ppermute | solution.py:202
  43.6 4.6 %collective-permute-done.15.refs_2_ = f32[136,128]{1,0:T(8,128)S(1)} collective-permute-done((f32[136,128]{1,0:T(8,128)S(1)}, f32[136,128]{1,0:T(8,128)S(1)}, u32[]{:S(2)}, u32[]{:S(2)}) %collective-permute-start.15) | collective-permute-done | bytes 69664 | tf_op jit(solution)/shard_map/ppermute | solution.py:202
  48.2 1.4 %collective-permute-done.16.refs_3_ = f32[136,128]{1,0:T(8,128)S(1)} collective-permute-done((f32[136,128]{1,0:T(8,128)S(1)}, f32[136,128]{1,0:T(8,128)S(1)}, u32[]{:S(2)}, u32[]{:S(2)}) %collective-permute-start.16) | collective-permute-done | bytes 69664 | tf_op jit(solution)/shard_map/ppermute | solution.py:202
  49.6 0.8 %shard_map.128 = (f32[128,128]{1,0:T(8,128)}, f32[128,128]{1,0:T(8,128)}) custom-call(f32[128,128]{1,0:T(8,128)S(1)} %copy-done.1, f32[128,128]{1,0:T(8,128)S(1)} %get-tuple-element.20.e_ref, f32[136,128]{1,0:T(8,128)S(1)} %get-tuple-element.22.refs_0_, f32[136,128]{1,0:T(8,128)S(1)} %collective-permute-done.14.refs_1_, ...), custom_call_target="tpu_custom_call" | custom-call | bytes 540672 | tf_op jit(solution)/shard_map/pallas_call | solution.py:190
  (41 shorter events, 0.8 us)
Async XLA Ops:
  0.6 14.3 %copy-start.2 = (f32[256,256]{1,0:T(8,128)S(1)}, f32[256,256]{1,0:T(8,128)}, u32[]{:S(2)}) copy-start(f32[256,256]{1,0:T(8,128)} %root_ref.1) | copy-start | bytes 786436
  3.0 11.9 %copy-start.1 = (f32[128,128]{1,0:T(8,128)S(1)}, f32[128,128]{1,0:T(8,128)}, u32[]{:S(2)}) copy-start(f32[128,128]{1,0:T(8,128)} %dinv_ref.3) | copy-start | bytes 196612
  3.0 13.5 %collective-permute-start = (f32[256,128]{1,0:T(8,128)}, f32[256,128]{1,0:T(8,128)S(1)}, u32[]{:S(2)}, u32[]{:S(2)}) collective-permute-start(f32[256,128]{1,0:T(8,128)} %shard_map.120.refs_0_), channel_id=1, source_target_pairs={{0,12},{4,8},{8,4},{12,0},{1,13},{5,9},{9,5},{13,1},{2,14},{6,10},... | collective-permute-start | bytes 393224 | tf_op jit(solution)/shard_map/ppermute | solution.py:202
  8.2 11.3 %collective-permute-start.1 = (f32[256,128]{1,0:T(8,128)}, f32[256,128]{1,0:T(8,128)S(1)}, u32[]{:S(2)}, u32[]{:S(2)}) collective-permute-start(f32[256,128]{1,0:T(8,128)} %shard_map.120.refs_0_), channel_id=1, source_target_pairs={{0,8},{4,12},{8,0},{12,4},{1,9},{5,13},{9,1},{13,5},{2,10},{6,14},... | collective-permute-start | bytes 393224 | tf_op jit(solution)/shard_map/ppermute | solution.py:202
  8.2 11.3 %collective-permute-start.2 = (f32[256,128]{1,0:T(8,128)}, f32[256,128]{1,0:T(8,128)S(1)}, u32[]{:S(2)}, u32[]{:S(2)}) collective-permute-start(f32[256,128]{1,0:T(8,128)} %shard_map.120.refs_0_), channel_id=1, source_target_pairs={{0,4},{4,0},{8,12},{12,8},{1,5},{5,1},{9,13},{13,9},{2,6},{6,2},{1... | collective-permute-start | bytes 393224 | tf_op jit(solution)/shard_map/ppermute | solution.py:202
  14.9 4.6 %copy-start = (f32[256,128]{1,0:T(8,128)S(1)}, f32[256,128]{1,0:T(8,128)}, u32[]{:S(2)}) copy-start(f32[256,128]{1,0:T(8,128)} %shard_map.120.refs_0_) | copy-start | bytes 393220
  14.9 4.6 %copy-start.4 = (f32[256,128]{1,0:T(8,128)S(1)}, f32[256,128]{1,0:T(8,128)}, u32[]{:S(2)}) copy-start(f32[256,128]{1,0:T(8,128)} %refs_4_.1) | copy-start | bytes 393220
  14.9 4.5 %copy-start.6 = (s32[4]{0:T(128)S(1)}, s32[4]{0:T(128)}, u32[]{:S(2)}) copy-start(s32[4]{0:T(128)} %refs_6_.1) | copy-start | bytes 52
  14.9 4.5 %copy-start.7 = (s32[2,1]{0,1:T(1,128)S(1)}, s32[2,1]{0,1:T(1,128)}, u32[]{:S(2)}) copy-start(s32[2,1]{0,1:T(1,128)} %param.14) | copy-start | bytes 28
  15.0 10.4 %collective-permute-start.9 = (f32[320,256]{1,0:T(8,128)S(1)}, f32[320,256]{1,0:T(8,128)S(1)}, u32[]{:S(2)}, u32[]{:S(2)}) collective-permute-start(f32[320,256]{1,0:T(8,128)S(1)} %shard_map.124.refs_0_), channel_id=1, source_target_pairs={{0,2},{1,3},{2,0},{3,1},{4,6},{5,7},{6,4},{7,5},{8,10},{9,11},{10,... | collective-permute-start | bytes 983048 | tf_op jit(solution)/shard_map/ppermute | solution.py:202
  20.3 1.4 %collective-permute-start.4 = (f32[256,128]{1,0:T(8,128)S(1)}, f32[256,128]{1,0:T(8,128)S(1)}, u32[]{:S(2)}, u32[]{:S(2)}) collective-permute-start(f32[256,128]{1,0:T(8,128)S(1)} %get-tuple-element.16.own_ref), channel_id=1, source_target_pairs={{0,1},{1,0},{2,3},{3,2},{4,5},{5,4},{6,7},{7,6},{8,9},{9,8},{10,11... | collective-permute-start | bytes 393224 | tf_op jit(solution)/shard_map/ppermute | solution.py:202
  20.4 5.7 %collective-permute-start.7 = (f32[160,256]{1,0:T(8,128)S(1)}, f32[160,256]{1,0:T(8,128)S(1)}, u32[]{:S(2)}, u32[]{:S(2)}) collective-permute-start(f32[160,256]{1,0:T(8,128)S(1)} %get-tuple-element.31), channel_id=1, source_target_pairs={{0,1},{1,0},{2,3},{3,2},{4,5},{5,4},{6,7},{7,6},{8,9},{9,8},{10,11... | collective-permute-start | bytes 491528 | tf_op jit(solution)/shard_map/ppermute | solution.py:202
  20.9 9.7 %collective-permute-start.8 = (f32[160,256]{1,0:T(8,128)S(1)}, f32[160,256]{1,0:T(8,128)S(1)}, u32[]{:S(2)}, u32[]{:S(2)}) collective-permute-start(f32[160,256]{1,0:T(8,128)S(1)} %get-tuple-element.30), channel_id=1, source_target_pairs={{0,1},{1,0},{2,3},{3,2},{4,5},{5,4},{6,7},{7,6},{8,9},{9,8},{10,11... | collective-permute-start | bytes 491528 | tf_op jit(solution)/shard_map/ppermute | solution.py:202
  21.7 8.9 %collective-permute-start.5 = (f32[512,128]{1,0:T(8,128)S(1)}, f32[512,128]{1,0:T(8,128)S(1)}, u32[]{:S(2)}, u32[]{:S(2)}) collective-permute-start(f32[512,128]{1,0:T(8,128)S(1)} %shard_map.123), channel_id=1, source_target_pairs={{0,2},{1,3},{2,0},{3,1},{4,6},{5,7},{6,4},{7,5},{8,10},{9,11},{10,... | collective-permute-start | bytes 786440 | tf_op jit(solution)/shard_map/ppermute | solution.py:202
  23.3 11.0 %collective-permute-start.12 = (f32[512,128]{1,0:T(8,128)S(1)}, f32[512,128]{1,0:T(8,128)S(1)}, u32[]{:S(2)}, u32[]{:S(2)}) collective-permute-start(f32[512,128]{1,0:T(8,128)S(1)} %shard_map.122.after_ref), channel_id=1, source_target_pairs={{2,0},{4,1},{10,2},{12,3},{3,4},{5,5},{11,6},{13,7},{0,8},{6,9},{8... | collective-permute-start | bytes 786440 | tf_op jit(solution)/shard_map/ppermute | solution.py:253
  25.4 9.0 %collective-permute-start.13 = (f32[512,128]{1,0:T(8,128)S(1)}, f32[512,128]{1,0:T(8,128)S(1)}, u32[]{:S(2)}, u32[]{:S(2)}) collective-permute-start(f32[512,128]{1,0:T(8,128)S(1)} %shard_map.122.after_ref), channel_id=1, source_target_pairs={{0,0},{6,1},{8,2},{14,3},{1,4},{7,5},{9,6},{15,7},{2,8},{4,9},{10,... | collective-permute-start | bytes 786440 | tf_op jit(solution)/shard_map/ppermute | solution.py:253
  26.1 5.1 %collective-permute-start.10 = (f32[160,256]{1,0:T(8,128)S(1)}, f32[160,256]{1,0:T(8,128)S(1)}, u32[]{:S(2)}, u32[]{:S(2)}) collective-permute-start(f32[160,256]{1,0:T(8,128)S(1)} %get-tuple-element.29), channel_id=1, source_target_pairs={{0,1},{1,0},{2,3},{3,2},{4,5},{5,4},{6,7},{7,6},{8,9},{9,8},{10,11... | collective-permute-start | bytes 491528 | tf_op jit(solution)/shard_map/ppermute | solution.py:202
  30.6 1.4 %copy-start.5 = (f32[128,128]{1,0:T(8,128)S(1)}, f32[128,128]{1,0:T(8,128)}, u32[]{:S(2)}) copy-start(f32[128,128]{1,0:T(8,128)} %refs_8_.1) | copy-start | bytes 196612
  30.6 1.4 %collective-permute-start.11 = (f32[160,256]{1,0:T(8,128)S(1)}, f32[160,256]{1,0:T(8,128)S(1)}, u32[]{:S(2)}, u32[]{:S(2)}) collective-permute-start(f32[160,256]{1,0:T(8,128)S(1)} %get-tuple-element.28), channel_id=1, source_target_pairs={{0,1},{1,0},{2,3},{3,2},{4,5},{5,4},{6,7},{7,6},{8,9},{9,8},{10,11... | collective-permute-start | bytes 491528 | tf_op jit(solution)/shard_map/ppermute | solution.py:202
  30.6 2.4 %collective-permute-start.3 = (f32[256,128]{1,0:T(8,128)S(1)}, f32[256,128]{1,0:T(8,128)S(1)}, u32[]{:S(2)}, u32[]{:S(2)}) collective-permute-start(f32[256,128]{1,0:T(8,128)S(1)} %get-tuple-element.26), channel_id=1, source_target_pairs={{0,1},{1,0},{2,3},{3,2},{4,5},{5,4},{6,7},{7,6},{8,9},{9,8},{10,11... | collective-permute-start | bytes 393224 | tf_op jit(solution)/shard_map/ppermute | solution.py:202
  31.2 1.9 %collective-permute-start.6 = (f32[256,128]{1,0:T(8,128)S(1)}, f32[256,128]{1,0:T(8,128)S(1)}, u32[]{:S(2)}, u32[]{:S(2)}) collective-permute-start(f32[256,128]{1,0:T(8,128)S(1)} %get-tuple-element.32), channel_id=1, source_target_pairs={{0,1},{1,0},{2,3},{3,2},{4,5},{5,4},{6,7},{7,6},{8,9},{9,8},{10,11... | collective-permute-start | bytes 393224 | tf_op jit(solution)/shard_map/ppermute | solution.py:202
  35.6 8.0 %collective-permute-start.14 = (f32[136,128]{1,0:T(8,128)S(1)}, f32[136,128]{1,0:T(8,128)S(1)}, u32[]{:S(2)}, u32[]{:S(2)}) collective-permute-start(f32[136,128]{1,0:T(8,128)S(1)} %get-tuple-element.22.refs_0_), channel_id=1, source_target_pairs={{0,4},{4,0},{8,12},{12,8},{1,5},{5,1},{9,13},{13,9},{2,6},{6,2},{1... | collective-permute-start | bytes 208904 | tf_op jit(solution)/shard_map/ppermute | solution.py:202
  40.3 7.8 %collective-permute-start.15 = (f32[136,128]{1,0:T(8,128)S(1)}, f32[136,128]{1,0:T(8,128)S(1)}, u32[]{:S(2)}, u32[]{:S(2)}) collective-permute-start(f32[136,128]{1,0:T(8,128)S(1)} %get-tuple-element.22.refs_0_), channel_id=1, source_target_pairs={{0,8},{4,12},{8,0},{12,4},{1,9},{5,13},{9,1},{13,5},{2,10},{6,14},... | collective-permute-start | bytes 208904 | tf_op jit(solution)/shard_map/ppermute | solution.py:202
  43.4 6.2 %collective-permute-start.16 = (f32[136,128]{1,0:T(8,128)S(1)}, f32[136,128]{1,0:T(8,128)S(1)}, u32[]{:S(2)}, u32[]{:S(2)}) collective-permute-start(f32[136,128]{1,0:T(8,128)S(1)} %get-tuple-element.22.refs_0_), channel_id=1, source_target_pairs={{0,12},{4,8},{8,4},{12,0},{1,13},{5,9},{9,5},{13,1},{2,14},{6,10},... | collective-permute-start | bytes 208904 | tf_op jit(solution)/shard_map/ppermute | solution.py:202
  (1 other events, 1.4 us)

commit v7 on v6

--- a/solution.py
+++ b/solution.py
@@ -47,13 +47,6 @@
             cols = slice(j * BLOCK, (j + 1) * BLOCK)
             factor = pattern_ref[i * across + j].astype(jnp.float32)
             out_ref[rows, cols] = values_ref[rows, cols] * factor
-
-
-def mask_kernel(values_ref, pattern_ref, out_ref, raw_ref, sem):
-    copy = pltpu.make_async_copy(values_ref, raw_ref, sem)
-    copy.start()
-    copy.wait()
-    apply_mask(raw_ref, pattern_ref, out_ref)
 
 
 def child_kernel(nrow, ncol, *refs):
@@ -114,44 +107,55 @@
     e_ref[...] = dinv_ref[...] + dot_split(lower, split(product), TN)
 
 
-def spread(nrow, ncol, refs, high_ref, low_ref):
+def spread(nrow, ncol, refs, w_ref):
     base, own, _ = slots(nrow, ncol)
     depth = refs[0].shape[0] // 2
+    block = w_ref.shape[2] // 2
     for t in range(ncol):
         slot = base ^ t
         part = refs[-1 - t // 2][t % 2 * depth : (t % 2 + 1) * depth]
-        high_ref[slot], low_ref[slot] = split(part)
+        w_ref[slot, :, :block], w_ref[slot, :, block:] = split(part)
     return own, depth
 
 
-def products(nrow, ncol, own, depth, r_refs, w_refs):
-    total = None
+def products(nrow, ncol, own, depth, r_refs, w_ref):
+    block = w_ref.shape[2] // 2
+
+    def one(left, right, dims):
+        return lax.dot_general(left, right, (dims, ((), ())), preferred_element_type=jnp.float32)
+
+    wide, rest = None, None
     for j in range(ncol):
-        term = dot_split((r_refs[0][j], r_refs[1][j]), (w_refs[0][j], w_refs[1][j]), NN)
-        total = term if total is None else total + term
+        term = one(r_refs[0][j], w_ref[j], NN)
+        wide = term if wide is None else wide + term
+        term = one(r_refs[1][j], w_ref[j, :, :block], NN)
+        rest = term if rest is None else rest + term
+    total = wide[:, :block] + (wide[:, block:] + rest)
     diag = None
     for i, slot in enumerate(own):
-        part = split(total[i * depth : (i + 1) * depth])
-        term = dot_split((w_refs[0][slot], w_refs[1][slot]), part, TN)
+        high, low = split(total[i * depth : (i + 1) * depth])
+        tall = one(w_ref[slot], high, TN)
+        term = tall[:block] + (tall[block:] + one(w_ref[slot, :, :block], low, TN))
         diag = term if diag is None else diag + term
     return total, diag
 
 
 def first_kernel(nrow, ncol, *refs):
-    rh_ref, rl_ref, x_ref, d_ref, fh_ref, fl_ref = refs[ncol:]
+    rh_ref, rl_ref, x_ref, d_ref, w_ref = refs[ncol:]
+    block = x_ref.shape[1]
     own = slots(nrow, ncol)[1]
     depth = refs[0].shape[0]
     for j in range(ncol):
-        fh_ref[j], fl_ref[j] = split(refs[j][...])
-    total, diag = products(nrow, ncol, own, depth, (rh_ref, rl_ref), (fh_ref, fl_ref))
+        w_ref[j, :, :block], w_ref[j, :, block:] = split(refs[j][...])
+    total, diag = products(nrow, ncol, own, depth, (rh_ref, rl_ref), w_ref)
     x_ref[...] = -total
     d_ref[...] = diag
 
 
 def second_kernel(nrow, ncol, *refs):
-    rh_ref, rl_ref, d_ref, y_ref, m_ref, sh_ref, sl_ref = refs[ncol // 2 :]
-    own, depth = spread(nrow, ncol, refs[: ncol // 2], sh_ref, sl_ref)
-    total, diag = products(nrow, ncol, own, depth, (rh_ref, rl_ref), (sh_ref, sl_ref))
+    rh_ref, rl_ref, d_ref, y_ref, m_ref, w_ref = refs[ncol // 2 :]
+    own, depth = spread(nrow, ncol, refs[: ncol // 2], w_ref)
+    total, diag = products(nrow, ncol, own, depth, (rh_ref, rl_ref), w_ref)
     y_ref[...] = -total
     block = diag.shape[0]
     across = lax.broadcasted_iota(jnp.int32, diag.shape, 1)
@@ -271,13 +275,9 @@
     block = dinv_first.shape[0]
     rows, depth = inverse_root.shape
     wide = lower_first.shape
-    first = pl.pallas_call(
-        mask_kernel,
-        out_shape=jax.ShapeDtypeStruct(wide, f32),
-        in_specs=[pl.BlockSpec(memory_space=pl.ANY), SMEM],
-        out_specs=VMEM,
-        scratch_shapes=[pltpu.VMEM(wide, f32), pltpu.SemaphoreType.DMA],
-    )(lower_first, mask_first.reshape(-1))
+    tiles = mask_first.shape
+    cells = lower_first.reshape(tiles[0], BLOCK, tiles[1], BLOCK)
+    first = (cells * mask_first.astype(f32)[:, None, :, None]).reshape(wide)
     f_row = [first] + [swap(first, "row", nrow, m) for m in range(nrow - 1, 0, -1)]
     sides = lax.all_gather(lower_parent, "col", axis=0, tiled=True)
     tall = (rows + block * block // depth, depth)
@@ -307,7 +307,7 @@
             f_parts[j ^ bit] = swap(after(sent, pair) if 2 * bit == ncol else sent, "col", ncol, bit)
         bit //= 2
     halves = [((ncol, rows, depth), bf16)] * 2
-    pieces = [((ncol, depth, block), bf16)] * 2
+    pieces = [((ncol, depth, 2 * block), bf16)]
     start, r_high, r_low = call(
         functools.partial(panel_kernel, nrow, ncol),
         [((block, block), f32)] + halves,

time: 50.5 us -> 49.7 us (0.984)
  Pallas kernels: 7.61 us -> 5 us
  other arithmetic: 0 us -> 1.73 us
    pallas_call x1 -> x0, Pallas kernels: 2.37 us -> none  [on_device(): pl.pallas_call(mask_kernel, out_shape=jax.ShapeDtypeStruct(wide, f32), in...]
    mul x0 -> x2, other arithmetic: none -> 1.73 us  [on_device(): first = (cells * mask_first.astype(f32)[:, None, :, None]).reshape(wide)]
where the time goes in v7:
time: 49.7 us; the launch traced here: 49.4 us
  starting transfers between devices  24.6 us (49%)
  waiting for transfers between devices  11.2 us (23%)
  blocking collectives  5.88 us (12%)
  Pallas kernels  5 us (10%)
  other arithmetic  1.73 us (3%)
  between operations  0.82 us (2%)
    ppermute x15, starting transfers between devices, swap(): return lax.ppermute(x, axis, [(i, i ^ bit) for i in range(size)])  22 us
    ppermute x15, waiting for transfers between devices, swap(): return lax.ppermute(x, axis, [(i, i ^ bit) for i in range(size)])  11.2 us
    all_gather x1, blocking collectives, on_device(): sides = lax.all_gather(lower_parent, 'col', axis=0, tiled=True)  5.88 us
    pallas_call x8, Pallas kernels, call(): pl.pallas_call(kernel, out_shape=[jax.ShapeDtypeStruct(shape, dtype) for...  5 us
    ppermute x2, starting transfers between devices, turn(): out.append(lax.ppermute(part, ('row', 'col'), pairs))  2.59 us
    mul x2, other arithmetic, on_device(): first = (cells * mask_first.astype(f32)[:, None, :, None]).reshape(wide)  1.73 us
  transfers between devices with their start and end apart: 17, of which 7 were waited for; matrix products, arithmetic and copies ran while one was open for 0% of the time, Pallas kernels for 6%

profile of v7, /device:TPU:0, one launch (start us, length us, event | category | flops | bytes accessed | tf_op | source)
XLA Modules:
  0.0 49.4 jit_solution(11316005633918689461)
XLA Ops:
  0.6 0.7 %convert_bitcast_fusion = f32[2]{0:T(128)S(1)} fusion(s32[2,1]{0,1:T(1,128)} %param.11), kind=kLoop, calls=%fused_computation.1 | loop fusion | flops 2 | bytes 16 | tf_op jit(solution)/shard_map/mul | solution.py:280
  1.4 1.0 %broadcast_multiply_fusion.refs_0_ = f32[256,128]{1,0:T(8,128)S(1)} fusion(f32[256,128]{1,0:T(8,128)} %param.10, f32[256]{0:T(256)S(1)} %broadcast_bitcast_fusion), kind=kLoop, calls=%fused_computation | loop fusion | flops 32768 | bytes 263168 | tf_op jit(solution)/shard_map/mul | solution.py:280
  2.5 5.1 %collective-permute-start = (f32[256,128]{1,0:T(8,128)S(1)}, f32[256,128]{1,0:T(8,128)S(1)}, u32[]{:S(2)}, u32[]{:S(2)}) collective-permute-start(f32[256,128]{1,0:T(8,128)S(1)} %broadcast_multiply_fusion.refs_0_), channel_id=1, source_target_pairs={{0,12},{4,8},{8,4},{12,0},{1,13},{5,9},{9,5},{13,1},{2,14},{6,10},... | collective-permute-start | bytes 393224 | tf_op jit(solution)/shard_map/ppermute | solution.py:206
  7.6 0.6 %collective-permute-start.2 = (f32[256,128]{1,0:T(8,128)S(1)}, f32[256,128]{1,0:T(8,128)S(1)}, u32[]{:S(2)}, u32[]{:S(2)}) collective-permute-start(f32[256,128]{1,0:T(8,128)S(1)} %broadcast_multiply_fusion.refs_0_), channel_id=1, source_target_pairs={{0,4},{4,0},{8,12},{12,8},{1,5},{5,1},{9,13},{13,9},{2,6},{6,2},{1... | collective-permute-start | bytes 393224 | tf_op jit(solution)/shard_map/ppermute | solution.py:206
  8.2 5.9 %all_gather.3.refs_6_.after_ref = f32[512,128]{1,0:T(8,128)S(1)} all-gather(f32[128,128]{1,0:T(8,128)S(1)} %copy-done.2), channel_id=1, replica_groups=mesh['pole'=2,'row'=4,'col'=4] {'col'}, dimensions={0}, use_global_device_ids=true | all-gather | bytes 327680 | tf_op jit(solution)/shard_map/all_gather | solution.py:282
  14.2 1.6 %collective-permute-start.9 = (f32[320,256]{1,0:T(8,128)S(1)}, f32[320,256]{1,0:T(8,128)S(1)}, u32[]{:S(2)}, u32[]{:S(2)}) collective-permute-start(f32[320,256]{1,0:T(8,128)S(1)} %shard_map.123.refs_0_), channel_id=1, source_target_pairs={{0,2},{1,3},{2,0},{3,1},{4,6},{5,7},{6,4},{7,5},{8,10},{9,11},{10,... | collective-permute-start | bytes 983048 | tf_op jit(solution)/shard_map/ppermute | solution.py:206
  15.8 2.9 %collective-permute-done.1.refs_2_ = f32[256,128]{1,0:T(8,128)S(1)} collective-permute-done((f32[256,128]{1,0:T(8,128)S(1)}, f32[256,128]{1,0:T(8,128)S(1)}, u32[]{:S(2)}, u32[]{:S(2)}) %collective-permute-start.1) | collective-permute-done | bytes 131104 | tf_op jit(solution)/shard_map/ppermute | solution.py:206
  18.7 0.8 %shard_map.120 = (f32[1024,128]{1,0:T(8,128)S(1)}, f32[256,128]{1,0:T(8,128)S(1)}) custom-call(f32[256,128]{1,0:T(8,128)S(1)} %broadcast_multiply_fusion.refs_0_, f32[256,128]{1,0:T(8,128)S(1)} %collective-permute-done.refs_1_, f32[256,128]{1,0:T(8,128)S(1)} %collective-permute-done.1.refs_2_, f32[256,128]{1,0:T(8,128)S(1)} %collective-permute-done.2.refs_3_, ...), custom_call_target="tpu_custom_call" | custom-call | bytes 2097152 | tf_op jit(solution)/shard_map/pallas_call | solution.py:194
  20.3 0.6 %collective-permute-done.4.other_ref = f32[256,128]{1,0:T(8,128)S(1)} collective-permute-done((f32[256,128]{1,0:T(8,128)S(1)}, f32[256,128]{1,0:T(8,128)S(1)}, u32[]{:S(2)}, u32[]{:S(2)}) %collective-permute-start.4) | collective-permute-done | bytes 131104 | tf_op jit(solution)/shard_map/ppermute | solution.py:206
  20.9 1.6 %collective-permute-start.5 = (f32[512,128]{1,0:T(8,128)S(1)}, f32[512,128]{1,0:T(8,128)S(1)}, u32[]{:S(2)}, u32[]{:S(2)}) collective-permute-start(f32[512,128]{1,0:T(8,128)S(1)} %shard_map.122), channel_id=1, source_target_pairs={{0,2},{1,3},{2,0},{3,1},{4,6},{5,7},{6,4},{7,5},{8,10},{9,11},{10,... | collective-permute-start | bytes 786440 | tf_op jit(solution)/shard_map/ppermute | solution.py:206
  22.5 1.9 %collective-permute-start.12 = (f32[512,128]{1,0:T(8,128)S(1)}, f32[512,128]{1,0:T(8,128)S(1)}, u32[]{:S(2)}, u32[]{:S(2)}) collective-permute-start(f32[512,128]{1,0:T(8,128)S(1)} %shard_map.121.after_ref), channel_id=1, source_target_pairs={{2,0},{4,1},{10,2},{12,3},{3,4},{5,5},{11,6},{13,7},{0,8},{6,9},{8... | collective-permute-start | bytes 786440 | tf_op jit(solution)/shard_map/ppermute | solution.py:257
  24.5 0.7 %collective-permute-start.13 = (f32[512,128]{1,0:T(8,128)S(1)}, f32[512,128]{1,0:T(8,128)S(1)}, u32[]{:S(2)}, u32[]{:S(2)}) collective-permute-start(f32[512,128]{1,0:T(8,128)S(1)} %shard_map.121.after_ref), channel_id=1, source_target_pairs={{0,0},{6,1},{8,2},{14,3},{1,4},{7,5},{9,6},{15,7},{2,8},{4,9},{10,... | collective-permute-start | bytes 786440 | tf_op jit(solution)/shard_map/ppermute | solution.py:257
  25.3 3.8 %collective-permute-start.10 = (f32[160,256]{1,0:T(8,128)S(1)}, f32[160,256]{1,0:T(8,128)S(1)}, u32[]{:S(2)}, u32[]{:S(2)}) collective-permute-start(f32[160,256]{1,0:T(8,128)S(1)} %get-tuple-element.29), channel_id=1, source_target_pairs={{0,1},{1,0},{2,3},{3,2},{4,5},{5,4},{6,7},{7,6},{8,9},{9,8},{10,11... | collective-permute-start | bytes 491528 | tf_op jit(solution)/shard_map/ppermute | solution.py:206
  29.1 0.7 %collective-permute-done.5 = f32[512,128]{1,0:T(8,128)S(1)} collective-permute-done((f32[512,128]{1,0:T(8,128)S(1)}, f32[512,128]{1,0:T(8,128)S(1)}, u32[]{:S(2)}, u32[]{:S(2)}) %collective-permute-start.5) | collective-permute-done | bytes 262176 | tf_op jit(solution)/shard_map/ppermute | solution.py:206
  29.8 0.6 %collective-permute-start.3 = (f32[256,128]{1,0:T(8,128)S(1)}, f32[256,128]{1,0:T(8,128)S(1)}, u32[]{:S(2)}, u32[]{:S(2)}) collective-permute-start(f32[256,128]{1,0:T(8,128)S(1)} %get-tuple-element.26), channel_id=1, source_target_pairs={{0,1},{1,0},{2,3},{3,2},{4,5},{5,4},{6,7},{7,6},{8,9},{9,8},{10,11... | collective-permute-start | bytes 393224 | tf_op jit(solution)/shard_map/ppermute | solution.py:206
  30.5 0.7 %collective-permute-done.11.refs_5_ = f32[160,256]{1,0:T(8,128)S(1)} collective-permute-done((f32[160,256]{1,0:T(8,128)S(1)}, f32[160,256]{1,0:T(8,128)S(1)}, u32[]{:S(2)}, u32[]{:S(2)}) %collective-permute-start.11) | collective-permute-done | bytes 163872 | tf_op jit(solution)/shard_map/ppermute | solution.py:206
  31.2 1.0 %shard_map.124 = (f32[128,128]{1,0:T(8,128)S(1)}, bf16[4,256,256]{2,1,0:T(8,128)(2,1)S(1)}, bf16[4,256,256]{2,1,0:T(8,128)(2,1)S(1)}) custom-call(f32[320,256]{1,0:T(8,128)S(1)} %shard_map.123.refs_0_, f32[160,256]{1,0:T(8,128)S(1)} %collective-permute-done.7.refs_1_, f32[160,256]{1,0:T(8,128)S(1)} %collective-permute-done.8.refs_2_, ...), custom_call_target="tpu_custom_call" | custom-call | bytes 2621440 | tf_op jit(solution)/shard_map/pallas_call | solution.py:194
  32.3 1.1 %shard_map.125 = (f32[256,128]{1,0:T(8,128)}, f32[128,128]{1,0:T(8,128)S(1)}) custom-call(f32[256,128]{1,0:T(8,128)S(1)} %get-tuple-element.27.refs_0_, f32[256,128]{1,0:T(8,128)S(1)} %collective-permute-done.3.refs_1_, f32[256,128]{1,0:T(8,128)S(1)} %get-tuple-element.33.refs_2_, f32[256,128]{1,0:T(8,128)S(1)} %collective-permute-done.6.refs_3_, ...), custom_call_target="tpu_custom_call" | custom-call | bytes 2293760 | tf_op jit(solution)/shard_map/pallas_call | solution.py:194
  33.4 1.2 %shard_map.126 = (f32[256,128]{1,0:T(8,128)}, f32[136,128]{1,0:T(8,128)S(1)}) custom-call(f32[512,128]{1,0:T(8,128)S(1)} %collective-permute-done.12.refs_0_, f32[512,128]{1,0:T(8,128)S(1)} %collective-permute-done.13.refs_1_, bf16[4,256,256]{2,1,0:T(8,128)(2,1)S(1)} %get-tuple-element.17.refs_4_.refs_2_, ...), custom_call_target="tpu_custom_call" | custom-call | bytes 2363392 | tf_op jit(solution)/shard_map/pallas_call | solution.py:194
  34.6 4.8 %collective-permute-start.14 = (f32[136,128]{1,0:T(8,128)S(1)}, f32[136,128]{1,0:T(8,128)S(1)}, u32[]{:S(2)}, u32[]{:S(2)}) collective-permute-start(f32[136,128]{1,0:T(8,128)S(1)} %get-tuple-element.22.refs_0_), channel_id=1, source_target_pairs={{0,4},{4,0},{8,12},{12,8},{1,5},{5,1},{9,13},{13,9},{2,6},{6,2},{1... | collective-permute-start | bytes 208904 | tf_op jit(solution)/shard_map/ppermute | solution.py:206
  39.4 3.0 %collective-permute-start.15 = (f32[136,128]{1,0:T(8,128)S(1)}, f32[136,128]{1,0:T(8,128)S(1)}, u32[]{:S(2)}, u32[]{:S(2)}) collective-permute-start(f32[136,128]{1,0:T(8,128)S(1)} %get-tuple-element.22.refs_0_), channel_id=1, source_target_pairs={{0,8},{4,12},{8,0},{12,4},{1,9},{5,13},{9,1},{13,5},{2,10},{6,14},... | collective-permute-start | bytes 208904 | tf_op jit(solution)/shard_map/ppermute | solution.py:206
  42.6 4.8 %collective-permute-done.15.refs_2_ = f32[136,128]{1,0:T(8,128)S(1)} collective-permute-done((f32[136,128]{1,0:T(8,128)S(1)}, f32[136,128]{1,0:T(8,128)S(1)}, u32[]{:S(2)}, u32[]{:S(2)}) %collective-permute-start.15) | collective-permute-done | bytes 69664 | tf_op jit(solution)/shard_map/ppermute | solution.py:206
  47.3 1.4 %collective-permute-done.16.refs_3_ = f32[136,128]{1,0:T(8,128)S(1)} collective-permute-done((f32[136,128]{1,0:T(8,128)S(1)}, f32[136,128]{1,0:T(8,128)S(1)}, u32[]{:S(2)}, u32[]{:S(2)}) %collective-permute-start.16) | collective-permute-done | bytes 69664 | tf_op jit(solution)/shard_map/ppermute | solution.py:206
  48.7 0.8 %shard_map.127 = (f32[128,128]{1,0:T(8,128)}, f32[128,128]{1,0:T(8,128)}) custom-call(f32[128,128]{1,0:T(8,128)S(1)} %copy-done, f32[128,128]{1,0:T(8,128)S(1)} %get-tuple-element.20.e_ref, f32[136,128]{1,0:T(8,128)S(1)} %get-tuple-element.22.refs_0_, f32[136,128]{1,0:T(8,128)S(1)} %collective-permute-done.14.refs_1_, ...), custom_call_target="tpu_custom_call" | custom-call | bytes 540672 | tf_op jit(solution)/shard_map/pallas_call | solution.py:194
  (41 shorter events, 1.3 us)
Async XLA Ops:
  0.6 7.6 %copy-start.2 = (f32[128,128]{1,0:T(8,128)S(1)}, f32[128,128]{1,0:T(8,128)}, u32[]{:S(2)}) copy-start(f32[128,128]{1,0:T(8,128)} %refs_7_.3) | copy-start | bytes 196612
  1.4 12.7 %copy-start.1 = (f32[256,256]{1,0:T(8,128)S(1)}, f32[256,256]{1,0:T(8,128)}, u32[]{:S(2)}) copy-start(f32[256,256]{1,0:T(8,128)} %root_ref.1) | copy-start | bytes 786436
  2.5 11.7 %copy-start = (f32[128,128]{1,0:T(8,128)S(1)}, f32[128,128]{1,0:T(8,128)}, u32[]{:S(2)}) copy-start(f32[128,128]{1,0:T(8,128)} %dinv_ref.3) | copy-start | bytes 196612
  2.5 13.3 %collective-permute-start = (f32[256,128]{1,0:T(8,128)S(1)}, f32[256,128]{1,0:T(8,128)S(1)}, u32[]{:S(2)}, u32[]{:S(2)}) collective-permute-start(f32[256,128]{1,0:T(8,128)S(1)} %broadcast_multiply_fusion.refs_0_), channel_id=1, source_target_pairs={{0,12},{4,8},{8,4},{12,0},{1,13},{5,9},{9,5},{13,1},{2,14},{6,10},... | collective-permute-start | bytes 393224 | tf_op jit(solution)/shard_map/ppermute | solution.py:206
  7.6 11.1 %collective-permute-start.1 = (f32[256,128]{1,0:T(8,128)S(1)}, f32[256,128]{1,0:T(8,128)S(1)}, u32[]{:S(2)}, u32[]{:S(2)}) collective-permute-start(f32[256,128]{1,0:T(8,128)S(1)} %broadcast_multiply_fusion.refs_0_), channel_id=1, source_target_pairs={{0,8},{4,12},{8,0},{12,4},{1,9},{5,13},{9,1},{13,5},{2,10},{6,14},... | collective-permute-start | bytes 393224 | tf_op jit(solution)/shard_map/ppermute | solution.py:206
  7.6 11.1 %collective-permute-start.2 = (f32[256,128]{1,0:T(8,128)S(1)}, f32[256,128]{1,0:T(8,128)S(1)}, u32[]{:S(2)}, u32[]{:S(2)}) collective-permute-start(f32[256,128]{1,0:T(8,128)S(1)} %broadcast_multiply_fusion.refs_0_), channel_id=1, source_target_pairs={{0,4},{4,0},{8,12},{12,8},{1,5},{5,1},{9,13},{13,9},{2,6},{6,2},{1... | collective-permute-start | bytes 393224 | tf_op jit(solution)/shard_map/ppermute | solution.py:206
  14.1 4.6 %copy-start.3 = (f32[256,128]{1,0:T(8,128)S(1)}, f32[256,128]{1,0:T(8,128)}, u32[]{:S(2)}) copy-start(f32[256,128]{1,0:T(8,128)} %refs_4_.1) | copy-start | bytes 393220
  14.1 4.5 %copy-start.5 = (s32[4]{0:T(128)S(1)}, s32[4]{0:T(128)}, u32[]{:S(2)}) copy-start(s32[4]{0:T(128)} %refs_6_.1) | copy-start | bytes 52
  14.1 4.5 %copy-start.6 = (s32[2,1]{0,1:T(1,128)S(1)}, s32[2,1]{0,1:T(1,128)}, u32[]{:S(2)}) copy-start(s32[2,1]{0,1:T(1,128)} %param.14) | copy-start | bytes 28
  14.2 10.4 %collective-permute-start.9 = (f32[320,256]{1,0:T(8,128)S(1)}, f32[320,256]{1,0:T(8,128)S(1)}, u32[]{:S(2)}, u32[]{:S(2)}) collective-permute-start(f32[320,256]{1,0:T(8,128)S(1)} %shard_map.123.refs_0_), channel_id=1, source_target_pairs={{0,2},{1,3},{2,0},{3,1},{4,6},{5,7},{6,4},{7,5},{8,10},{9,11},{10,... | collective-permute-start | bytes 983048 | tf_op jit(solution)/shard_map/ppermute | solution.py:206
  19.5 1.4 %collective-permute-start.4 = (f32[256,128]{1,0:T(8,128)S(1)}, f32[256,128]{1,0:T(8,128)S(1)}, u32[]{:S(2)}, u32[]{:S(2)}) collective-permute-start(f32[256,128]{1,0:T(8,128)S(1)} %get-tuple-element.16.own_ref), channel_id=1, source_target_pairs={{0,1},{1,0},{2,3},{3,2},{4,5},{5,4},{6,7},{7,6},{8,9},{9,8},{10,11... | collective-permute-start | bytes 393224 | tf_op jit(solution)/shard_map/ppermute | solution.py:206
  19.6 5.7 %collective-permute-start.7 = (f32[160,256]{1,0:T(8,128)S(1)}, f32[160,256]{1,0:T(8,128)S(1)}, u32[]{:S(2)}, u32[]{:S(2)}) collective-permute-start(f32[160,256]{1,0:T(8,128)S(1)} %get-tuple-element.31), channel_id=1, source_target_pairs={{0,1},{1,0},{2,3},{3,2},{4,5},{5,4},{6,7},{7,6},{8,9},{9,8},{10,11... | collective-permute-start | bytes 491528 | tf_op jit(solution)/shard_map/ppermute | solution.py:206
  20.2 9.7 %collective-permute-start.8 = (f32[160,256]{1,0:T(8,128)S(1)}, f32[160,256]{1,0:T(8,128)S(1)}, u32[]{:S(2)}, u32[]{:S(2)}) collective-permute-start(f32[160,256]{1,0:T(8,128)S(1)} %get-tuple-element.30), channel_id=1, source_target_pairs={{0,1},{1,0},{2,3},{3,2},{4,5},{5,4},{6,7},{7,6},{8,9},{9,8},{10,11... | collective-permute-start | bytes 491528 | tf_op jit(solution)/shard_map/ppermute | solution.py:206
  20.9 8.9 %collective-permute-start.5 = (f32[512,128]{1,0:T(8,128)S(1)}, f32[512,128]{1,0:T(8,128)S(1)}, u32[]{:S(2)}, u32[]{:S(2)}) collective-permute-start(f32[512,128]{1,0:T(8,128)S(1)} %shard_map.122), channel_id=1, source_target_pairs={{0,2},{1,3},{2,0},{3,1},{4,6},{5,7},{6,4},{7,5},{8,10},{9,11},{10,... | collective-permute-start | bytes 786440 | tf_op jit(solution)/shard_map/ppermute | solution.py:206
  22.5 10.9 %collective-permute-start.12 = (f32[512,128]{1,0:T(8,128)S(1)}, f32[512,128]{1,0:T(8,128)S(1)}, u32[]{:S(2)}, u32[]{:S(2)}) collective-permute-start(f32[512,128]{1,0:T(8,128)S(1)} %shard_map.121.after_ref), channel_id=1, source_target_pairs={{2,0},{4,1},{10,2},{12,3},{3,4},{5,5},{11,6},{13,7},{0,8},{6,9},{8... | collective-permute-start | bytes 786440 | tf_op jit(solution)/shard_map/ppermute | solution.py:257
  24.5 8.9 %collective-permute-start.13 = (f32[512,128]{1,0:T(8,128)S(1)}, f32[512,128]{1,0:T(8,128)S(1)}, u32[]{:S(2)}, u32[]{:S(2)}) collective-permute-start(f32[512,128]{1,0:T(8,128)S(1)} %shard_map.121.after_ref), channel_id=1, source_target_pairs={{0,0},{6,1},{8,2},{14,3},{1,4},{7,5},{9,6},{15,7},{2,8},{4,9},{10,... | collective-permute-start | bytes 786440 | tf_op jit(solution)/shard_map/ppermute | solution.py:257
  25.3 5.2 %collective-permute-start.10 = (f32[160,256]{1,0:T(8,128)S(1)}, f32[160,256]{1,0:T(8,128)S(1)}, u32[]{:S(2)}, u32[]{:S(2)}) collective-permute-start(f32[160,256]{1,0:T(8,128)S(1)} %get-tuple-element.29), channel_id=1, source_target_pairs={{0,1},{1,0},{2,3},{3,2},{4,5},{5,4},{6,7},{7,6},{8,9},{9,8},{10,11... | collective-permute-start | bytes 491528 | tf_op jit(solution)/shard_map/ppermute | solution.py:206
  29.8 1.4 %copy-start.4 = (f32[128,128]{1,0:T(8,128)S(1)}, f32[128,128]{1,0:T(8,128)}, u32[]{:S(2)}) copy-start(f32[128,128]{1,0:T(8,128)} %refs_8_.1) | copy-start | bytes 196612
  29.8 1.4 %collective-permute-start.11 = (f32[160,256]{1,0:T(8,128)S(1)}, f32[160,256]{1,0:T(8,128)S(1)}, u32[]{:S(2)}, u32[]{:S(2)}) collective-permute-start(f32[160,256]{1,0:T(8,128)S(1)} %get-tuple-element.28), channel_id=1, source_target_pairs={{0,1},{1,0},{2,3},{3,2},{4,5},{5,4},{6,7},{7,6},{8,9},{9,8},{10,11... | collective-permute-start | bytes 491528 | tf_op jit(solution)/shard_map/ppermute | solution.py:206
  29.8 2.4 %collective-permute-start.3 = (f32[256,128]{1,0:T(8,128)S(1)}, f32[256,128]{1,0:T(8,128)S(1)}, u32[]{:S(2)}, u32[]{:S(2)}) collective-permute-start(f32[256,128]{1,0:T(8,128)S(1)} %get-tuple-element.26), channel_id=1, source_target_pairs={{0,1},{1,0},{2,3},{3,2},{4,5},{5,4},{6,7},{7,6},{8,9},{9,8},{10,11... | collective-permute-start | bytes 393224 | tf_op jit(solution)/shard_map/ppermute | solution.py:206
  30.4 1.8 %collective-permute-start.6 = (f32[256,128]{1,0:T(8,128)S(1)}, f32[256,128]{1,0:T(8,128)S(1)}, u32[]{:S(2)}, u32[]{:S(2)}) collective-permute-start(f32[256,128]{1,0:T(8,128)S(1)} %get-tuple-element.32), channel_id=1, source_target_pairs={{0,1},{1,0},{2,3},{3,2},{4,5},{5,4},{6,7},{7,6},{8,9},{9,8},{10,11... | collective-permute-start | bytes 393224 | tf_op jit(solution)/shard_map/ppermute | solution.py:206
  34.6 7.9 %collective-permute-start.14 = (f32[136,128]{1,0:T(8,128)S(1)}, f32[136,128]{1,0:T(8,128)S(1)}, u32[]{:S(2)}, u32[]{:S(2)}) collective-permute-start(f32[136,128]{1,0:T(8,128)S(1)} %get-tuple-element.22.refs_0_), channel_id=1, source_target_pairs={{0,4},{4,0},{8,12},{12,8},{1,5},{5,1},{9,13},{13,9},{2,6},{6,2},{1... | collective-permute-start | bytes 208904 | tf_op jit(solution)/shard_map/ppermute | solution.py:206
  39.4 7.9 %collective-permute-start.15 = (f32[136,128]{1,0:T(8,128)S(1)}, f32[136,128]{1,0:T(8,128)S(1)}, u32[]{:S(2)}, u32[]{:S(2)}) collective-permute-start(f32[136,128]{1,0:T(8,128)S(1)} %get-tuple-element.22.refs_0_), channel_id=1, source_target_pairs={{0,8},{4,12},{8,0},{12,4},{1,9},{5,13},{9,1},{13,5},{2,10},{6,14},... | collective-permute-start | bytes 208904 | tf_op jit(solution)/shard_map/ppermute | solution.py:206
  42.5 6.2 %collective-permute-start.16 = (f32[136,128]{1,0:T(8,128)S(1)}, f32[136,128]{1,0:T(8,128)S(1)}, u32[]{:S(2)}, u32[]{:S(2)}) collective-permute-start(f32[136,128]{1,0:T(8,128)S(1)} %get-tuple-element.22.refs_0_), channel_id=1, source_target_pairs={{0,12},{4,8},{8,4},{12,0},{1,13},{5,9},{9,5},{13,1},{2,14},{6,10},... | collective-permute-start | bytes 208904 | tf_op jit(solution)/shard_map/ppermute | solution.py:206

commit v8 on v7

--- a/solution.py
+++ b/solution.py
@@ -341,7 +341,7 @@
         dinv_first,
         start,
         packed,
-        *[swap(packed, "row", nrow, j) for j in range(1, nrow)],
+        *[swap(packed, "row", nrow, j) for j in range(nrow - 1, 0, -1)],
     )
     return (inverse_first, diag_first, inverse_second, diag_second)
 

time: 49.7 us -> 49 us (0.986)
  waiting for transfers between devices: 11.2 us -> 10.6 us
    ppermute x15, waiting for transfers between devices: 11.2 us -> 10.6 us  [swap(): return lax.ppermute(x, axis, [(i, i ^ bit) for i in range(size)])]
where the time goes in v8:
time: 49 us; the launch traced here: 48.8 us
  starting transfers between devices  24.5 us (50%)
  waiting for transfers between devices  10.6 us (22%)
  blocking collectives  5.88 us (12%)
  Pallas kernels  5 us (10%)
  other arithmetic  1.73 us (4%)
  between operations  0.82 us (2%)
    ppermute x15, starting transfers between devices, swap(): return lax.ppermute(x, axis, [(i, i ^ bit) for i in range(size)])  21.9 us
    ppermute x15, waiting for transfers between devices, swap(): return lax.ppermute(x, axis, [(i, i ^ bit) for i in range(size)])  10.6 us
    all_gather x1, blocking collectives, on_device(): sides = lax.all_gather(lower_parent, 'col', axis=0, tiled=True)  5.88 us
    pallas_call x8, Pallas kernels, call(): pl.pallas_call(kernel, out_shape=[jax.ShapeDtypeStruct(shape, dtype) for...  5 us
    ppermute x2, starting transfers between devices, turn(): out.append(lax.ppermute(part, ('row', 'col'), pairs))  2.59 us
    mul x2, other arithmetic, on_device(): first = (cells * mask_first.astype(f32)[:, None, :, None]).reshape(wide)  1.73 us
  transfers between devices with their start and end apart: 17, of which 7 were waited for; matrix products, arithmetic and copies ran while one was open for 0% of the time, Pallas kernels for 6%

profile of v8, /device:TPU:0, one launch (start us, length us, event | category | flops | bytes accessed | tf_op | source)
XLA Modules:
  0.0 48.8 jit_solution(18111629267496417102)
XLA Ops:
  0.6 0.7 %convert_bitcast_fusion = f32[2]{0:T(128)S(1)} fusion(s32[2,1]{0,1:T(1,128)} %param.11), kind=kLoop, calls=%fused_computation.1 | loop fusion | flops 2 | bytes 16 | tf_op jit(solution)/shard_map/mul | solution.py:280
  1.4 1.0 %broadcast_multiply_fusion.refs_0_ = f32[256,128]{1,0:T(8,128)S(1)} fusion(f32[256,128]{1,0:T(8,128)} %param.10, f32[256]{0:T(256)S(1)} %broadcast_bitcast_fusion), kind=kLoop, calls=%fused_computation | loop fusion | flops 32768 | bytes 263168 | tf_op jit(solution)/shard_map/mul | solution.py:280
  2.5 5.1 %collective-permute-start = (f32[256,128]{1,0:T(8,128)S(1)}, f32[256,128]{1,0:T(8,128)S(1)}, u32[]{:S(2)}, u32[]{:S(2)}) collective-permute-start(f32[256,128]{1,0:T(8,128)S(1)} %broadcast_multiply_fusion.refs_0_), channel_id=1, source_target_pairs={{0,12},{4,8},{8,4},{12,0},{1,13},{5,9},{9,5},{13,1},{2,14},{6,10},... | collective-permute-start | bytes 393224 | tf_op jit(solution)/shard_map/ppermute | solution.py:206
  7.6 0.6 %collective-permute-start.2 = (f32[256,128]{1,0:T(8,128)S(1)}, f32[256,128]{1,0:T(8,128)S(1)}, u32[]{:S(2)}, u32[]{:S(2)}) collective-permute-start(f32[256,128]{1,0:T(8,128)S(1)} %broadcast_multiply_fusion.refs_0_), channel_id=1, source_target_pairs={{0,4},{4,0},{8,12},{12,8},{1,5},{5,1},{9,13},{13,9},{2,6},{6,2},{1... | collective-permute-start | bytes 393224 | tf_op jit(solution)/shard_map/ppermute | solution.py:206
  8.2 5.9 %all_gather.3.refs_6_.after_ref = f32[512,128]{1,0:T(8,128)S(1)} all-gather(f32[128,128]{1,0:T(8,128)S(1)} %copy-done.2), channel_id=1, replica_groups=mesh['pole'=2,'row'=4,'col'=4] {'col'}, dimensions={0}, use_global_device_ids=true | all-gather | bytes 327680 | tf_op jit(solution)/shard_map/all_gather | solution.py:282
  14.2 1.6 %collective-permute-start.9 = (f32[320,256]{1,0:T(8,128)S(1)}, f32[320,256]{1,0:T(8,128)S(1)}, u32[]{:S(2)}, u32[]{:S(2)}) collective-permute-start(f32[320,256]{1,0:T(8,128)S(1)} %shard_map.123.refs_0_), channel_id=1, source_target_pairs={{0,2},{1,3},{2,0},{3,1},{4,6},{5,7},{6,4},{7,5},{8,10},{9,11},{10,... | collective-permute-start | bytes 983048 | tf_op jit(solution)/shard_map/ppermute | solution.py:206
  15.8 2.9 %collective-permute-done.1.refs_2_ = f32[256,128]{1,0:T(8,128)S(1)} collective-permute-done((f32[256,128]{1,0:T(8,128)S(1)}, f32[256,128]{1,0:T(8,128)S(1)}, u32[]{:S(2)}, u32[]{:S(2)}) %collective-permute-start.1) | collective-permute-done | bytes 131104 | tf_op jit(solution)/shard_map/ppermute | solution.py:206
  18.7 0.8 %shard_map.120 = (f32[1024,128]{1,0:T(8,128)S(1)}, f32[256,128]{1,0:T(8,128)S(1)}) custom-call(f32[256,128]{1,0:T(8,128)S(1)} %broadcast_multiply_fusion.refs_0_, f32[256,128]{1,0:T(8,128)S(1)} %collective-permute-done.refs_1_, f32[256,128]{1,0:T(8,128)S(1)} %collective-permute-done.1.refs_2_, f32[256,128]{1,0:T(8,128)S(1)} %collective-permute-done.2.refs_3_, ...), custom_call_target="tpu_custom_call" | custom-call | bytes 2097152 | tf_op jit(solution)/shard_map/pallas_call | solution.py:194
  20.3 0.6 %collective-permute-done.4.other_ref = f32[256,128]{1,0:T(8,128)S(1)} collective-permute-done((f32[256,128]{1,0:T(8,128)S(1)}, f32[256,128]{1,0:T(8,128)S(1)}, u32[]{:S(2)}, u32[]{:S(2)}) %collective-permute-start.4) | collective-permute-done | bytes 131104 | tf_op jit(solution)/shard_map/ppermute | solution.py:206
  20.9 1.6 %collective-permute-start.5 = (f32[512,128]{1,0:T(8,128)S(1)}, f32[512,128]{1,0:T(8,128)S(1)}, u32[]{:S(2)}, u32[]{:S(2)}) collective-permute-start(f32[512,128]{1,0:T(8,128)S(1)} %shard_map.122), channel_id=1, source_target_pairs={{0,2},{1,3},{2,0},{3,1},{4,6},{5,7},{6,4},{7,5},{8,10},{9,11},{10,... | collective-permute-start | bytes 786440 | tf_op jit(solution)/shard_map/ppermute | solution.py:206
  22.5 1.9 %collective-permute-start.12 = (f32[512,128]{1,0:T(8,128)S(1)}, f32[512,128]{1,0:T(8,128)S(1)}, u32[]{:S(2)}, u32[]{:S(2)}) collective-permute-start(f32[512,128]{1,0:T(8,128)S(1)} %shard_map.121.after_ref), channel_id=1, source_target_pairs={{2,0},{4,1},{10,2},{12,3},{3,4},{5,5},{11,6},{13,7},{0,8},{6,9},{8... | collective-permute-start | bytes 786440 | tf_op jit(solution)/shard_map/ppermute | solution.py:257
  24.5 0.7 %collective-permute-start.13 = (f32[512,128]{1,0:T(8,128)S(1)}, f32[512,128]{1,0:T(8,128)S(1)}, u32[]{:S(2)}, u32[]{:S(2)}) collective-permute-start(f32[512,128]{1,0:T(8,128)S(1)} %shard_map.121.after_ref), channel_id=1, source_target_pairs={{0,0},{6,1},{8,2},{14,3},{1,4},{7,5},{9,6},{15,7},{2,8},{4,9},{10,... | collective-permute-start | bytes 786440 | tf_op jit(solution)/shard_map/ppermute | solution.py:257
  25.3 3.8 %collective-permute-start.10 = (f32[160,256]{1,0:T(8,128)S(1)}, f32[160,256]{1,0:T(8,128)S(1)}, u32[]{:S(2)}, u32[]{:S(2)}) collective-permute-start(f32[160,256]{1,0:T(8,128)S(1)} %get-tuple-element.29), channel_id=1, source_target_pairs={{0,1},{1,0},{2,3},{3,2},{4,5},{5,4},{6,7},{7,6},{8,9},{9,8},{10,11... | collective-permute-start | bytes 491528 | tf_op jit(solution)/shard_map/ppermute | solution.py:206
  29.1 0.7 %collective-permute-done.5 = f32[512,128]{1,0:T(8,128)S(1)} collective-permute-done((f32[512,128]{1,0:T(8,128)S(1)}, f32[512,128]{1,0:T(8,128)S(1)}, u32[]{:S(2)}, u32[]{:S(2)}) %collective-permute-start.5) | collective-permute-done | bytes 262176 | tf_op jit(solution)/shard_map/ppermute | solution.py:206
  29.8 0.6 %collective-permute-start.3 = (f32[256,128]{1,0:T(8,128)S(1)}, f32[256,128]{1,0:T(8,128)S(1)}, u32[]{:S(2)}, u32[]{:S(2)}) collective-permute-start(f32[256,128]{1,0:T(8,128)S(1)} %get-tuple-element.26), channel_id=1, source_target_pairs={{0,1},{1,0},{2,3},{3,2},{4,5},{5,4},{6,7},{7,6},{8,9},{9,8},{10,11... | collective-permute-start | bytes 393224 | tf_op jit(solution)/shard_map/ppermute | solution.py:206
  30.5 0.7 %collective-permute-done.11.refs_5_ = f32[160,256]{1,0:T(8,128)S(1)} collective-permute-done((f32[160,256]{1,0:T(8,128)S(1)}, f32[160,256]{1,0:T(8,128)S(1)}, u32[]{:S(2)}, u32[]{:S(2)}) %collective-permute-start.11) | collective-permute-done | bytes 163872 | tf_op jit(solution)/shard_map/ppermute | solution.py:206
  31.2 1.0 %shard_map.124 = (f32[128,128]{1,0:T(8,128)S(1)}, bf16[4,256,256]{2,1,0:T(8,128)(2,1)S(1)}, bf16[4,256,256]{2,1,0:T(8,128)(2,1)S(1)}) custom-call(f32[320,256]{1,0:T(8,128)S(1)} %shard_map.123.refs_0_, f32[160,256]{1,0:T(8,128)S(1)} %collective-permute-done.7.refs_1_, f32[160,256]{1,0:T(8,128)S(1)} %collective-permute-done.8.refs_2_, ...), custom_call_target="tpu_custom_call" | custom-call | bytes 2621440 | tf_op jit(solution)/shard_map/pallas_call | solution.py:194
  32.3 1.1 %shard_map.125 = (f32[256,128]{1,0:T(8,128)}, f32[128,128]{1,0:T(8,128)S(1)}) custom-call(f32[256,128]{1,0:T(8,128)S(1)} %get-tuple-element.27.refs_0_, f32[256,128]{1,0:T(8,128)S(1)} %collective-permute-done.3.refs_1_, f32[256,128]{1,0:T(8,128)S(1)} %get-tuple-element.33.refs_2_, f32[256,128]{1,0:T(8,128)S(1)} %collective-permute-done.6.refs_3_, ...), custom_call_target="tpu_custom_call" | custom-call | bytes 2293760 | tf_op jit(solution)/shard_map/pallas_call | solution.py:194
  33.4 1.2 %shard_map.126 = (f32[256,128]{1,0:T(8,128)}, f32[136,128]{1,0:T(8,128)S(1)}) custom-call(f32[512,128]{1,0:T(8,128)S(1)} %collective-permute-done.12.refs_0_, f32[512,128]{1,0:T(8,128)S(1)} %collective-permute-done.13.refs_1_, bf16[4,256,256]{2,1,0:T(8,128)(2,1)S(1)} %get-tuple-element.17.refs_4_.refs_2_, ...), custom_call_target="tpu_custom_call" | custom-call | bytes 2363392 | tf_op jit(solution)/shard_map/pallas_call | solution.py:194
  34.6 7.3 %collective-permute-start.14 = (f32[136,128]{1,0:T(8,128)S(1)}, f32[136,128]{1,0:T(8,128)S(1)}, u32[]{:S(2)}, u32[]{:S(2)}) collective-permute-start(f32[136,128]{1,0:T(8,128)S(1)} %get-tuple-element.22.refs_0_), channel_id=1, source_target_pairs={{0,12},{4,8},{8,4},{12,0},{1,13},{5,9},{9,5},{13,1},{2,14},{6,10},... | collective-permute-start | bytes 208904 | tf_op jit(solution)/shard_map/ppermute | solution.py:206
  41.9 0.6 %collective-permute-start.16 = (f32[136,128]{1,0:T(8,128)S(1)}, f32[136,128]{1,0:T(8,128)S(1)}, u32[]{:S(2)}, u32[]{:S(2)}) collective-permute-start(f32[136,128]{1,0:T(8,128)S(1)} %get-tuple-element.22.refs_0_), channel_id=1, source_target_pairs={{0,4},{4,0},{8,12},{12,8},{1,5},{5,1},{9,13},{13,9},{2,6},{6,2},{1... | collective-permute-start | bytes 208904 | tf_op jit(solution)/shard_map/ppermute | solution.py:206
  42.5 2.2 %collective-permute-done.14.refs_1_ = f32[136,128]{1,0:T(8,128)S(1)} collective-permute-done((f32[136,128]{1,0:T(8,128)S(1)}, f32[136,128]{1,0:T(8,128)S(1)}, u32[]{:S(2)}, u32[]{:S(2)}) %collective-permute-start.14) | collective-permute-done | bytes 69664 | tf_op jit(solution)/shard_map/ppermute | solution.py:206
  44.7 3.3 %collective-permute-done.15.refs_2_ = f32[136,128]{1,0:T(8,128)S(1)} collective-permute-done((f32[136,128]{1,0:T(8,128)S(1)}, f32[136,128]{1,0:T(8,128)S(1)}, u32[]{:S(2)}, u32[]{:S(2)}) %collective-permute-start.15) | collective-permute-done | bytes 69664 | tf_op jit(solution)/shard_map/ppermute | solution.py:206
  48.0 0.8 %shard_map.127 = (f32[128,128]{1,0:T(8,128)}, f32[128,128]{1,0:T(8,128)}) custom-call(f32[128,128]{1,0:T(8,128)S(1)} %copy-done, f32[128,128]{1,0:T(8,128)S(1)} %get-tuple-element.20.e_ref, f32[136,128]{1,0:T(8,128)S(1)} %get-tuple-element.22.refs_0_, f32[136,128]{1,0:T(8,128)S(1)} %collective-permute-done.14.refs_1_, ...), custom_call_target="tpu_custom_call" | custom-call | bytes 540672 | tf_op jit(solution)/shard_map/pallas_call | solution.py:194
  (41 shorter events, 1.2 us)
Async XLA Ops:
  0.6 7.6 %copy-start.2 = (f32[128,128]{1,0:T(8,128)S(1)}, f32[128,128]{1,0:T(8,128)}, u32[]{:S(2)}) copy-start(f32[128,128]{1,0:T(8,128)} %refs_7_.3) | copy-start | bytes 196612
  1.4 12.7 %copy-start.1 = (f32[256,256]{1,0:T(8,128)S(1)}, f32[256,256]{1,0:T(8,128)}, u32[]{:S(2)}) copy-start(f32[256,256]{1,0:T(8,128)} %root_ref.1) | copy-start | bytes 786436
  2.5 11.7 %copy-start = (f32[128,128]{1,0:T(8,128)S(1)}, f32[128,128]{1,0:T(8,128)}, u32[]{:S(2)}) copy-start(f32[128,128]{1,0:T(8,128)} %dinv_ref.3) | copy-start | bytes 196612
  2.5 13.3 %collective-permute-start = (f32[256,128]{1,0:T(8,128)S(1)}, f32[256,128]{1,0:T(8,128)S(1)}, u32[]{:S(2)}, u32[]{:S(2)}) collective-permute-start(f32[256,128]{1,0:T(8,128)S(1)} %broadcast_multiply_fusion.refs_0_), channel_id=1, source_target_pairs={{0,12},{4,8},{8,4},{12,0},{1,13},{5,9},{9,5},{13,1},{2,14},{6,10},... | collective-permute-start | bytes 393224 | tf_op jit(solution)/shard_map/ppermute | solution.py:206
  7.6 11.1 %collective-permute-start.1 = (f32[256,128]{1,0:T(8,128)S(1)}, f32[256,128]{1,0:T(8,128)S(1)}, u32[]{:S(2)}, u32[]{:S(2)}) collective-permute-start(f32[256,128]{1,0:T(8,128)S(1)} %broadcast_multiply_fusion.refs_0_), channel_id=1, source_target_pairs={{0,8},{4,12},{8,0},{12,4},{1,9},{5,13},{9,1},{13,5},{2,10},{6,14},... | collective-permute-start | bytes 393224 | tf_op jit(solution)/shard_map/ppermute | solution.py:206
  7.6 11.1 %collective-permute-start.2 = (f32[256,128]{1,0:T(8,128)S(1)}, f32[256,128]{1,0:T(8,128)S(1)}, u32[]{:S(2)}, u32[]{:S(2)}) collective-permute-start(f32[256,128]{1,0:T(8,128)S(1)} %broadcast_multiply_fusion.refs_0_), channel_id=1, source_target_pairs={{0,4},{4,0},{8,12},{12,8},{1,5},{5,1},{9,13},{13,9},{2,6},{6,2},{1... | collective-permute-start | bytes 393224 | tf_op jit(solution)/shard_map/ppermute | solution.py:206
  14.1 4.6 %copy-start.3 = (f32[256,128]{1,0:T(8,128)S(1)}, f32[256,128]{1,0:T(8,128)}, u32[]{:S(2)}) copy-start(f32[256,128]{1,0:T(8,128)} %refs_4_.1) | copy-start | bytes 393220
  14.1 4.5 %copy-start.5 = (s32[4]{0:T(128)S(1)}, s32[4]{0:T(128)}, u32[]{:S(2)}) copy-start(s32[4]{0:T(128)} %refs_6_.1) | copy-start | bytes 52
  14.1 4.5 %copy-start.6 = (s32[2,1]{0,1:T(1,128)S(1)}, s32[2,1]{0,1:T(1,128)}, u32[]{:S(2)}) copy-start(s32[2,1]{0,1:T(1,128)} %param.14) | copy-start | bytes 28
  14.2 10.4 %collective-permute-start.9 = (f32[320,256]{1,0:T(8,128)S(1)}, f32[320,256]{1,0:T(8,128)S(1)}, u32[]{:S(2)}, u32[]{:S(2)}) collective-permute-start(f32[320,256]{1,0:T(8,128)S(1)} %shard_map.123.refs_0_), channel_id=1, source_target_pairs={{0,2},{1,3},{2,0},{3,1},{4,6},{5,7},{6,4},{7,5},{8,10},{9,11},{10,... | collective-permute-start | bytes 983048 | tf_op jit(solution)/shard_map/ppermute | solution.py:206
  19.5 1.4 %collective-permute-start.4 = (f32[256,128]{1,0:T(8,128)S(1)}, f32[256,128]{1,0:T(8,128)S(1)}, u32[]{:S(2)}, u32[]{:S(2)}) collective-permute-start(f32[256,128]{1,0:T(8,128)S(1)} %get-tuple-element.16.own_ref), channel_id=1, source_target_pairs={{0,1},{1,0},{2,3},{3,2},{4,5},{5,4},{6,7},{7,6},{8,9},{9,8},{10,11... | collective-permute-start | bytes 393224 | tf_op jit(solution)/shard_map/ppermute | solution.py:206
  19.6 5.7 %collective-permute-start.7 = (f32[160,256]{1,0:T(8,128)S(1)}, f32[160,256]{1,0:T(8,128)S(1)}, u32[]{:S(2)}, u32[]{:S(2)}) collective-permute-start(f32[160,256]{1,0:T(8,128)S(1)} %get-tuple-element.31), channel_id=1, source_target_pairs={{0,1},{1,0},{2,3},{3,2},{4,5},{5,4},{6,7},{7,6},{8,9},{9,8},{10,11... | collective-permute-start | bytes 491528 | tf_op jit(solution)/shard_map/ppermute | solution.py:206
  20.2 9.7 %collective-permute-start.8 = (f32[160,256]{1,0:T(8,128)S(1)}, f32[160,256]{1,0:T(8,128)S(1)}, u32[]{:S(2)}, u32[]{:S(2)}) collective-permute-start(f32[160,256]{1,0:T(8,128)S(1)} %get-tuple-element.30), channel_id=1, source_target_pairs={{0,1},{1,0},{2,3},{3,2},{4,5},{5,4},{6,7},{7,6},{8,9},{9,8},{10,11... | collective-permute-start | bytes 491528 | tf_op jit(solution)/shard_map/ppermute | solution.py:206
  20.9 8.9 %collective-permute-start.5 = (f32[512,128]{1,0:T(8,128)S(1)}, f32[512,128]{1,0:T(8,128)S(1)}, u32[]{:S(2)}, u32[]{:S(2)}) collective-permute-start(f32[512,128]{1,0:T(8,128)S(1)} %shard_map.122), channel_id=1, source_target_pairs={{0,2},{1,3},{2,0},{3,1},{4,6},{5,7},{6,4},{7,5},{8,10},{9,11},{10,... | collective-permute-start | bytes 786440 | tf_op jit(solution)/shard_map/ppermute | solution.py:206
  22.5 10.9 %collective-permute-start.12 = (f32[512,128]{1,0:T(8,128)S(1)}, f32[512,128]{1,0:T(8,128)S(1)}, u32[]{:S(2)}, u32[]{:S(2)}) collective-permute-start(f32[512,128]{1,0:T(8,128)S(1)} %shard_map.121.after_ref), channel_id=1, source_target_pairs={{2,0},{4,1},{10,2},{12,3},{3,4},{5,5},{11,6},{13,7},{0,8},{6,9},{8... | collective-permute-start | bytes 786440 | tf_op jit(solution)/shard_map/ppermute | solution.py:257
  24.5 8.9 %collective-permute-start.13 = (f32[512,128]{1,0:T(8,128)S(1)}, f32[512,128]{1,0:T(8,128)S(1)}, u32[]{:S(2)}, u32[]{:S(2)}) collective-permute-start(f32[512,128]{1,0:T(8,128)S(1)} %shard_map.121.after_ref), channel_id=1, source_target_pairs={{0,0},{6,1},{8,2},{14,3},{1,4},{7,5},{9,6},{15,7},{2,8},{4,9},{10,... | collective-permute-start | bytes 786440 | tf_op jit(solution)/shard_map/ppermute | solution.py:257
  25.3 5.2 %collective-permute-start.10 = (f32[160,256]{1,0:T(8,128)S(1)}, f32[160,256]{1,0:T(8,128)S(1)}, u32[]{:S(2)}, u32[]{:S(2)}) collective-permute-start(f32[160,256]{1,0:T(8,128)S(1)} %get-tuple-element.29), channel_id=1, source_target_pairs={{0,1},{1,0},{2,3},{3,2},{4,5},{5,4},{6,7},{7,6},{8,9},{9,8},{10,11... | collective-permute-start | bytes 491528 | tf_op jit(solution)/shard_map/ppermute | solution.py:206
  29.8 1.4 %copy-start.4 = (f32[128,128]{1,0:T(8,128)S(1)}, f32[128,128]{1,0:T(8,128)}, u32[]{:S(2)}) copy-start(f32[128,128]{1,0:T(8,128)} %refs_8_.1) | copy-start | bytes 196612
  29.8 1.4 %collective-permute-start.11 = (f32[160,256]{1,0:T(8,128)S(1)}, f32[160,256]{1,0:T(8,128)S(1)}, u32[]{:S(2)}, u32[]{:S(2)}) collective-permute-start(f32[160,256]{1,0:T(8,128)S(1)} %get-tuple-element.28), channel_id=1, source_target_pairs={{0,1},{1,0},{2,3},{3,2},{4,5},{5,4},{6,7},{7,6},{8,9},{9,8},{10,11... | collective-permute-start | bytes 491528 | tf_op jit(solution)/shard_map/ppermute | solution.py:206
  29.8 2.4 %collective-permute-start.3 = (f32[256,128]{1,0:T(8,128)S(1)}, f32[256,128]{1,0:T(8,128)S(1)}, u32[]{:S(2)}, u32[]{:S(2)}) collective-permute-start(f32[256,128]{1,0:T(8,128)S(1)} %get-tuple-element.26), channel_id=1, source_target_pairs={{0,1},{1,0},{2,3},{3,2},{4,5},{5,4},{6,7},{7,6},{8,9},{9,8},{10,11... | collective-permute-start | bytes 393224 | tf_op jit(solution)/shard_map/ppermute | solution.py:206
  30.4 1.8 %collective-permute-start.6 = (f32[256,128]{1,0:T(8,128)S(1)}, f32[256,128]{1,0:T(8,128)S(1)}, u32[]{:S(2)}, u32[]{:S(2)}) collective-permute-start(f32[256,128]{1,0:T(8,128)S(1)} %get-tuple-element.32), channel_id=1, source_target_pairs={{0,1},{1,0},{2,3},{3,2},{4,5},{5,4},{6,7},{7,6},{8,9},{9,8},{10,11... | collective-permute-start | bytes 393224 | tf_op jit(solution)/shard_map/ppermute | solution.py:206
  34.6 10.1 %collective-permute-start.14 = (f32[136,128]{1,0:T(8,128)S(1)}, f32[136,128]{1,0:T(8,128)S(1)}, u32[]{:S(2)}, u32[]{:S(2)}) collective-permute-start(f32[136,128]{1,0:T(8,128)S(1)} %get-tuple-element.22.refs_0_), channel_id=1, source_target_pairs={{0,12},{4,8},{8,4},{12,0},{1,13},{5,9},{9,5},{13,1},{2,14},{6,10},... | collective-permute-start | bytes 208904 | tf_op jit(solution)/shard_map/ppermute | solution.py:206
  41.9 6.1 %collective-permute-start.15 = (f32[136,128]{1,0:T(8,128)S(1)}, f32[136,128]{1,0:T(8,128)S(1)}, u32[]{:S(2)}, u32[]{:S(2)}) collective-permute-start(f32[136,128]{1,0:T(8,128)S(1)} %get-tuple-element.22.refs_0_), channel_id=1, source_target_pairs={{0,8},{4,12},{8,0},{12,4},{1,9},{5,13},{9,1},{13,5},{2,10},{6,14},... | collective-permute-start | bytes 208904 | tf_op jit(solution)/shard_map/ppermute | solution.py:206
  41.9 6.1 %collective-permute-start.16 = (f32[136,128]{1,0:T(8,128)S(1)}, f32[136,128]{1,0:T(8,128)S(1)}, u32[]{:S(2)}, u32[]{:S(2)}) collective-permute-start(f32[136,128]{1,0:T(8,128)S(1)} %get-tuple-element.22.refs_0_), channel_id=1, source_target_pairs={{0,4},{4,0},{8,12},{12,8},{1,5},{5,1},{9,13},{13,9},{2,6},{6,2},{1... | collective-permute-start | bytes 208904 | tf_op jit(solution)/shard_map/ppermute | solution.py:206
